TPU v7x, 256 devices: a whole 4x4x8 slice. The times are simulated.
256 devices in a mesh: prow: 16 (over y, x), pcol: 16 (over z, core).
Axes of the slice: x: 4, y: 4, z: 8, core: 2. Of those that a mesh axis runs over, the one named last changes fastest.
Arguments:
- coupling: float32 [8, 2048, 8, 2048], P(None, 'prow', None, 'pcol')
- diagonal: float32 [8, 2048], P(None, 'prow'), as said below
Outputs:
- trailing: float32 [8, 2048, 8, 2048], P(None, 'prow', None, 'pcol')
Inputs may be any that keep to these rules, and one draw needn't show every extreme that they name: `diagonal`: every entry is positive.
All inputs are finite; a program needn't handle non-finite values.
Results may differ from a plain program's by a relative error of at most 0.00005.
Values sent between devices are 32-bit elements; how exact they have to be, the bound alone decides.
No kernel may reach another device: no remote copies, remote signals or barrier semaphores. Data moves between devices by JAX's collectives and lax.ppermute only.
A program may use at most 128 MiB of HBM per device.

v0:
```python
import jax
import jax.numpy as jnp
from jax import lax
from jax.sharding import PartitionSpec as P


def broadcast(block, axis, source):
    block = jnp.where(lax.axis_index(axis) == source, block, jnp.zeros_like(block))
    return lax.psum(block, axis)


def pivot_factor(column, diagonal, panel_step, row_blocks, row_count, col_count):
    block_size = column.shape[1]
    identity = jnp.eye(block_size, dtype=jnp.float32)
    pivot_block = column[panel_step // row_count] + jnp.diag(diagonal[panel_step // row_count])
    shared = broadcast(pivot_block, "prow", panel_step % row_count)
    lower_factor = jnp.linalg.cholesky(shared)
    inverse = lax.linalg.triangular_solve(lower_factor, identity, left_side=True, lower=True)
    solved = jnp.einsum("anr,mr->anm", column, inverse, precision=lax.Precision.HIGHEST)
    block_index = row_blocks[:, None, None]
    panel_rows = jnp.where(
        block_index == panel_step,
        lower_factor[None],
        jnp.where(block_index > panel_step, solved, jnp.float32(0.0)),
    )
    return broadcast(panel_rows, "pcol", panel_step % col_count)


def transposed(panel_rows, col_blocks, row_count):
    rows_dev = panel_rows.shape[0]
    gathered = lax.all_gather(panel_rows, "prow", axis=0, tiled=True)
    gather_index = col_blocks % row_count * rows_dev + col_blocks // row_count
    return jnp.take(gathered, gather_index, axis=0)


def apply_update(trailing, panel_rows, panel_cols):
    product = jnp.einsum("anr,cmr->ancm", panel_rows, panel_cols, precision=lax.Precision.HIGHEST)
    return trailing - product


def on_device(coupling, diagonal):
    rows_dev = coupling.shape[0]
    cols_dev = coupling.shape[2]
    row_count = lax.axis_size("prow")
    col_count = lax.axis_size("pcol")
    prow_place = lax.axis_index("prow")
    pcol_place = lax.axis_index("pcol")
    row_blocks = jnp.arange(rows_dev, dtype=jnp.int32) * row_count + prow_place
    col_blocks = jnp.arange(cols_dev, dtype=jnp.int32) * col_count + pcol_place
    first_rows = pivot_factor(coupling[:, :, 0, :], diagonal, 0, row_blocks, row_count, col_count)
    first_cols = transposed(first_rows, col_blocks, row_count)
    trailing = apply_update(coupling, first_rows, first_cols)
    second_rows = pivot_factor(
        trailing[:, :, 1 // col_count, :], diagonal, 1, row_blocks, row_count, col_count
    )
    second_cols = transposed(second_rows, col_blocks, row_count)
    trailing = apply_update(trailing, second_rows, second_cols)
    keep_rows = (row_blocks >= 2)[:, None, None, None]
    keep_cols = (col_blocks >= 2)[None, None, :, None]
    return jnp.where(keep_rows & keep_cols, trailing, jnp.float32(0.0))


def solution(mesh):
    return jax.shard_map(
        on_device,
        mesh=mesh,
        in_specs=(P(None, "prow", None, "pcol"), P(None, "prow")),
        out_specs=P(None, "prow", None, "pcol"),
        check_vma=False,
    )
```

profile of v0, /device:TPU:1, one launch (start us, length us, event | category | flops | bytes accessed | tf_op | source)
XLA Modules:
  0.0 664.9 jit_solution(10280276951244474521)
XLA Ops:
  6.5 5.4 copy.25
  12.6 1.5 fusion.17
  14.2 93.4 %all-reduce.5.cloned.1.call-done = f32[128,128]{0,1:T(8,128)} async-done(((f32[128,128]{0,1:T(8,128)}), f32[128,128]{0,1:T(8,128)}) %all-reduce.5.cloned.1.call-update) | async-done | bytes 65552 | tf_op jit(solution)/shard_map/psum | solution.py:9
  107.6 0.9 copy.20
  109.4 11.7 %cholesky.44 = f32[128,128]{1,0:T(8,128)S(1)} custom-call(f32[128,128]{1,0:T(8,128)S(1)} %fusion.22), custom_call_target="Cholesky" | custom-call | tf_op jit(solution)/shard_map/jit(cholesky)/cholesky | solution.py:17
  122.4 9.8 %custom-call.6 = f32[1,128,128]{1,2,0:T(8,128)S(1)} custom-call(f32[1,128,128]{2,1,0:T(8,128)S(1)} %get-tuple-element.10), custom_call_target="InvertDiagBlocksLowerTriangular" | custom-call | tf_op jit(solution)/shard_map/triangular_solve/custom-call.0 | solution.py:18
  132.7 1.4 fusion.4
  134.1 110.7 %all-reduce.7.cloned.1.call-done = f32[8,128,128]{1,2,0:T(8,128)} async-done(((f32[8,128,128]{1,2,0:T(8,128)}), f32[8,128,128]{1,2,0:T(8,128)}) %all-reduce.7.cloned.1.call-update) | async-done | bytes 524304 | tf_op jit(solution)/shard_map/psum | solution.py:9
  244.8 2.1 copy.23
  247.1 76.4 %all-gather.3.cloned.1.call-done = f32[128,128,128]{2,1,0:T(8,128)} async-done(((f32[8,128,128]{2,1,0:T(8,128)}), f32[128,128,128]{2,1,0:T(8,128)}) %all-gather.3.cloned.1.call-update) | async-done | bytes 8388624 | tf_op jit(solution)/shard_map/all_gather | solution.py:31
  323.4 4.0 gather_fusion
  327.4 5.7 convolution_subtract_fusion
  333.1 2.0 copy-done
  336.0 89.1 %all-reduce.9.cloned.1.call-done = f32[128,128]{0,1:T(8,128)} async-done(((f32[128,128]{0,1:T(8,128)}), f32[128,128]{0,1:T(8,128)}) %all-reduce.9.cloned.1.call-update) | async-done | bytes 65552 | tf_op jit(solution)/shard_map/psum | solution.py:9
  425.1 0.9 copy.27
  426.9 11.7 %cholesky.55 = f32[128,128]{1,0:T(8,128)S(1)} custom-call(f32[128,128]{1,0:T(8,128)S(1)} %fusion.20), custom_call_target="Cholesky" | custom-call | tf_op jit(solution)/shard_map/jit(cholesky)/cholesky | solution.py:17
  440.0 9.8 %custom-call.7 = f32[1,128,128]{1,2,0:T(8,128)S(1)} custom-call(f32[1,128,128]{2,1,0:T(8,128)S(1)} %get-tuple-element.6), custom_call_target="InvertDiagBlocksLowerTriangular" | custom-call | tf_op jit(solution)/shard_map/triangular_solve/custom-call.0 | solution.py:18
  450.2 2.5 fusion.1
  452.7 110.7 %all-reduce.11.cloned.1.call-done = f32[8,128,128]{1,2,0:T(8,128)} async-done(((f32[8,128,128]{1,2,0:T(8,128)}), f32[8,128,128]{1,2,0:T(8,128)}) %all-reduce.11.cloned.1.call-update) | async-done | bytes 524304 | tf_op jit(solution)/shard_map/psum | solution.py:9
  563.4 2.1 copy.31
  565.7 76.2 %all-gather.5.cloned.1.call-done = f32[128,128,128]{2,1,0:T(8,128)} async-done(((f32[8,128,128]{2,1,0:T(8,128)}), f32[128,128,128]{2,1,0:T(8,128)}) %all-gather.5.cloned.1.call-update) | async-done | bytes 8388624 | tf_op jit(solution)/shard_map/all_gather | solution.py:31
  641.9 4.0 gather_fusion.1
  645.8 6.9 %subtract_select_fusion = f32[8,128,8,128]{1,3,2,0:T(8,128)} fusion(f32[8,128,8,128]{1,3,2,0:T(8,128)} %copy-done, pred[8,8]{1,0:T(8,128)(4,1)S(1)} %broadcast_and_fusion, f32[8,128,128]{1,2,0:T(8,128)} %all-reduce.11.cloned.1.call-done, f32[8,128,128]{2,1,0:T(8,128)S(1)} %gather_fusion.1, pred[8]{0:T(512)(128)(4,1)S(1)} %compare_and_fusion), kind=kOutput, calls=%fused_computation.2 | convolution fusion | flops 1612840960 | bytes 9437256 | tf_op jit(solution)/shard_map/anr,cmr->ancm/dot_general | solution.py:37
  652.7 5.3 copy.34
  (37 shorter events, 7.1 us)
Async XLA Ops:
  6.5 101.0 %all-reduce.5.cloned.1.call-start = ((), (), s32[]{:S(2)}) async-start(), calls=%async_computation | async-start | bytes 131072 | tf_op jit(solution)/shard_map/psum | solution.py:9
  6.5 126.1 %slice-start = ((f32[8,128,8,128]{3,2,1,0:T(8,128)}), f32[8,128,1,128]{3,2,1,0:T(1,128)S(1)}, s32[]{:S(2)}) async-start(f32[8,128,8,128]{3,2,1,0:T(8,128)} %param.7), calls=%async_computation.6 | async-start | bytes 1048576 | tf_op jit(solution)/shard_map/slice | solution.py:50
  14.1 230.7 %all-reduce.7.cloned.1.call-start = ((), (), s32[]{:S(2)}) async-start(), calls=%async_computation.1 | async-start | bytes 1048576 | tf_op jit(solution)/shard_map/psum | solution.py:9
  134.1 189.3 %all-gather.3.cloned.1.call-start = ((), (), s32[]{:S(2)}) async-start(), calls=%async_computation.2 | async-start | bytes 8912896 | tf_op jit(solution)/shard_map/all_gather | solution.py:31
  246.9 178.2 %all-reduce.9.cloned.1.call-start = ((), (), s32[]{:S(2)}) async-start(), calls=%async_computation.3 | async-start | bytes 131072 | tf_op jit(solution)/shard_map/psum | solution.py:9
  333.1 2.0 copy-start
  335.7 227.7 %all-reduce.11.cloned.1.call-start = ((), (), s32[]{:S(2)}) async-start(), calls=%async_computation.4 | async-start | bytes 1048576 | tf_op jit(solution)/shard_map/psum | solution.py:9
  452.7 189.2 %all-gather.5.cloned.1.call-start = ((), (), s32[]{:S(2)}) async-start(), calls=%async_computation.5 | async-start | bytes 8912896 | tf_op jit(solution)/shard_map/all_gather | solution.py:31
Sparse Core Ops, SparseCore 0:
  14.3 93.2 all-reduce.4
  134.2 110.5 all-reduce.6
  247.3 76.1 all-gather.2
  335.9 89.2 all-reduce.8
  452.8 110.5 all-reduce.10
  565.7 76.1 all-gather.4
where the time goes:
time: 666 us; the launch traced here: 665 us
  waiting for transfers between devices  557 us (84%)
  other arithmetic  49.7 us (7%)
  local copies, waits for them, and re-layouts  27.6 us (4%)
  matrix products  17 us (3%)
  between operations  13.7 us (2%)
    psum x4, waiting for transfers between devices, broadcast(): return lax.psum(block, axis)  404 us
    all_gather x2, waiting for transfers between devices, transposed(): gathered = lax.all_gather(panel_rows, 'prow', axis=0, tiled=True)  153 us
    another operation x6, other arithmetic, pivot_factor(): lower_factor = jnp.linalg.cholesky(shared)  24.8 us
    another operation x4, other arithmetic, pivot_factor(): lax.linalg.triangular_solve(lower_factor, identity, left_side=True, lower...  20.9 us
  transfers between devices with their start and end apart: 6, of which 6 were waited for; matrix products, arithmetic and copies ran while one was open for 0% of the time, Pallas kernels for 0%

commit v1 on v0

v1 whole, which is shorter than its diff:
```python
import jax
import jax.numpy as jnp
from jax import lax
from jax.experimental import pallas as pl
from jax.experimental.pallas import tpu as pltpu
from jax.sharding import PartitionSpec as P

f32 = jnp.float32
bf16 = jnp.bfloat16
HIGHEST = lax.Precision.HIGHEST
AXES = ("prow", "pcol")
NT = (((1,), (1,)), ((), ()))
TN = (((0,), (0,)), ((), ()))


def place_of(row, col):
    return row % 4, row // 4, col // 2, col % 2


def send(value, target):
    pairs = []
    for row in range(16):
        for col in range(16):
            to = target(*place_of(row, col))
            if to is not None:
                x, y, z, core = to
                pairs.append((row * 16 + col, (y * 4 + x) * 16 + z * 2 + core))
    return lax.ppermute(value, AXES, pairs)


def invert_factor(rows):
    sub = lax.broadcasted_iota(jnp.int32, (8, 128), 0)
    lane = lax.broadcasted_iota(jnp.int32, (8, 128), 1)
    spread = lambda v, i: jnp.broadcast_to(v[i:i + 1, :], (8, 128))
    rows = list(rows)
    out = []
    for g in range(16):
        first = 8 * g
        column = lambda i, l: jnp.broadcast_to(rows[i][:, first + l:first + l + 1], (8, 128))
        own = [column(g, l) for l in range(8)]
        below = [[column(i, l) for l in range(8)] for i in range(g + 1, 16)]
        panel = rows[g]
        kept = jnp.zeros((8, 128), f32)
        for p in range(8):
            here = sub == p
            panel = jnp.where(lane == first + p, jnp.where(here, 1.0, 0.0), panel)
            pivot = spread(own[p], p)
            inv = 1.0 / pivot
            factor = own[p] * inv
            row = spread(panel, p)
            kept = jnp.where(here, row * lax.rsqrt(pivot), kept)
            panel = jnp.where(here, row * inv, panel - factor * row)
            for l in range(p + 1, 8):
                mine = spread(own[l], p)
                own[l] = jnp.where(here, mine * inv, own[l] - factor * mine)
        out.append(jnp.where(lane <= sub + first, kept, 0.0))
        cleared = (lane >= first) & (lane < first + 8)
        spreads = [spread(panel, l) for l in range(8)]
        for n, i in enumerate(range(g + 1, 16)):
            acc = jnp.where(cleared, 0.0, rows[i])
            for l in range(8):
                acc = acc - below[n][l] * spreads[l]
            rows[i] = acc
    return out


def exact(a, b, dims=(((1,), (0,)), ((), ()))):
    return lax.dot_general(a, b, dims, precision=HIGHEST, preferred_element_type=f32)


def groups(block):
    return [block[8 * i:8 * i + 8, :] for i in range(16)]


def factor_kernel(packed_ref, cross_ref, w_ref):
    r = lax.broadcasted_iota(jnp.int32, (128, 128), 0)
    c = lax.broadcasted_iota(jnp.int32, (128, 128), 1)
    packed = packed_ref[0:128, :]
    turned = packed.T
    s0 = jnp.where(r >= c, packed, turned)
    s1 = jnp.where(r < c, packed, jnp.where(r > c, turned, packed_ref[128:129, :]))
    w0 = jnp.concatenate(invert_factor(groups(s0)), axis=0)
    y = exact(w0, cross_ref[...])
    s1 = s1 - exact(y, y, TN)
    z = exact(y, w0, TN)
    w1 = jnp.concatenate(invert_factor(groups(s1)), axis=0)
    w_ref[0:128, 0:128] = w0
    w_ref[0:128, 128:256] = jnp.zeros((128, 128), f32)
    w_ref[128:256, 0:128] = -exact(w1, z)
    w_ref[128:256, 128:256] = w1


def factor(packed, cross):
    return pl.pallas_call(
        factor_kernel,
        out_shape=jax.ShapeDtypeStruct((256, 256), f32),
        cost_estimate=pl.CostEstimate(flops=2 * 256**3, bytes_accessed=500000, transcendentals=256),
    )(packed, cross)


def halves(x):
    high = x.astype(bf16)
    return high, (x - high.astype(f32)).astype(bf16)


def product(a, b, dims=(((1,), (0,)), ((), ()))):
    (ah, al), (bh, bl) = a, b
    dot = lambda p, q: lax.dot_general(p, q, dims, preferred_element_type=f32)
    return dot(ah, bh) + (dot(ah, bl) + dot(al, bh))


def update_kernel(place_ref, x_ref, ra_ref, rb_ref, ha_ref, hb_ref, w_ref, o_ref, out_ref, sem):
    w = halves(w_ref[...])
    cols = jnp.concatenate(
        [jnp.concatenate([h[:, c, :] for c in range(8)], axis=1) for h in (ha_ref, hb_ref)], axis=0
    )
    z = halves(product(w, halves(cols)))
    y = [
        halves(product(halves(jnp.concatenate([ra_ref[a], rb_ref[a]], axis=1)), w, NT))
        for a in range(8)
    ]
    keep_row = place_ref[0] >= 2
    keep_col = place_ref[1] >= 2
    copies = []
    for a in range(8):
        v = x_ref[a] - product(y[a], z).reshape(128, 8, 128)
        if a == 0:
            v = jnp.where(keep_row, v, 0.0)
        c = lax.broadcasted_iota(jnp.int32, v.shape, 1)
        out_ref[a] = jnp.where(jnp.logical_or(keep_col, c > 0), v, 0.0)
        copy = pltpu.make_async_copy(out_ref.at[a], o_ref.at[a], sem.at[a])
        copy.start()
        copies.append(copy)
    for copy in copies:
        copy.wait()


def update(place, x, ra, rb, ha, hb, w):
    vmem = pl.BlockSpec(memory_space=pltpu.VMEM)
    return pl.pallas_call(
        update_kernel,
        in_specs=[pl.BlockSpec(memory_space=pltpu.SMEM)] + [vmem] * 6,
        out_specs=pl.BlockSpec(memory_space=pl.ANY),
        scratch_shapes=[pltpu.VMEM((8, 128, 8, 128), f32), pltpu.SemaphoreType.DMA((8,))],
        out_shape=jax.ShapeDtypeStruct((8, 128, 8, 128), f32),
        compiler_params=pltpu.CompilerParams(vmem_limit_bytes=40 * 1024 * 1024),
        cost_estimate=pl.CostEstimate(flops=6 * 1024**2 * 256, bytes_accessed=8 * 1024**2, transcendentals=0),
    )(place, x, ra, rb, ha, hb, w)


def spread_pivots(coupling, diagonal, x, y, z, core):
    own = coupling[0, :, 0, :]
    r = lax.broadcasted_iota(jnp.int32, (128, 128), 0)
    c = lax.broadcasted_iota(jnp.int32, (128, 128), 1)
    own = own + jnp.where((r == c) & (x == core), diagonal[0][None, :], 0.0)
    moves = {(0, 0): (1, 0), (1, 1): (0, 0), (0, 1): (1, 1)}
    first = send(
        own,
        lambda x, y, z, k: (moves[x, k][0], 0, 0, moves[x, k][1]) if y == z == 0 and (x, k) in moves else None,
    )
    second = send(own, lambda x, y, z, k: (1, 0, 0, 0) if (x, y, z, k) == (1, 0, 0, 1) else None)
    s0 = jnp.where(x == 0, own, first)
    s1 = jnp.where(x == 0, first, second)
    packed = jnp.where(r >= c, s0, s1)
    packed = jnp.where(core == 0, packed, jnp.where(x == 0, own, first))
    last = jnp.sum(jnp.where(r == c, s1, 0.0), axis=0, keepdims=True)
    held = jnp.concatenate([packed, jnp.broadcast_to(last, (8, 128))], axis=0)
    held = jnp.where((y == 0) & (z == 0) & (x < 2), held, 0.0)
    held += send(held, lambda x, y, z, k: (x + 2, y, z, k) if x < 2 and y == z == 0 else None)
    held += send(held, lambda x, y, z, k: (x, y + 2, z, k) if y == z == 0 else None)
    held += send(held, lambda x, y, z, k: (x, y + 1, z, k) if y % 2 == z == 0 else None)
    held += send(held, lambda x, y, z, k: (x, y, z + 4, k) if z == 0 else None)
    held += send(held, lambda x, y, z, k: (x, y, z + 2, k) if z % 4 == 0 else None)
    held += send(held, lambda x, y, z, k: (x, y, z + 1, k) if z % 2 == 0 else None)
    other = send(held, lambda x, y, z, k: (x, y, z, 1 - k))
    return jnp.where(core == 0, held, other), jnp.where(core == 0, other, held)[0:128]


def spread_rows(coupling, x, y, z, core):
    own = jnp.where(z == 0, coupling[:, :, 0, :], 0.0)
    near = send(own, lambda x, y, z, k: (x, y, 3, k) if z == 0 else None)
    far = send(own, lambda x, y, z, k: (x, y, 5, k) if z == 0 else None)
    held = own + near + far
    up = {0: 1, 3: 4, 5: 6}
    down = {0: 7, 3: 2}
    near = send(held, lambda x, y, z, k: (x, y, up[z], k) if z in up else None)
    far = send(held, lambda x, y, z, k: (x, y, down[z], k) if z in down else None)
    held = held + near + far
    other = send(held, lambda x, y, z, k: (x, y, z, 1 - k))
    return jnp.where(core == 0, held, other), jnp.where(core == 0, other, held)


def spread_cols(coupling, x, y, z, core):
    own = coupling[0]
    held = jnp.where(y == 0, own, 0.0)
    for n in (1, 3, 2):
        held += send(own, lambda x, y, z, k: (x, n, z, k) if x < 2 and y == 0 else None)
    got = []
    for to in ({0: 1, 1: 0}, {0: 3, 1: 2}, {0: 2, 1: 3}):
        got.append(send(held, lambda x, y, z, k: (to[x], y, z, k) if x < 2 else None))
    pick = lambda n, a, b, c, d: jnp.where(n == 0, a, jnp.where(n == 1, b, jnp.where(n == 2, c, d)))
    return pick(x, held, got[0], got[2], got[1]), pick(x, got[0], held, got[1], got[2])


def on_device(coupling, diagonal):
    row = lax.axis_index("prow")
    col = lax.axis_index("pcol")
    here = place_of(row, col)
    packed, cross = spread_pivots(coupling, diagonal, *here)
    ra, rb = spread_rows(coupling, *here)
    ha, hb = spread_cols(coupling, *here)
    w = factor(packed, cross)
    place = jnp.stack([row, col]).astype(jnp.int32)
    return update(place, coupling, ra, rb, ha, hb, w)


def solution(mesh):
    return jax.shard_map(
        on_device,
        mesh=mesh,
        in_specs=(P(None, "prow", None, "pcol"), P(None, "prow")),
        out_specs=P(None, "prow", None, "pcol"),
        check_vma=False,
    )
```

time: 666 us -> 94.8 us (0.14)
  the two profiles are of different devices: /device:TPU:1 before, /device:TPU:16 now
where the time goes in v1:
time: 94.8 us; the launch traced here: 94.1 us
  waiting for transfers between devices  39.7 us (42%)
  starting transfers between devices  27.1 us (29%)
  Pallas kernels  17.1 us (18%)
  local copies, waits for them, and re-layouts  5.34 us (6%)
  other arithmetic  4.34 us (5%)
    ppermute x20, waiting for transfers between devices, send(): return lax.ppermute(value, AXES, pairs)  39.7 us
    ppermute x20, starting transfers between devices, send(): return lax.ppermute(value, AXES, pairs)  27.1 us
    pallas_call x1, Pallas kernels, factor(): pl.pallas_call(factor_kernel, out_shape=jax.ShapeDtypeStruct((256, 256),...  11.6 us
    pallas_call x1, Pallas kernels, update(): pl.pallas_call(update_kernel, in_specs=[pl.BlockSpec(memory_space=pltpu.S...  5.43 us
    slice x1, local copies, waits for them, and re-layouts, spread_rows(): own = jnp.where(z == 0, coupling[:, :, 0, :], 0.0)  2.49 us
  transfers between devices with their start and end apart: 20, of which 5 were waited for; matrix products, arithmetic and copies ran while one was open for 8% of the time, Pallas kernels for 12%

profile of v1, /device:TPU:16, one launch (start us, length us, event | category | flops | bytes accessed | tf_op | source)
XLA Modules:
  0.0 94.1 jit_solution(7115091293661162234)
XLA Ops:
  4.0 1.3 %collective-permute-start.14 = (f32[136,128]{1,0:T(8,128)S(1)}, f32[136,128]{1,0:T(8,128)S(1)}, u32[]{:S(2)}, u32[]{:S(2)}) collective-permute-start(f32[136,128]{1,0:T(8,128)S(1)} %fusion.1), channel_id=1, source_target_pairs={{0,128},{1,129},{16,144},{17,145},{32,160},{33,161},{48,176},{49,1... | collective-permute-start | bytes 208904 | tf_op jit(solution)/shard_map/ppermute | solution.py:28
  5.3 2.5 %slice.15 = f32[8,128,1,128]{3,2,1,0:T(1,128)S(1)} slice(f32[8,128,8,128]{3,2,1,0:T(8,128)} %x_ref.1), slice={[0:8], [0:128], [0:1], [0:128]} | slice | bytes 1048576 | tf_op jit(solution)/shard_map/slice | solution.py:180
  7.8 9.2 %collective-permute-done.14 = f32[136,128]{1,0:T(8,128)S(1)} collective-permute-done((f32[136,128]{1,0:T(8,128)S(1)}, f32[136,128]{1,0:T(8,128)S(1)}, u32[]{:S(2)}, u32[]{:S(2)}) %collective-permute-start.14) | collective-permute-done | bytes 69664 | tf_op jit(solution)/shard_map/ppermute | solution.py:28
  17.0 1.3 %collective-permute-start.15 = (f32[136,128]{1,0:T(8,128)S(1)}, f32[136,128]{1,0:T(8,128)S(1)}, u32[]{:S(2)}, u32[]{:S(2)}) collective-permute-start(f32[136,128]{1,0:T(8,128)S(1)} %add.62), channel_id=1, source_target_pairs={{0,64},{1,65},{16,80},{17,81},{32,96},{33,97},{48,112},{49,113},{1... | collective-permute-start | bytes 208904 | tf_op jit(solution)/shard_map/ppermute | solution.py:28
  18.4 1.3 %collective-permute-start.1 = (f32[8,128,128]{2,1,0:T(8,128)S(1)}, f32[8,128,128]{2,1,0:T(8,128)S(1)}, u32[]{:S(2)}, u32[]{:S(2)}) collective-permute-start(f32[8,128,128]{2,1,0:T(8,128)S(1)} %select_bitcast_fusion), channel_id=1, source_target_pairs={{0,10},{1,11},{16,26},{17,27},{32,42},{33,43},{48,58},{49,59},{64,... | collective-permute-start | bytes 1572872 | tf_op jit(solution)/shard_map/ppermute | solution.py:28
  19.7 1.3 %collective-permute-start = (f32[8,128,128]{2,1,0:T(8,128)S(1)}, f32[8,128,128]{2,1,0:T(8,128)S(1)}, u32[]{:S(2)}, u32[]{:S(2)}) collective-permute-start(f32[8,128,128]{2,1,0:T(8,128)S(1)} %select_bitcast_fusion), channel_id=1, source_target_pairs={{0,6},{1,7},{16,22},{17,23},{32,38},{33,39},{48,54},{49,55},{64,70... | collective-permute-start | bytes 1572872 | tf_op jit(solution)/shard_map/ppermute | solution.py:28
  21.1 1.3 %collective-permute-start.16 = (f32[136,128]{1,0:T(8,128)S(1)}, f32[136,128]{1,0:T(8,128)S(1)}, u32[]{:S(2)}, u32[]{:S(2)}) collective-permute-start(f32[136,128]{1,0:T(8,128)S(1)} %add.63), channel_id=1, source_target_pairs={{0,8},{1,9},{16,24},{17,25},{32,40},{33,41},{48,56},{49,57},{64,72... | collective-permute-start | bytes 208904 | tf_op jit(solution)/shard_map/ppermute | solution.py:28
  22.4 10.4 %collective-permute-done.16 = f32[136,128]{1,0:T(8,128)S(1)} collective-permute-done((f32[136,128]{1,0:T(8,128)S(1)}, f32[136,128]{1,0:T(8,128)S(1)}, u32[]{:S(2)}, u32[]{:S(2)}) %collective-permute-start.16) | collective-permute-done | bytes 69664 | tf_op jit(solution)/shard_map/ppermute | solution.py:28
  32.8 1.3 %collective-permute-start.17 = (f32[136,128]{1,0:T(8,128)S(1)}, f32[136,128]{1,0:T(8,128)S(1)}, u32[]{:S(2)}, u32[]{:S(2)}) collective-permute-start(f32[136,128]{1,0:T(8,128)S(1)} %add.64), channel_id=1, source_target_pairs={{0,4},{1,5},{8,12},{9,13},{16,20},{17,21},{24,28},{25,29},{32,36},... | collective-permute-start | bytes 208904 | tf_op jit(solution)/shard_map/ppermute | solution.py:28
  34.1 1.1 %slice_bitcast_fusion = f32[128,8,128]{2,1,0:T(8,128)S(1)} fusion(f32[8,128,8,128]{3,2,1,0:T(8,128)} %x_ref.1), kind=kLoop, calls=%fused_computation.3 | loop fusion | bytes 1048576 | tf_op jit(solution)/shard_map/squeeze | solution.py:194
  36.6 1.3 %collective-permute-start.7 = (f32[128,8,128]{2,1,0:T(8,128)S(1)}, f32[128,8,128]{2,1,0:T(8,128)S(1)}, u32[]{:S(2)}, u32[]{:S(2)}) collective-permute-start(f32[128,8,128]{2,1,0:T(8,128)S(1)} %slice_bitcast_fusion), channel_id=1, source_target_pairs={{0,128},{1,129},{2,130},{3,131},{4,132},{5,133},{6,134},{7,135},{8... | collective-permute-start | bytes 1572872 | tf_op jit(solution)/shard_map/ppermute | solution.py:28
  37.9 1.3 %collective-permute-start.18 = (f32[136,128]{1,0:T(8,128)S(1)}, f32[136,128]{1,0:T(8,128)S(1)}, u32[]{:S(2)}, u32[]{:S(2)}) collective-permute-start(f32[136,128]{1,0:T(8,128)S(1)} %add.65), channel_id=1, source_target_pairs={{0,2},{1,3},{4,6},{5,7},{8,10},{9,11},{12,14},{13,15},{16,18},{17,... | collective-permute-start | bytes 208904 | tf_op jit(solution)/shard_map/ppermute | solution.py:28
  39.3 2.1 %collective-permute-start.3 = (f32[8,128,128]{2,1,0:T(8,128)S(1)}, f32[8,128,128]{2,1,0:T(8,128)}, u32[]{:S(2)}, u32[]{:S(2)}) collective-permute-start(f32[8,128,128]{2,1,0:T(8,128)S(1)} %add_add_fusion.2), channel_id=1, source_target_pairs={{0,14},{1,15},{6,4},{7,5},{16,30},{17,31},{22,20},{23,21},{32,46},... | collective-permute-start | bytes 1572872 | tf_op jit(solution)/shard_map/ppermute | solution.py:28
  41.4 4.8 %collective-permute-start.2 = (f32[8,128,128]{2,1,0:T(8,128)S(1)}, f32[8,128,128]{2,1,0:T(8,128)}, u32[]{:S(2)}, u32[]{:S(2)}) collective-permute-start(f32[8,128,128]{2,1,0:T(8,128)S(1)} %add_add_fusion.2), channel_id=1, source_target_pairs={{0,2},{1,3},{6,8},{7,9},{10,12},{11,13},{16,18},{17,19},{22,24},{2... | collective-permute-start | bytes 1572872 | tf_op jit(solution)/shard_map/ppermute | solution.py:28
  46.4 15.1 %collective-permute-done.7 = f32[128,8,128]{2,1,0:T(8,128)S(1)} collective-permute-done((f32[128,8,128]{2,1,0:T(8,128)S(1)}, f32[128,8,128]{2,1,0:T(8,128)S(1)}, u32[]{:S(2)}, u32[]{:S(2)}) %collective-permute-start.7) | collective-permute-done | bytes 524320 | tf_op jit(solution)/shard_map/ppermute | solution.py:28
  61.6 1.2 %add_add_fusion = f32[128,8,128]{2,1,0:T(8,128)S(1)} fusion(f32[128,8,128]{2,1,0:T(8,128)S(1)} %collective-permute-done.7, f32[128,8,128]{2,1,0:T(8,128)S(1)} %collective-permute-done.6, f32[128,8,128]{2,1,0:T(8,128)S(1)} %collective-permute-done.5, pred[]{:T(512)S(6)} %eq.45, f32[8,128,8,128]{3,2,1,0:T(8,128)} %x_ref.1), kind=kLoop, calls=%fused_computation.2 | loop fusion | flops 524288 | bytes 2621441 | tf_op jit(solution)/shard_map/add | solution.py:197
  62.7 1.3 %collective-permute-start.10 = (f32[128,8,128]{2,1,0:T(8,128)S(1)}, f32[128,8,128]{2,1,0:T(8,128)S(1)}, u32[]{:S(2)}, u32[]{:S(2)}) collective-permute-start(f32[128,8,128]{2,1,0:T(8,128)S(1)} %add_add_fusion), channel_id=1, source_target_pairs={{0,48},{1,49},{2,50},{3,51},{4,52},{5,53},{6,54},{7,55},{8,56},{9,... | collective-permute-start | bytes 1572872 | tf_op jit(solution)/shard_map/ppermute | solution.py:28
  64.1 1.3 %collective-permute-start.9 = (f32[128,8,128]{2,1,0:T(8,128)S(1)}, f32[128,8,128]{2,1,0:T(8,128)S(1)}, u32[]{:S(2)}, u32[]{:S(2)}) collective-permute-start(f32[128,8,128]{2,1,0:T(8,128)S(1)} %add_add_fusion), channel_id=1, source_target_pairs={{0,32},{1,33},{2,34},{3,35},{4,36},{5,37},{6,38},{7,39},{8,40},{9,... | collective-permute-start | bytes 1572872 | tf_op jit(solution)/shard_map/ppermute | solution.py:28
  65.4 3.4 %collective-permute-start.8 = (f32[128,8,128]{2,1,0:T(8,128)S(1)}, f32[128,8,128]{2,1,0:T(8,128)S(1)}, u32[]{:S(2)}, u32[]{:S(2)}) collective-permute-start(f32[128,8,128]{2,1,0:T(8,128)S(1)} %add_add_fusion), channel_id=1, source_target_pairs={{0,16},{1,17},{2,18},{3,19},{4,20},{5,21},{6,22},{7,23},{8,24},{9,... | collective-permute-start | bytes 1572872 | tf_op jit(solution)/shard_map/ppermute | solution.py:28
  69.5 1.3 %add_add_fusion.1 = f32[8,128,128]{2,1,0:T(8,128)S(1)} fusion(f32[8,128,128]{2,1,0:T(8,128)} %collective-permute-done.3, f32[8,128,128]{2,1,0:T(8,128)S(1)} %add_add_fusion.2, f32[8,128,128]{2,1,0:T(8,128)} %collective-permute-done.2), kind=kLoop, calls=%fused_computation.4 | loop fusion | flops 262144 | bytes 2097152 | tf_op jit(solution)/shard_map/add | solution.py:188
  71.7 11.6 %shard_map.28.w_ref = f32[256,256]{1,0:T(8,128)} custom-call(f32[136,128]{1,0:T(8,128)} %broadcast_select_fusion.2.packed_ref, f32[128,128]{1,0:T(8,128)} %slice_select_fusion.cross_ref), custom_call_target="tpu_custom_call" | custom-call | flops 33554432 | bytes 500000 | tf_op jit(solution)/shard_map/pallas_call | solution.py:94
  83.3 1.6 %collective-permute-done.10 = f32[128,8,128]{2,1,0:T(8,128)S(1)} collective-permute-done((f32[128,8,128]{2,1,0:T(8,128)S(1)}, f32[128,8,128]{2,1,0:T(8,128)S(1)}, u32[]{:S(2)}, u32[]{:S(2)}) %collective-permute-start.10) | collective-permute-done | bytes 524320 | tf_op jit(solution)/shard_map/ppermute | solution.py:28
  84.9 3.3 %collective-permute-done.8 = f32[128,8,128]{2,1,0:T(8,128)S(1)} collective-permute-done((f32[128,8,128]{2,1,0:T(8,128)S(1)}, f32[128,8,128]{2,1,0:T(8,128)S(1)}, u32[]{:S(2)}, u32[]{:S(2)}) %collective-permute-start.8) | collective-permute-done | bytes 524320 | tf_op jit(solution)/shard_map/ppermute | solution.py:28
  88.5 5.4 %shard_map.29 = f32[8,128,8,128]{3,2,1,0:T(8,128)} custom-call(s32[2]{0:T(128)S(1)} %pad_add_fusion.place_ref, f32[8,128,8,128]{3,2,1,0:T(8,128)S(1)} %copy-done, f32[8,128,128]{2,1,0:T(8,128)S(1)} %get-tuple-element.8.ra_ref, f32[8,128,128]{2,1,0:T(8,128)S(1)} %get-tuple-element.7.rb_ref, f32[128,8,128]{2,1,0:T(8,128)S(1)} %get-tuple-element.6.ha_ref, ...), custom_call_target="tpu_custom_call" | custom-call | flops 1610612736 | bytes 8388608 | tf_op jit(solution)/shard_map/pallas_call | solution.py:140
  (45 shorter events, 7.4 us)
Async XLA Ops:
  1.8 1.4 %collective-permute-start.12 = (f32[128,128]{1,0:T(8,128)S(1)}, f32[128,128]{1,0:T(8,128)S(1)}, u32[]{:S(2)}, u32[]{:S(2)}) collective-permute-start(f32[128,128]{1,0:T(8,128)S(1)} %select_add_fusion), channel_id=1, source_target_pairs={{17,16}} | collective-permute-start | bytes 196616 | tf_op jit(solution)/shard_map/ppermute | solution.py:28
  2.5 0.7 collective-permute-start.11
  3.3 0.7 collective-permute-start.13
  4.0 13.0 %collective-permute-start.14 = (f32[136,128]{1,0:T(8,128)S(1)}, f32[136,128]{1,0:T(8,128)S(1)}, u32[]{:S(2)}, u32[]{:S(2)}) collective-permute-start(f32[136,128]{1,0:T(8,128)S(1)} %fusion.1), channel_id=1, source_target_pairs={{0,128},{1,129},{16,144},{17,145},{32,160},{33,161},{48,176},{49,1... | collective-permute-start | bytes 208904 | tf_op jit(solution)/shard_map/ppermute | solution.py:28
  17.0 4.0 %collective-permute-start.15 = (f32[136,128]{1,0:T(8,128)S(1)}, f32[136,128]{1,0:T(8,128)S(1)}, u32[]{:S(2)}, u32[]{:S(2)}) collective-permute-start(f32[136,128]{1,0:T(8,128)S(1)} %add.62), channel_id=1, source_target_pairs={{0,64},{1,65},{16,80},{17,81},{32,96},{33,97},{48,112},{49,113},{1... | collective-permute-start | bytes 208904 | tf_op jit(solution)/shard_map/ppermute | solution.py:28
  18.4 19.5 %collective-permute-start.1 = (f32[8,128,128]{2,1,0:T(8,128)S(1)}, f32[8,128,128]{2,1,0:T(8,128)S(1)}, u32[]{:S(2)}, u32[]{:S(2)}) collective-permute-start(f32[8,128,128]{2,1,0:T(8,128)S(1)} %select_bitcast_fusion), channel_id=1, source_target_pairs={{0,10},{1,11},{16,26},{17,27},{32,42},{33,43},{48,58},{49,59},{64,... | collective-permute-start | bytes 1572872 | tf_op jit(solution)/shard_map/ppermute | solution.py:28
  19.7 19.5 %collective-permute-start = (f32[8,128,128]{2,1,0:T(8,128)S(1)}, f32[8,128,128]{2,1,0:T(8,128)S(1)}, u32[]{:S(2)}, u32[]{:S(2)}) collective-permute-start(f32[8,128,128]{2,1,0:T(8,128)S(1)} %select_bitcast_fusion), channel_id=1, source_target_pairs={{0,6},{1,7},{16,22},{17,23},{32,38},{33,39},{48,54},{49,55},{64,70... | collective-permute-start | bytes 1572872 | tf_op jit(solution)/shard_map/ppermute | solution.py:28
  21.1 11.7 %collective-permute-start.16 = (f32[136,128]{1,0:T(8,128)S(1)}, f32[136,128]{1,0:T(8,128)S(1)}, u32[]{:S(2)}, u32[]{:S(2)}) collective-permute-start(f32[136,128]{1,0:T(8,128)S(1)} %add.63), channel_id=1, source_target_pairs={{0,8},{1,9},{16,24},{17,25},{32,40},{33,41},{48,56},{49,57},{64,72... | collective-permute-start | bytes 208904 | tf_op jit(solution)/shard_map/ppermute | solution.py:28
  32.8 3.8 %collective-permute-start.17 = (f32[136,128]{1,0:T(8,128)S(1)}, f32[136,128]{1,0:T(8,128)S(1)}, u32[]{:S(2)}, u32[]{:S(2)}) collective-permute-start(f32[136,128]{1,0:T(8,128)S(1)} %add.64), channel_id=1, source_target_pairs={{0,4},{1,5},{8,12},{9,13},{16,20},{17,21},{24,28},{25,29},{32,36},... | collective-permute-start | bytes 208904 | tf_op jit(solution)/shard_map/ppermute | solution.py:28
  35.2 11.1 %collective-permute-start.6 = (f32[128,8,128]{2,1,0:T(8,128)S(1)}, f32[128,8,128]{2,1,0:T(8,128)S(1)}, u32[]{:S(2)}, u32[]{:S(2)}) collective-permute-start(f32[128,8,128]{2,1,0:T(8,128)S(1)} %slice_bitcast_fusion), channel_id=1, source_target_pairs={{0,192},{1,193},{2,194},{3,195},{4,196},{5,197},{6,198},{7,199},{8... | collective-permute-start | bytes 1572872 | tf_op jit(solution)/shard_map/ppermute | solution.py:28
  35.9 10.5 %collective-permute-start.5 = (f32[128,8,128]{2,1,0:T(8,128)S(1)}, f32[128,8,128]{2,1,0:T(8,128)S(1)}, u32[]{:S(2)}, u32[]{:S(2)}) collective-permute-start(f32[128,8,128]{2,1,0:T(8,128)S(1)} %slice_bitcast_fusion), channel_id=1, source_target_pairs={{0,64},{1,65},{2,66},{3,67},{4,68},{5,69},{6,70},{7,71},{8,72},{9,... | collective-permute-start | bytes 1572872 | tf_op jit(solution)/shard_map/ppermute | solution.py:28
  36.6 25.0 %collective-permute-start.7 = (f32[128,8,128]{2,1,0:T(8,128)S(1)}, f32[128,8,128]{2,1,0:T(8,128)S(1)}, u32[]{:S(2)}, u32[]{:S(2)}) collective-permute-start(f32[128,8,128]{2,1,0:T(8,128)S(1)} %slice_bitcast_fusion), channel_id=1, source_target_pairs={{0,128},{1,129},{2,130},{3,131},{4,132},{5,133},{6,134},{7,135},{8... | collective-permute-start | bytes 1572872 | tf_op jit(solution)/shard_map/ppermute | solution.py:28
  37.9 3.5 %collective-permute-start.18 = (f32[136,128]{1,0:T(8,128)S(1)}, f32[136,128]{1,0:T(8,128)S(1)}, u32[]{:S(2)}, u32[]{:S(2)}) collective-permute-start(f32[136,128]{1,0:T(8,128)S(1)} %add.65), channel_id=1, source_target_pairs={{0,2},{1,3},{4,6},{5,7},{8,10},{9,11},{12,14},{13,15},{16,18},{17,... | collective-permute-start | bytes 208904 | tf_op jit(solution)/shard_map/ppermute | solution.py:28
  39.3 30.1 %collective-permute-start.3 = (f32[8,128,128]{2,1,0:T(8,128)S(1)}, f32[8,128,128]{2,1,0:T(8,128)}, u32[]{:S(2)}, u32[]{:S(2)}) collective-permute-start(f32[8,128,128]{2,1,0:T(8,128)S(1)} %add_add_fusion.2), channel_id=1, source_target_pairs={{0,14},{1,15},{6,4},{7,5},{16,30},{17,31},{22,20},{23,21},{32,46},... | collective-permute-start | bytes 1572872 | tf_op jit(solution)/shard_map/ppermute | solution.py:28
  41.4 28.0 %collective-permute-start.2 = (f32[8,128,128]{2,1,0:T(8,128)S(1)}, f32[8,128,128]{2,1,0:T(8,128)}, u32[]{:S(2)}, u32[]{:S(2)}) collective-permute-start(f32[8,128,128]{2,1,0:T(8,128)S(1)} %add_add_fusion.2), channel_id=1, source_target_pairs={{0,2},{1,3},{6,8},{7,9},{10,12},{11,13},{16,18},{17,19},{22,24},{2... | collective-permute-start | bytes 1572872 | tf_op jit(solution)/shard_map/ppermute | solution.py:28
  46.3 19.1 %collective-permute-start.19 = (f32[136,128]{1,0:T(8,128)S(1)}, f32[136,128]{1,0:T(8,128)S(1)}, u32[]{:S(2)}, u32[]{:S(2)}) collective-permute-start(f32[136,128]{1,0:T(8,128)S(1)} %add.66), channel_id=1, source_target_pairs={{0,1},{1,0},{2,3},{3,2},{4,5},{5,4},{6,7},{7,6},{8,9},{9,8},{10,11... | collective-permute-start | bytes 208904 | tf_op jit(solution)/shard_map/ppermute | solution.py:28
  62.7 22.2 %collective-permute-start.10 = (f32[128,8,128]{2,1,0:T(8,128)S(1)}, f32[128,8,128]{2,1,0:T(8,128)S(1)}, u32[]{:S(2)}, u32[]{:S(2)}) collective-permute-start(f32[128,8,128]{2,1,0:T(8,128)S(1)} %add_add_fusion), channel_id=1, source_target_pairs={{0,48},{1,49},{2,50},{3,51},{4,52},{5,53},{6,54},{7,55},{8,56},{9,... | collective-permute-start | bytes 1572872 | tf_op jit(solution)/shard_map/ppermute | solution.py:28
  64.1 20.9 %collective-permute-start.9 = (f32[128,8,128]{2,1,0:T(8,128)S(1)}, f32[128,8,128]{2,1,0:T(8,128)S(1)}, u32[]{:S(2)}, u32[]{:S(2)}) collective-permute-start(f32[128,8,128]{2,1,0:T(8,128)S(1)} %add_add_fusion), channel_id=1, source_target_pairs={{0,32},{1,33},{2,34},{3,35},{4,36},{5,37},{6,38},{7,39},{8,40},{9,... | collective-permute-start | bytes 1572872 | tf_op jit(solution)/shard_map/ppermute | solution.py:28
  65.4 22.8 %collective-permute-start.8 = (f32[128,8,128]{2,1,0:T(8,128)S(1)}, f32[128,8,128]{2,1,0:T(8,128)S(1)}, u32[]{:S(2)}, u32[]{:S(2)}) collective-permute-start(f32[128,8,128]{2,1,0:T(8,128)S(1)} %add_add_fusion), channel_id=1, source_target_pairs={{0,16},{1,17},{2,18},{3,19},{4,20},{5,21},{6,22},{7,23},{8,24},{9,... | collective-permute-start | bytes 1572872 | tf_op jit(solution)/shard_map/ppermute | solution.py:28
  70.8 17.6 %collective-permute-start.4 = (f32[8,128,128]{2,1,0:T(8,128)S(1)}, f32[8,128,128]{2,1,0:T(8,128)S(1)}, u32[]{:S(2)}, u32[]{:S(2)}) collective-permute-start(f32[8,128,128]{2,1,0:T(8,128)S(1)} %add_add_fusion.1), channel_id=1, source_target_pairs={{0,1},{1,0},{2,3},{3,2},{4,5},{5,4},{6,7},{7,6},{8,9},{9,8},{10,11... | collective-permute-start | bytes 1572872 | tf_op jit(solution)/shard_map/ppermute | solution.py:28
  83.3 5.2 %copy-start = (f32[8,128,8,128]{3,2,1,0:T(8,128)S(1)}, f32[8,128,8,128]{3,2,1,0:T(8,128)}, u32[]{:S(2)}) copy-start(f32[8,128,8,128]{3,2,1,0:T(8,128)} %x_ref.1) | copy-start | bytes 12582916
  83.3 5.2 %copy-start.1 = (f32[256,256]{1,0:T(8,128)S(1)}, f32[256,256]{1,0:T(8,128)}, u32[]{:S(2)}) copy-start(f32[256,256]{1,0:T(8,128)} %shard_map.28.w_ref) | copy-start | bytes 786436

commit v2 on v1

v2 whole, which is shorter than its diff:
```python
import jax
import jax.numpy as jnp
from jax import lax
from jax.experimental import pallas as pl
from jax.experimental.pallas import tpu as pltpu
from jax.sharding import PartitionSpec as P

f32 = jnp.float32
bf16 = jnp.bfloat16
HIGHEST = lax.Precision.HIGHEST
AXES = ("prow", "pcol")
NT = (((1,), (1,)), ((), ()))
TN = (((0,), (0,)), ((), ()))


def place_of(row, col):
    return row & 3, row >> 2, col >> 1, col & 1


def send(value, target):
    pairs = []
    for row in range(16):
        for col in range(16):
            to = target(*place_of(row, col))
            if to is not None:
                x, y, z, core = to
                pairs.append((row * 16 + col, (y * 4 + x) * 16 + z * 2 + core))
    return lax.ppermute(value, AXES, pairs)


def invert_factor(rows):
    sub = lax.broadcasted_iota(jnp.int32, (8, 128), 0)
    lane = lax.broadcasted_iota(jnp.int32, (8, 128), 1)
    spread = lambda v, i: jnp.broadcast_to(v[i:i + 1, :], (8, 128))
    rows = list(rows)
    out = []
    for g in range(16):
        first = 8 * g
        column = lambda i, l: jnp.broadcast_to(rows[i][:, first + l:first + l + 1], (8, 128))
        own = [column(g, l) for l in range(8)]
        below = [[column(i, l) for l in range(8)] for i in range(g + 1, 16)]
        panel = rows[g]
        kept = jnp.zeros((8, 128), f32)
        for p in range(8):
            here = sub == p
            panel = jnp.where(lane == first + p, jnp.where(here, 1.0, 0.0), panel)
            pivot = spread(own[p], p)
            inv = 1.0 / pivot
            factor = own[p] * inv
            row = spread(panel, p)
            kept = jnp.where(here, row * lax.rsqrt(pivot), kept)
            panel = jnp.where(here, row * inv, panel - factor * row)
            for l in range(p + 1, 8):
                mine = spread(own[l], p)
                own[l] = jnp.where(here, mine * inv, own[l] - factor * mine)
        out.append(jnp.where(lane <= sub + first, kept, 0.0))
        cleared = (lane >= first) & (lane < first + 8)
        spreads = [spread(panel, l) for l in range(8)]
        for n, i in enumerate(range(g + 1, 16)):
            acc = jnp.where(cleared, 0.0, rows[i])
            for l in range(8):
                acc = acc - below[n][l] * spreads[l]
            rows[i] = acc
    return out


def exact(a, b, dims=(((1,), (0,)), ((), ()))):
    return lax.dot_general(a, b, dims, precision=HIGHEST, preferred_element_type=f32)


def groups(block):
    return [block[8 * i:8 * i + 8, :] for i in range(16)]


def factor_kernel(core_ref, held_ref, other_ref, w_ref):
    core = core_ref[0]
    first = core == 0
    s0 = jnp.where(first, held_ref[0], other_ref[0])
    cross = jnp.where(first, other_ref[0], held_ref[0])
    s1 = jnp.where(first, other_ref[1], held_ref[1])
    w0 = jnp.concatenate(invert_factor(groups(s0)), axis=0)
    y = exact(w0, cross)
    s1 = s1 - exact(y, y, TN)
    z = exact(y, w0, TN)
    w1 = jnp.concatenate(invert_factor(groups(s1)), axis=0)
    w_ref[0:128, 0:128] = w0
    w_ref[0:128, 128:256] = jnp.zeros((128, 128), f32)
    w_ref[128:256, 0:128] = -exact(w1, z)
    w_ref[128:256, 128:256] = w1


def factor(core, held, other):
    vmem = pl.BlockSpec(memory_space=pltpu.VMEM)
    return pl.pallas_call(
        factor_kernel,
        in_specs=[pl.BlockSpec(memory_space=pltpu.SMEM), vmem, vmem],
        out_specs=vmem,
        out_shape=jax.ShapeDtypeStruct((256, 256), f32),
        cost_estimate=pl.CostEstimate(flops=2 * 256**3, bytes_accessed=500000, transcendentals=256),
    )(core, held, other)


def halves(x):
    high = x.astype(bf16)
    return high, (x - high.astype(f32)).astype(bf16)


def product(a, b, dims=(((1,), (0,)), ((), ()))):
    (ah, al), (bh, bl) = a, b
    dot = lambda p, q: lax.dot_general(p, q, dims, preferred_element_type=f32)
    return dot(ah, bh) + (dot(ah, bl) + dot(al, bh))


def update_kernel(place_ref, x_ref, held_ref, other_ref, h0_ref, h1_ref, h2_ref, h3_ref, w_ref, o_ref, out_ref, col_ref, sem):
    w = halves(w_ref[...])
    y_place = place_ref[0] // 4
    for n, h in enumerate((h0_ref, h1_ref, h2_ref, h3_ref)):
        start = pl.multiple_of(32 * lax.rem(y_place + 4 - n, 4), 32)
        for p in range(2):
            col_ref[p, pl.ds(start, 32)] = h[p]
    cols = jnp.concatenate(
        [jnp.concatenate([col_ref[p, :, c, :] for c in range(8)], axis=1) for p in range(2)], axis=0
    )
    first = lax.rem(place_ref[1], 2) == 0
    z = halves(product(w, halves(cols)))
    y = [
        halves(product(halves(jnp.concatenate(
            [jnp.where(first, held_ref[a], other_ref[a]), jnp.where(first, other_ref[a], held_ref[a])], axis=1
        )), w, NT))
        for a in range(8)
    ]
    keep_row = place_ref[0] >= 2
    keep_col = place_ref[1] >= 2
    copies = []
    for a in range(8):
        v = x_ref[a] - product(y[a], z).reshape(128, 8, 128)
        if a == 0:
            v = jnp.where(keep_row, v, 0.0)
        c = lax.broadcasted_iota(jnp.int32, v.shape, 1)
        out_ref[a] = jnp.where(jnp.logical_or(keep_col, c > 0), v, 0.0)
        copy = pltpu.make_async_copy(out_ref.at[a], o_ref.at[a], sem.at[a])
        copy.start()
        copies.append(copy)
    for copy in copies:
        copy.wait()


def update(place, x, rows, cols, w):
    vmem = pl.BlockSpec(memory_space=pltpu.VMEM)
    return pl.pallas_call(
        update_kernel,
        in_specs=[pl.BlockSpec(memory_space=pltpu.SMEM)] + [vmem] * 8,
        out_specs=pl.BlockSpec(memory_space=pl.ANY),
        scratch_shapes=[pltpu.VMEM((8, 128, 8, 128), f32), pltpu.VMEM((2, 128, 8, 128), f32), pltpu.SemaphoreType.DMA((8,))],
        out_shape=jax.ShapeDtypeStruct((8, 128, 8, 128), f32),
        compiler_params=pltpu.CompilerParams(vmem_limit_bytes=40 * 1024 * 1024),
        cost_estimate=pl.CostEstimate(flops=6 * 1024**2 * 256, bytes_accessed=8 * 1024**2, transcendentals=0),
    )(place, x, *rows, *cols, w)


def turns(values, turned):
    return [send(v, lambda x, y, z, k: (*turned(n, x, y), z, k)) for n, v in zip((1, 2, 3), values)]


def along_x(n, x, y):
    return (x + n) % 4, y


def along_y(n, x, y):
    return x, (y + n) % 4


def pick(i, options):
    out = options[3]
    for n in (2, 1, 0):
        out = jnp.where(i == n, options[n], out)
    return out


def columns_zero_and_one(own, got, x):
    ways = [own, *got]
    return jnp.stack([pick(x, ways), pick((x + 3) & 3, ways)])


def along_z(held):
    near = send(held, lambda x, y, z, k: (x, y, 3, k) if z == 0 else None)
    far = send(held, lambda x, y, z, k: (x, y, 5, k) if z == 0 else None)
    held = held + near + far
    up = {0: 1, 3: 4, 5: 6}
    down = {0: 7, 3: 2}
    near = send(held, lambda x, y, z, k: (x, y, up[z], k) if z in up else None)
    far = send(held, lambda x, y, z, k: (x, y, down[z], k) if z in down else None)
    return held + near + far


def swap(held):
    return send(held, lambda x, y, z, k: (x, y, z, 1 - k))


def spread_pivots(coupling, diagonal, x, y, z, core):
    own = coupling[0, :, 0, :]
    r = lax.broadcasted_iota(jnp.int32, (128, 128), 0)
    c = lax.broadcasted_iota(jnp.int32, (128, 128), 1)
    own = own + jnp.where((r == c) & (x == core), diagonal[0][None, :], 0.0)
    own = along_z(jnp.where(z == 0, own, 0.0))
    own = pick(y, [own, *turns([own] * 3, along_y)])
    held = columns_zero_and_one(own, turns([own] * 3, along_x), x)
    return held, swap(held)


def spread_rows(coupling, x, y, z, core):
    held = along_z(jnp.where(z == 0, coupling[:, :, 0, :], 0.0))
    return held, swap(held)


def spread_cols(coupling, x, y, z, core):
    quarters = [coupling[0, 32 * n:32 * n + 32] for n in range(4)]
    own = pick(y, [quarters[0], *turns(quarters[1:], along_y)])
    both = columns_zero_and_one(own, turns([own] * 3, along_x), x)
    return [both, *turns([both] * 3, along_y)]


def on_device(coupling, diagonal):
    row = lax.axis_index("prow")
    col = lax.axis_index("pcol")
    here = place_of(row, col)
    pivots = spread_pivots(coupling, diagonal, *here)
    rows = spread_rows(coupling, *here)
    cols = spread_cols(coupling, *here)
    place = jnp.stack([row, col]).astype(jnp.int32)
    w = factor(place[1:] & 1, *pivots)
    return update(place, coupling, rows, cols, w)


def solution(mesh):
    return jax.shard_map(
        on_device,
        mesh=mesh,
        in_specs=(P(None, "prow", None, "pcol"), P(None, "prow")),
        out_specs=P(None, "prow", None, "pcol"),
        check_vma=False,
    )
```

time: 94.8 us -> 87.5 us (0.923)
  the two profiles are of different devices: /device:TPU:16 before, /device:TPU:1 now
where the time goes in v2:
time: 87.5 us; the launch traced here: 87.1 us
  starting transfers between devices  51.5 us (59%)
  Pallas kernels  17.2 us (20%)
  local copies, waits for them, and re-layouts  9.09 us (10%)
  waiting for transfers between devices  7.5 us (9%)
  other arithmetic  1.37 us (2%)
    ppermute x25, starting transfers between devices, send(): return lax.ppermute(value, AXES, pairs)  51.5 us
    pallas_call x1, Pallas kernels, factor(): pl.pallas_call(factor_kernel, in_specs=[pl.BlockSpec(memory_space=pltpu.S...  11.7 us
    ppermute x25, waiting for transfers between devices, send(): return lax.ppermute(value, AXES, pairs)  7.5 us
    pallas_call x1, Pallas kernels, update(): pl.pallas_call(update_kernel, in_specs=[pl.BlockSpec(memory_space=pltpu.S...  5.54 us
    unnamed x8, local copies, waits for them, and re-layouts  3.77 us
    slice x1, local copies, waits for them, and re-layouts, spread_rows(): held = along_z(jnp.where(z == 0, coupling[:, :, 0, :], 0.0))  2.49 us
  transfers between devices with their start and end apart: 25, of which 4 were waited for; matrix products, arithmetic and copies ran while one was open for 6% of the time, Pallas kernels for 13%

profile of v2, /device:TPU:1, one launch (start us, length us, event | category | flops | bytes accessed | tf_op | source)
XLA Modules:
  0.0 87.1 jit_solution(14286323629511607987)
XLA Ops:
  0.7 1.1 %slice.26 = f32[1,128,1,128]{3,2,1,0:T(1,128)S(1)} slice(f32[8,128,8,128]{3,2,1,0:T(8,128)} %x_ref.1), slice={[0:1], [0:128], [0:1], [0:128]} | slice | bytes 131072 | tf_op jit(solution)/shard_map/slice | solution.py:201
  1.8 9.2 %collective-permute-start.15 = (f32[128,128]{1,0:T(8,128)S(1)}, f32[128,128]{1,0:T(8,128)S(1)}, u32[]{:S(2)}, u32[]{:S(2)}) collective-permute-start(f32[128,128]{1,0:T(8,128)S(1)} %add_select_fusion), channel_id=1, source_target_pairs={{0,10},{1,11},{16,26},{17,27},{32,42},{33,43},{48,58},{49,59},{64,... | collective-permute-start | bytes 196616 | tf_op jit(solution)/shard_map/ppermute | solution.py:28
  11.0 1.3 %collective-permute-start.14 = (f32[128,128]{1,0:T(8,128)S(1)}, f32[128,128]{1,0:T(8,128)S(1)}, u32[]{:S(2)}, u32[]{:S(2)}) collective-permute-start(f32[128,128]{1,0:T(8,128)S(1)} %add_select_fusion), channel_id=1, source_target_pairs={{0,6},{1,7},{16,22},{17,23},{32,38},{33,39},{48,54},{49,55},{64,70... | collective-permute-start | bytes 196616 | tf_op jit(solution)/shard_map/ppermute | solution.py:28
  12.3 2.5 %slice.21 = f32[8,128,1,128]{3,2,1,0:T(1,128)S(1)} slice(f32[8,128,8,128]{3,2,1,0:T(8,128)} %x_ref.1), slice={[0:8], [0:128], [0:1], [0:128]} | slice | bytes 1048576 | tf_op jit(solution)/shard_map/slice | solution.py:212
  14.9 1.3 %collective-permute-start.1 = (f32[8,128,128]{2,1,0:T(8,128)S(1)}, f32[8,128,128]{2,1,0:T(8,128)S(1)}, u32[]{:S(2)}, u32[]{:S(2)}) collective-permute-start(f32[8,128,128]{2,1,0:T(8,128)S(1)} %select_bitcast_fusion), channel_id=1, source_target_pairs={{0,10},{1,11},{16,26},{17,27},{32,42},{33,43},{48,58},{49,59},{64,... | collective-permute-start | bytes 1572872 | tf_op jit(solution)/shard_map/ppermute | solution.py:28
  16.2 1.3 %collective-permute-start = (f32[8,128,128]{2,1,0:T(8,128)S(1)}, f32[8,128,128]{2,1,0:T(8,128)S(1)}, u32[]{:S(2)}, u32[]{:S(2)}) collective-permute-start(f32[8,128,128]{2,1,0:T(8,128)S(1)} %select_bitcast_fusion), channel_id=1, source_target_pairs={{0,6},{1,7},{16,22},{17,23},{32,38},{33,39},{48,54},{49,55},{64,70... | collective-permute-start | bytes 1572872 | tf_op jit(solution)/shard_map/ppermute | solution.py:28
  17.6 1.3 %collective-permute-start.17 = (f32[128,128]{1,0:T(8,128)S(1)}, f32[128,128]{1,0:T(8,128)S(1)}, u32[]{:S(2)}, u32[]{:S(2)}) collective-permute-start(f32[128,128]{1,0:T(8,128)S(1)} %add_add_fusion.3), channel_id=1, source_target_pairs={{0,14},{1,15},{6,4},{7,5},{16,30},{17,31},{22,20},{23,21},{32,46},... | collective-permute-start | bytes 196616 | tf_op jit(solution)/shard_map/ppermute | solution.py:28
  18.9 1.3 %collective-permute-start.16 = (f32[128,128]{1,0:T(8,128)S(1)}, f32[128,128]{1,0:T(8,128)S(1)}, u32[]{:S(2)}, u32[]{:S(2)}) collective-permute-start(f32[128,128]{1,0:T(8,128)S(1)} %add_add_fusion.3), channel_id=1, source_target_pairs={{0,2},{1,3},{6,8},{7,9},{10,12},{11,13},{16,18},{17,19},{22,24},{2... | collective-permute-start | bytes 196616 | tf_op jit(solution)/shard_map/ppermute | solution.py:28
  21.3 2.8 %collective-permute-start.7 = (f32[32,8,128]{2,1,0:T(8,128)S(1)}, f32[32,8,128]{2,1,0:T(8,128)S(1)}, u32[]{:S(2)}, u32[]{:S(2)}) collective-permute-start(f32[32,8,128]{2,1,0:T(8,128)S(1)} %get-tuple-element.5), channel_id=1, source_target_pairs={{0,192},{1,193},{2,194},{3,195},{4,196},{5,197},{6,198},{7,199},{8... | collective-permute-start | bytes 393224 | tf_op jit(solution)/shard_map/ppermute | solution.py:28
  24.1 4.1 %collective-permute-done.17 = f32[128,128]{1,0:T(8,128)S(1)} collective-permute-done((f32[128,128]{1,0:T(8,128)S(1)}, f32[128,128]{1,0:T(8,128)S(1)}, u32[]{:S(2)}, u32[]{:S(2)}) %collective-permute-start.17) | collective-permute-done | bytes 65568 | tf_op jit(solution)/shard_map/ppermute | solution.py:28
  28.1 2.9 %collective-permute-start.6 = (f32[32,8,128]{2,1,0:T(8,128)S(1)}, f32[32,8,128]{2,1,0:T(8,128)S(1)}, u32[]{:S(2)}, u32[]{:S(2)}) collective-permute-start(f32[32,8,128]{2,1,0:T(8,128)S(1)} %get-tuple-element.6), channel_id=1, source_target_pairs={{0,128},{1,129},{2,130},{3,131},{4,132},{5,133},{6,134},{7,135},{8... | collective-permute-start | bytes 393224 | tf_op jit(solution)/shard_map/ppermute | solution.py:28
  31.5 2.4 %collective-permute-start.20 = (f32[128,128]{1,0:T(8,128)S(1)}, f32[128,128]{1,0:T(8,128)S(1)}, u32[]{:S(2)}, u32[]{:S(2)}) collective-permute-start(f32[128,128]{1,0:T(8,128)S(1)} %add_add_fusion.2), channel_id=1, source_target_pairs={{0,192},{1,193},{2,194},{3,195},{4,196},{5,197},{6,198},{7,199},{8... | collective-permute-start | bytes 196616 | tf_op jit(solution)/shard_map/ppermute | solution.py:28
  34.7 5.0 %collective-permute-start.3 = (f32[8,128,128]{2,1,0:T(8,128)S(1)}, f32[8,128,128]{2,1,0:T(8,128)S(1)}, u32[]{:S(2)}, u32[]{:S(2)}) collective-permute-start(f32[8,128,128]{2,1,0:T(8,128)S(1)} %add_add_fusion.1), channel_id=1, source_target_pairs={{0,14},{1,15},{6,4},{7,5},{16,30},{17,31},{22,20},{23,21},{32,46},... | collective-permute-start | bytes 1572872 | tf_op jit(solution)/shard_map/ppermute | solution.py:28
  39.8 1.3 %collective-permute-start.2 = (f32[8,128,128]{2,1,0:T(8,128)S(1)}, f32[8,128,128]{2,1,0:T(8,128)S(1)}, u32[]{:S(2)}, u32[]{:S(2)}) collective-permute-start(f32[8,128,128]{2,1,0:T(8,128)S(1)} %add_add_fusion.1), channel_id=1, source_target_pairs={{0,2},{1,3},{6,8},{7,9},{10,12},{11,13},{16,18},{17,19},{22,24},{2... | collective-permute-start | bytes 1572872 | tf_op jit(solution)/shard_map/ppermute | solution.py:28
  42.0 2.6 %collective-permute-start.10 = (f32[32,8,128]{2,1,0:T(8,128)S(1)}, f32[32,8,128]{2,1,0:T(8,128)S(1)}, u32[]{:S(2)}, u32[]{:S(2)}) collective-permute-start(f32[32,8,128]{2,1,0:T(8,128)S(1)} %bitcast_select_fusion), channel_id=1, source_target_pairs={{0,48},{1,49},{2,50},{3,51},{4,52},{5,53},{6,54},{7,55},{8,56},{9,... | collective-permute-start | bytes 393224 | tf_op jit(solution)/shard_map/ppermute | solution.py:28
  45.8 2.2 %collective-permute-done.10 = f32[32,8,128]{2,1,0:T(8,128)S(1)} collective-permute-done((f32[32,8,128]{2,1,0:T(8,128)S(1)}, f32[32,8,128]{2,1,0:T(8,128)S(1)}, u32[]{:S(2)}, u32[]{:S(2)}) %collective-permute-start.10) | collective-permute-done | bytes 131104 | tf_op jit(solution)/shard_map/ppermute | solution.py:28
  47.9 3.1 %collective-permute-start.23 = (f32[128,128]{1,0:T(8,128)S(1)}, f32[128,128]{1,0:T(8,128)S(1)}, u32[]{:S(2)}, u32[]{:S(2)}) collective-permute-start(f32[128,128]{1,0:T(8,128)S(1)} %select_select_fusion), channel_id=1, source_target_pairs={{0,48},{1,49},{2,50},{3,51},{4,52},{5,53},{6,54},{7,55},{8,56},{9,... | collective-permute-start | bytes 196616 | tf_op jit(solution)/shard_map/ppermute | solution.py:28
  51.8 5.5 %collective-permute-start.4 = (f32[8,128,128]{2,1,0:T(8,128)S(1)}, f32[8,128,128]{2,1,0:T(8,128)S(1)}, u32[]{:S(2)}, u32[]{:S(2)}) collective-permute-start(f32[8,128,128]{2,1,0:T(8,128)S(1)} %add_add_fusion.held_ref), channel_id=1, source_target_pairs={{0,1},{1,0},{2,3},{3,2},{4,5},{5,4},{6,7},{7,6},{8,9},{9,8},{10,11... | collective-permute-start | bytes 1572872 | tf_op jit(solution)/shard_map/ppermute | solution.py:28
  57.3 2.7 %collective-permute-start.13 = (f32[2,32,8,128]{3,2,1,0:T(8,128)S(1)}, f32[2,32,8,128]{3,2,1,0:T(8,128)S(1)}, u32[]{:S(2)}, u32[]{:S(2)}) collective-permute-start(f32[2,32,8,128]{3,2,1,0:T(8,128)S(1)} %pad_maximum_fusion.h0_ref), channel_id=1, source_target_pairs={{0,192},{1,193},{2,194},{3,195},{4,196},{5,197},{6,198},{7,199},{8... | collective-permute-start | bytes 786440 | tf_op jit(solution)/shard_map/ppermute | solution.py:28
  60.0 1.7 %collective-permute-start.12 = (f32[2,32,8,128]{3,2,1,0:T(8,128)S(1)}, f32[2,32,8,128]{3,2,1,0:T(8,128)S(1)}, u32[]{:S(2)}, u32[]{:S(2)}) collective-permute-start(f32[2,32,8,128]{3,2,1,0:T(8,128)S(1)} %pad_maximum_fusion.h0_ref), channel_id=1, source_target_pairs={{0,128},{1,129},{2,130},{3,131},{4,132},{5,133},{6,134},{7,135},{8... | collective-permute-start | bytes 786440 | tf_op jit(solution)/shard_map/ppermute | solution.py:28
  61.9 3.0 %collective-permute-start.24 = (f32[2,128,128]{2,1,0:T(8,128)S(1)}, f32[2,128,128]{2,1,0:T(8,128)S(1)}, u32[]{:S(2)}, u32[]{:S(2)}) collective-permute-start(f32[2,128,128]{2,1,0:T(8,128)S(1)} %pad_maximum_fusion.1.held_ref), channel_id=1, source_target_pairs={{0,1},{1,0},{2,3},{3,2},{4,5},{5,4},{6,7},{7,6},{8,9},{9,8},{10,11... | collective-permute-start | bytes 393224 | tf_op jit(solution)/shard_map/ppermute | solution.py:28
  66.6 11.7 %shard_map.28.w_ref = f32[256,256]{1,0:T(8,128)} custom-call(s32[1]{0:T(128)S(6)} %and.23.core_ref, f32[2,128,128]{2,1,0:T(8,128)} %copy-done.2, f32[2,128,128]{2,1,0:T(8,128)} %copy-done.3), custom_call_target="tpu_custom_call" | custom-call | flops 33554432 | bytes 500000 | tf_op jit(solution)/shard_map/pallas_call | solution.py:94
  78.2 2.2 %copy-done = f32[8,128,8,128]{3,2,1,0:T(8,128)S(1)} copy-done((f32[8,128,8,128]{3,2,1,0:T(8,128)S(1)}, f32[8,128,8,128]{3,2,1,0:T(8,128)}, u32[]{:S(2)}) %copy-start) | copy-done | bytes 4194328
  81.4 5.5 %shard_map.29 = f32[8,128,8,128]{3,2,1,0:T(8,128)} custom-call(s32[2]{0:T(128)S(1)} %pad_add_fusion.place_ref, f32[8,128,8,128]{3,2,1,0:T(8,128)S(1)} %copy-done, f32[8,128,128]{2,1,0:T(8,128)S(1)} %add_add_fusion.held_ref, f32[8,128,128]{2,1,0:T(8,128)S(1)} %collective-permute-done.4.other_ref, f32[2,32,8,128]{3,2,1,0:T(8,128)S(1)} %pad_maximum_fusion.h0_ref, ...), custom_call_target="tpu_custom_call" | custom-call | flops 1610612736 | bytes 8388608 | tf_op jit(solution)/shard_map/pallas_call | solution.py:150
  (53 shorter events, 8.7 us)
Async XLA Ops:
  1.8 15.7 %collective-permute-start.15 = (f32[128,128]{1,0:T(8,128)S(1)}, f32[128,128]{1,0:T(8,128)S(1)}, u32[]{:S(2)}, u32[]{:S(2)}) collective-permute-start(f32[128,128]{1,0:T(8,128)S(1)} %add_select_fusion), channel_id=1, source_target_pairs={{0,10},{1,11},{16,26},{17,27},{32,42},{33,43},{48,58},{49,59},{64,... | collective-permute-start | bytes 196616 | tf_op jit(solution)/shard_map/ppermute | solution.py:28
  11.0 6.5 %collective-permute-start.14 = (f32[128,128]{1,0:T(8,128)S(1)}, f32[128,128]{1,0:T(8,128)S(1)}, u32[]{:S(2)}, u32[]{:S(2)}) collective-permute-start(f32[128,128]{1,0:T(8,128)S(1)} %add_select_fusion), channel_id=1, source_target_pairs={{0,6},{1,7},{16,22},{17,23},{32,38},{33,39},{48,54},{49,55},{64,70... | collective-permute-start | bytes 196616 | tf_op jit(solution)/shard_map/ppermute | solution.py:28
  14.9 16.6 %collective-permute-start.1 = (f32[8,128,128]{2,1,0:T(8,128)S(1)}, f32[8,128,128]{2,1,0:T(8,128)S(1)}, u32[]{:S(2)}, u32[]{:S(2)}) collective-permute-start(f32[8,128,128]{2,1,0:T(8,128)S(1)} %select_bitcast_fusion), channel_id=1, source_target_pairs={{0,10},{1,11},{16,26},{17,27},{32,42},{33,43},{48,58},{49,59},{64,... | collective-permute-start | bytes 1572872 | tf_op jit(solution)/shard_map/ppermute | solution.py:28
  16.2 17.6 %collective-permute-start = (f32[8,128,128]{2,1,0:T(8,128)S(1)}, f32[8,128,128]{2,1,0:T(8,128)S(1)}, u32[]{:S(2)}, u32[]{:S(2)}) collective-permute-start(f32[8,128,128]{2,1,0:T(8,128)S(1)} %select_bitcast_fusion), channel_id=1, source_target_pairs={{0,6},{1,7},{16,22},{17,23},{32,38},{33,39},{48,54},{49,55},{64,70... | collective-permute-start | bytes 1572872 | tf_op jit(solution)/shard_map/ppermute | solution.py:28
  17.6 10.6 %collective-permute-start.17 = (f32[128,128]{1,0:T(8,128)S(1)}, f32[128,128]{1,0:T(8,128)S(1)}, u32[]{:S(2)}, u32[]{:S(2)}) collective-permute-start(f32[128,128]{1,0:T(8,128)S(1)} %add_add_fusion.3), channel_id=1, source_target_pairs={{0,14},{1,15},{6,4},{7,5},{16,30},{17,31},{22,20},{23,21},{32,46},... | collective-permute-start | bytes 196616 | tf_op jit(solution)/shard_map/ppermute | solution.py:28
  18.9 12.2 %collective-permute-start.16 = (f32[128,128]{1,0:T(8,128)S(1)}, f32[128,128]{1,0:T(8,128)S(1)}, u32[]{:S(2)}, u32[]{:S(2)}) collective-permute-start(f32[128,128]{1,0:T(8,128)S(1)} %add_add_fusion.3), channel_id=1, source_target_pairs={{0,2},{1,3},{6,8},{7,9},{10,12},{11,13},{16,18},{17,19},{22,24},{2... | collective-permute-start | bytes 196616 | tf_op jit(solution)/shard_map/ppermute | solution.py:28
  21.3 12.8 %collective-permute-start.7 = (f32[32,8,128]{2,1,0:T(8,128)S(1)}, f32[32,8,128]{2,1,0:T(8,128)S(1)}, u32[]{:S(2)}, u32[]{:S(2)}) collective-permute-start(f32[32,8,128]{2,1,0:T(8,128)S(1)} %get-tuple-element.5), channel_id=1, source_target_pairs={{0,192},{1,193},{2,194},{3,195},{4,196},{5,197},{6,198},{7,199},{8... | collective-permute-start | bytes 393224 | tf_op jit(solution)/shard_map/ppermute | solution.py:28
  28.1 6.6 %collective-permute-start.6 = (f32[32,8,128]{2,1,0:T(8,128)S(1)}, f32[32,8,128]{2,1,0:T(8,128)S(1)}, u32[]{:S(2)}, u32[]{:S(2)}) collective-permute-start(f32[32,8,128]{2,1,0:T(8,128)S(1)} %get-tuple-element.6), channel_id=1, source_target_pairs={{0,128},{1,129},{2,130},{3,131},{4,132},{5,133},{6,134},{7,135},{8... | collective-permute-start | bytes 393224 | tf_op jit(solution)/shard_map/ppermute | solution.py:28
  31.1 8.7 %collective-permute-start.5 = (f32[32,8,128]{2,1,0:T(8,128)S(1)}, f32[32,8,128]{2,1,0:T(8,128)S(1)}, u32[]{:S(2)}, u32[]{:S(2)}) collective-permute-start(f32[32,8,128]{2,1,0:T(8,128)S(1)} %get-tuple-element.7), channel_id=1, source_target_pairs={{0,64},{1,65},{2,66},{3,67},{4,68},{5,69},{6,70},{7,71},{8,72},{9,... | collective-permute-start | bytes 393224 | tf_op jit(solution)/shard_map/ppermute | solution.py:28
  31.5 10.5 %collective-permute-start.20 = (f32[128,128]{1,0:T(8,128)S(1)}, f32[128,128]{1,0:T(8,128)S(1)}, u32[]{:S(2)}, u32[]{:S(2)}) collective-permute-start(f32[128,128]{1,0:T(8,128)S(1)} %add_add_fusion.2), channel_id=1, source_target_pairs={{0,192},{1,193},{2,194},{3,195},{4,196},{5,197},{6,198},{7,199},{8... | collective-permute-start | bytes 196616 | tf_op jit(solution)/shard_map/ppermute | solution.py:28
  33.8 10.8 %collective-permute-start.19 = (f32[128,128]{1,0:T(8,128)S(1)}, f32[128,128]{1,0:T(8,128)S(1)}, u32[]{:S(2)}, u32[]{:S(2)}) collective-permute-start(f32[128,128]{1,0:T(8,128)S(1)} %add_add_fusion.2), channel_id=1, source_target_pairs={{0,128},{1,129},{2,130},{3,131},{4,132},{5,133},{6,134},{7,135},{8... | collective-permute-start | bytes 196616 | tf_op jit(solution)/shard_map/ppermute | solution.py:28
  34.1 11.1 %collective-permute-start.18 = (f32[128,128]{1,0:T(8,128)S(1)}, f32[128,128]{1,0:T(8,128)S(1)}, u32[]{:S(2)}, u32[]{:S(2)}) collective-permute-start(f32[128,128]{1,0:T(8,128)S(1)} %add_add_fusion.2), channel_id=1, source_target_pairs={{0,64},{1,65},{2,66},{3,67},{4,68},{5,69},{6,70},{7,71},{8,72},{9,... | collective-permute-start | bytes 196616 | tf_op jit(solution)/shard_map/ppermute | solution.py:28
  34.7 17.0 %collective-permute-start.3 = (f32[8,128,128]{2,1,0:T(8,128)S(1)}, f32[8,128,128]{2,1,0:T(8,128)S(1)}, u32[]{:S(2)}, u32[]{:S(2)}) collective-permute-start(f32[8,128,128]{2,1,0:T(8,128)S(1)} %add_add_fusion.1), channel_id=1, source_target_pairs={{0,14},{1,15},{6,4},{7,5},{16,30},{17,31},{22,20},{23,21},{32,46},... | collective-permute-start | bytes 1572872 | tf_op jit(solution)/shard_map/ppermute | solution.py:28
  39.8 11.9 %collective-permute-start.2 = (f32[8,128,128]{2,1,0:T(8,128)S(1)}, f32[8,128,128]{2,1,0:T(8,128)S(1)}, u32[]{:S(2)}, u32[]{:S(2)}) collective-permute-start(f32[8,128,128]{2,1,0:T(8,128)S(1)} %add_add_fusion.1), channel_id=1, source_target_pairs={{0,2},{1,3},{6,8},{7,9},{10,12},{11,13},{16,18},{17,19},{22,24},{2... | collective-permute-start | bytes 1572872 | tf_op jit(solution)/shard_map/ppermute | solution.py:28
  42.0 5.9 %collective-permute-start.10 = (f32[32,8,128]{2,1,0:T(8,128)S(1)}, f32[32,8,128]{2,1,0:T(8,128)S(1)}, u32[]{:S(2)}, u32[]{:S(2)}) collective-permute-start(f32[32,8,128]{2,1,0:T(8,128)S(1)} %bitcast_select_fusion), channel_id=1, source_target_pairs={{0,48},{1,49},{2,50},{3,51},{4,52},{5,53},{6,54},{7,55},{8,56},{9,... | collective-permute-start | bytes 393224 | tf_op jit(solution)/shard_map/ppermute | solution.py:28
  44.6 6.4 %collective-permute-start.9 = (f32[32,8,128]{2,1,0:T(8,128)S(1)}, f32[32,8,128]{2,1,0:T(8,128)S(1)}, u32[]{:S(2)}, u32[]{:S(2)}) collective-permute-start(f32[32,8,128]{2,1,0:T(8,128)S(1)} %bitcast_select_fusion), channel_id=1, source_target_pairs={{0,32},{1,33},{2,34},{3,35},{4,36},{5,37},{6,38},{7,39},{8,40},{9,... | collective-permute-start | bytes 393224 | tf_op jit(solution)/shard_map/ppermute | solution.py:28
  45.1 6.2 %collective-permute-start.8 = (f32[32,8,128]{2,1,0:T(8,128)S(1)}, f32[32,8,128]{2,1,0:T(8,128)S(1)}, u32[]{:S(2)}, u32[]{:S(2)}) collective-permute-start(f32[32,8,128]{2,1,0:T(8,128)S(1)} %bitcast_select_fusion), channel_id=1, source_target_pairs={{0,16},{1,17},{2,18},{3,19},{4,20},{5,21},{6,22},{7,23},{8,24},{9,... | collective-permute-start | bytes 393224 | tf_op jit(solution)/shard_map/ppermute | solution.py:28
  47.9 12.1 %collective-permute-start.23 = (f32[128,128]{1,0:T(8,128)S(1)}, f32[128,128]{1,0:T(8,128)S(1)}, u32[]{:S(2)}, u32[]{:S(2)}) collective-permute-start(f32[128,128]{1,0:T(8,128)S(1)} %select_select_fusion), channel_id=1, source_target_pairs={{0,48},{1,49},{2,50},{3,51},{4,52},{5,53},{6,54},{7,55},{8,56},{9,... | collective-permute-start | bytes 196616 | tf_op jit(solution)/shard_map/ppermute | solution.py:28
  51.0 10.7 %collective-permute-start.22 = (f32[128,128]{1,0:T(8,128)S(1)}, f32[128,128]{1,0:T(8,128)S(1)}, u32[]{:S(2)}, u32[]{:S(2)}) collective-permute-start(f32[128,128]{1,0:T(8,128)S(1)} %select_select_fusion), channel_id=1, source_target_pairs={{0,32},{1,33},{2,34},{3,35},{4,36},{5,37},{6,38},{7,39},{8,40},{9,... | collective-permute-start | bytes 196616 | tf_op jit(solution)/shard_map/ppermute | solution.py:28
  51.3 10.5 %collective-permute-start.21 = (f32[128,128]{1,0:T(8,128)S(1)}, f32[128,128]{1,0:T(8,128)S(1)}, u32[]{:S(2)}, u32[]{:S(2)}) collective-permute-start(f32[128,128]{1,0:T(8,128)S(1)} %select_select_fusion), channel_id=1, source_target_pairs={{0,16},{1,17},{2,18},{3,19},{4,20},{5,21},{6,22},{7,23},{8,24},{9,... | collective-permute-start | bytes 196616 | tf_op jit(solution)/shard_map/ppermute | solution.py:28
  51.8 26.5 %collective-permute-start.4 = (f32[8,128,128]{2,1,0:T(8,128)S(1)}, f32[8,128,128]{2,1,0:T(8,128)S(1)}, u32[]{:S(2)}, u32[]{:S(2)}) collective-permute-start(f32[8,128,128]{2,1,0:T(8,128)S(1)} %add_add_fusion.held_ref), channel_id=1, source_target_pairs={{0,1},{1,0},{2,3},{3,2},{4,5},{5,4},{6,7},{7,6},{8,9},{9,8},{10,11... | collective-permute-start | bytes 1572872 | tf_op jit(solution)/shard_map/ppermute | solution.py:28
  57.3 21.0 %collective-permute-start.13 = (f32[2,32,8,128]{3,2,1,0:T(8,128)S(1)}, f32[2,32,8,128]{3,2,1,0:T(8,128)S(1)}, u32[]{:S(2)}, u32[]{:S(2)}) collective-permute-start(f32[2,32,8,128]{3,2,1,0:T(8,128)S(1)} %pad_maximum_fusion.h0_ref), channel_id=1, source_target_pairs={{0,192},{1,193},{2,194},{3,195},{4,196},{5,197},{6,198},{7,199},{8... | collective-permute-start | bytes 786440 | tf_op jit(solution)/shard_map/ppermute | solution.py:28
  60.0 18.2 %collective-permute-start.12 = (f32[2,32,8,128]{3,2,1,0:T(8,128)S(1)}, f32[2,32,8,128]{3,2,1,0:T(8,128)S(1)}, u32[]{:S(2)}, u32[]{:S(2)}) collective-permute-start(f32[2,32,8,128]{3,2,1,0:T(8,128)S(1)} %pad_maximum_fusion.h0_ref), channel_id=1, source_target_pairs={{0,128},{1,129},{2,130},{3,131},{4,132},{5,133},{6,134},{7,135},{8... | collective-permute-start | bytes 786440 | tf_op jit(solution)/shard_map/ppermute | solution.py:28
  61.7 16.5 %collective-permute-start.11 = (f32[2,32,8,128]{3,2,1,0:T(8,128)S(1)}, f32[2,32,8,128]{3,2,1,0:T(8,128)S(1)}, u32[]{:S(2)}, u32[]{:S(2)}) collective-permute-start(f32[2,32,8,128]{3,2,1,0:T(8,128)S(1)} %pad_maximum_fusion.h0_ref), channel_id=1, source_target_pairs={{0,64},{1,65},{2,66},{3,67},{4,68},{5,69},{6,70},{7,71},{8,72},{9,... | collective-permute-start | bytes 786440 | tf_op jit(solution)/shard_map/ppermute | solution.py:28
  (5 other events, 11.9 us)

commit v3 on v2

--- a/solution.py
+++ b/solution.py
@@ -96,7 +96,8 @@
         in_specs=[pl.BlockSpec(memory_space=pltpu.SMEM), vmem, vmem],
         out_specs=vmem,
         out_shape=jax.ShapeDtypeStruct((256, 256), f32),
-        cost_estimate=pl.CostEstimate(flops=2 * 256**3, bytes_accessed=500000, transcendentals=256),
+        compiler_params=pltpu.CompilerParams(vmem_limit_bytes=8 * 1024 * 1024),
+        cost_estimate=pl.CostEstimate(flops=12 * 10**9, bytes_accessed=500000, transcendentals=256),
     )(core, held, other)
 
 
@@ -111,7 +112,7 @@
     return dot(ah, bh) + (dot(ah, bl) + dot(al, bh))
 
 
-def update_kernel(place_ref, x_ref, held_ref, other_ref, h0_ref, h1_ref, h2_ref, h3_ref, w_ref, o_ref, out_ref, col_ref, sem):
+def update_kernel(place_ref, x_ref, held_ref, o0_ref, o1_ref, o2_ref, o3_ref, h0_ref, h1_ref, h2_ref, h3_ref, w_ref, o_ref, out_ref, col_ref, sem):
     w = halves(w_ref[...])
     y_place = place_ref[0] // 4
     for n, h in enumerate((h0_ref, h1_ref, h2_ref, h3_ref)):
@@ -122,10 +123,11 @@
         [jnp.concatenate([col_ref[p, :, c, :] for c in range(8)], axis=1) for p in range(2)], axis=0
     )
     first = lax.rem(place_ref[1], 2) == 0
+    other = [ref[n] for ref in (o0_ref, o1_ref, o2_ref, o3_ref) for n in range(2)]
     z = halves(product(w, halves(cols)))
     y = [
         halves(product(halves(jnp.concatenate(
-            [jnp.where(first, held_ref[a], other_ref[a]), jnp.where(first, other_ref[a], held_ref[a])], axis=1
+            [jnp.where(first, held_ref[a], other[a]), jnp.where(first, other[a], held_ref[a])], axis=1
         )), w, NT))
         for a in range(8)
     ]
@@ -149,11 +151,11 @@
     vmem = pl.BlockSpec(memory_space=pltpu.VMEM)
     return pl.pallas_call(
         update_kernel,
-        in_specs=[pl.BlockSpec(memory_space=pltpu.SMEM)] + [vmem] * 8,
+        in_specs=[pl.BlockSpec(memory_space=pltpu.SMEM)] + [vmem] * 11,
         out_specs=pl.BlockSpec(memory_space=pl.ANY),
         scratch_shapes=[pltpu.VMEM((8, 128, 8, 128), f32), pltpu.VMEM((2, 128, 8, 128), f32), pltpu.SemaphoreType.DMA((8,))],
         out_shape=jax.ShapeDtypeStruct((8, 128, 8, 128), f32),
-        compiler_params=pltpu.CompilerParams(vmem_limit_bytes=40 * 1024 * 1024),
+        compiler_params=pltpu.CompilerParams(vmem_limit_bytes=24 * 1024 * 1024),
         cost_estimate=pl.CostEstimate(flops=6 * 1024**2 * 256, bytes_accessed=8 * 1024**2, transcendentals=0),
     )(place, x, *rows, *cols, w)
 
@@ -182,54 +184,61 @@
     return jnp.stack([pick(x, ways), pick((x + 3) & 3, ways)])
 
 
-def along_z(held):
+def after(value, *others):
+    return lax.optimization_barrier((value, *others))[0]
+
+
+def first_z(held):
     near = send(held, lambda x, y, z, k: (x, y, 3, k) if z == 0 else None)
     far = send(held, lambda x, y, z, k: (x, y, 5, k) if z == 0 else None)
-    held = held + near + far
+    return held, near, far
+
+
+def second_z(held):
     up = {0: 1, 3: 4, 5: 6}
     down = {0: 7, 3: 2}
     near = send(held, lambda x, y, z, k: (x, y, up[z], k) if z in up else None)
     far = send(held, lambda x, y, z, k: (x, y, down[z], k) if z in down else None)
-    return held + near + far
+    return held, near, far
+
+
+def total(parts):
+    return parts[0] + parts[1] + parts[2]
 
 
 def swap(held):
     return send(held, lambda x, y, z, k: (x, y, z, 1 - k))
 
 
-def spread_pivots(coupling, diagonal, x, y, z, core):
+def pivot_block(coupling, diagonal, x, core):
     own = coupling[0, :, 0, :]
     r = lax.broadcasted_iota(jnp.int32, (128, 128), 0)
     c = lax.broadcasted_iota(jnp.int32, (128, 128), 1)
-    own = own + jnp.where((r == c) & (x == core), diagonal[0][None, :], 0.0)
-    own = along_z(jnp.where(z == 0, own, 0.0))
-    own = pick(y, [own, *turns([own] * 3, along_y)])
-    held = columns_zero_and_one(own, turns([own] * 3, along_x), x)
-    return held, swap(held)
-
-
-def spread_rows(coupling, x, y, z, core):
-    held = along_z(jnp.where(z == 0, coupling[:, :, 0, :], 0.0))
-    return held, swap(held)
-
-
-def spread_cols(coupling, x, y, z, core):
-    quarters = [coupling[0, 32 * n:32 * n + 32] for n in range(4)]
-    own = pick(y, [quarters[0], *turns(quarters[1:], along_y)])
-    both = columns_zero_and_one(own, turns([own] * 3, along_x), x)
-    return [both, *turns([both] * 3, along_y)]
+    return own + jnp.where((r == c) & (x == core), diagonal[0][None, :], 0.0)
 
 
 def on_device(coupling, diagonal):
     row = lax.axis_index("prow")
     col = lax.axis_index("pcol")
-    here = place_of(row, col)
-    pivots = spread_pivots(coupling, diagonal, *here)
-    rows = spread_rows(coupling, *here)
-    cols = spread_cols(coupling, *here)
+    x, y, z, core = place_of(row, col)
     place = jnp.stack([row, col]).astype(jnp.int32)
-    w = factor(place[1:] & 1, *pivots)
-    return update(place, coupling, rows, cols, w)
+
+    pivot = jnp.where(z == 0, pivot_block(coupling, diagonal, x, core), 0.0)
+    rows = jnp.where(z == 0, coupling[:, :, 0, :], 0.0)
+    pivot = total(first_z(pivot))
+    rows = first_z(after(rows, pivot))
+    pivot = total(second_z(pivot))
+    quarters = [coupling[0, 32 * n:32 * n + 32] for n in range(4)]
+    cols = pick(y, [quarters[0], *turns(quarters[1:], along_y)])
+    pivot = pick(y, [pivot, *turns([pivot] * 3, along_y)])
+    cols = columns_zero_and_one(cols, turns([cols] * 3, along_x), x)
+    pivots = columns_zero_and_one(pivot, turns([pivot] * 3, along_x), x)
+    other_pivots = swap(pivots)
+    rows = second_z(total(rows))
+    cols = [cols, *turns([cols] * 3, along_y)]
+    w = factor(place[1:] & 1, pivots, other_pivots)
+    rows = total((after(rows[0], w), *rows[1:]))
+    return update(place, coupling, (rows, *[swap(rows[2 * n:2 * n + 2]) for n in range(4)]), cols, w)
 
 
 def solution(mesh):

time: 87.5 us -> 79.8 us (0.912)
  waiting for transfers between devices: 7.5 us -> 2.61 us
  local copies, waits for them, and re-layouts: 9.09 us -> 5.36 us
  starting transfers between devices: 51.5 us -> 54.1 us
  Pallas kernels: 17.2 us -> 15.5 us
    ppermute x25 -> x28, waiting for transfers between devices: 7.5 us -> 2.61 us  [send(): return lax.ppermute(value, AXES, pairs)]
    unnamed x8 -> x2, local copies, waits for them, and re-layouts: 3.77 us -> 0.01 us
    ppermute x25 -> x28, starting transfers between devices: 51.5 us -> 54.1 us  [send(): return lax.ppermute(value, AXES, pairs)]
    pallas_call x1, Pallas kernels: 11.7 us -> 9.98 us  [factor(): pl.pallas_call(factor_kernel, in_specs=[pl.BlockSpec(memory_space=pltpu.S...]
    slice x2 -> x3, local copies, waits for them, and re-layouts: 3.57 us -> 3.6 us  [the longest x1 2.49 us: on_device(): rows = jnp.where(z == 0, coupling[:, :, 0, :], 0.0)]
  transfers between devices with their start and end apart: 25 -> 28, of which waited for: 4 -> 6; matrix products, arithmetic and copies ran while one was open for 6% -> 6% of each run, Pallas kernels for 13% -> 13%
where the time goes in v3:
time: 79.8 us; the launch traced here: 79.4 us
  starting transfers between devices  54.1 us (68%)
  Pallas kernels  15.5 us (19%)
  local copies, waits for them, and re-layouts  5.36 us (7%)
  waiting for transfers between devices  2.61 us (3%)
  other arithmetic  1.37 us (2%)
    ppermute x28, starting transfers between devices, send(): return lax.ppermute(value, AXES, pairs)  54.1 us
    pallas_call x1, Pallas kernels, factor(): pl.pallas_call(factor_kernel, in_specs=[pl.BlockSpec(memory_space=pltpu.S...  9.98 us
    pallas_call x1, Pallas kernels, update(): pl.pallas_call(update_kernel, in_specs=[pl.BlockSpec(memory_space=pltpu.S...  5.56 us
    ppermute x28, waiting for transfers between devices, send(): return lax.ppermute(value, AXES, pairs)  2.61 us
    slice x1, local copies, waits for them, and re-layouts, on_device(): rows = jnp.where(z == 0, coupling[:, :, 0, :], 0.0)  2.49 us
  transfers between devices with their start and end apart: 28, of which 6 were waited for; matrix products, arithmetic and copies ran while one was open for 6% of the time, Pallas kernels for 13%

profile of v3, /device:TPU:1, one launch (start us, length us, event | category | flops | bytes accessed | tf_op | source)
XLA Modules:
  0.0 79.4 jit_solution(5590051985239388260)
XLA Ops:
  1.8 9.2 %collective-permute-start.1 = (f32[128,128]{1,0:T(8,128)S(1)}, f32[128,128]{1,0:T(8,128)S(1)}, u32[]{:S(2)}, u32[]{:S(2)}) collective-permute-start(f32[128,128]{1,0:T(8,128)S(1)} %add_select_fusion), channel_id=1, source_target_pairs={{0,10},{1,11},{16,26},{17,27},{32,42},{33,43},{48,58},{49,59},{64,... | collective-permute-start | bytes 196616 | tf_op jit(solution)/shard_map/ppermute | solution.py:28
  11.0 1.3 %collective-permute-start = (f32[128,128]{1,0:T(8,128)S(1)}, f32[128,128]{1,0:T(8,128)S(1)}, u32[]{:S(2)}, u32[]{:S(2)}) collective-permute-start(f32[128,128]{1,0:T(8,128)S(1)} %add_select_fusion), channel_id=1, source_target_pairs={{0,6},{1,7},{16,22},{17,23},{32,38},{33,39},{48,54},{49,55},{64,70... | collective-permute-start | bytes 196616 | tf_op jit(solution)/shard_map/ppermute | solution.py:28
  13.4 2.8 %collective-permute-start.21 = (f32[32,8,128]{2,1,0:T(8,128)S(1)}, f32[32,8,128]{2,1,0:T(8,128)S(1)}, u32[]{:S(2)}, u32[]{:S(2)}) collective-permute-start(f32[32,8,128]{2,1,0:T(8,128)S(1)} %get-tuple-element.9), channel_id=1, source_target_pairs={{0,192},{1,193},{2,194},{3,195},{4,196},{5,197},{6,198},{7,199},{8... | collective-permute-start | bytes 393224 | tf_op jit(solution)/shard_map/ppermute | solution.py:28
  17.2 2.5 %slice.33 = f32[8,128,1,128]{3,2,1,0:T(1,128)S(1)} slice(f32[8,128,8,128]{3,2,1,0:T(8,128)} %x_ref.1), slice={[0:8], [0:128], [0:1], [0:128]} | slice | bytes 1048576 | tf_op jit(solution)/shard_map/slice | solution.py:227
  19.8 1.3 %collective-permute-start.5 = (f32[128,128]{1,0:T(8,128)S(1)}, f32[128,128]{1,0:T(8,128)S(1)}, u32[]{:S(2)}, u32[]{:S(2)}) collective-permute-start(f32[128,128]{1,0:T(8,128)S(1)} %add_add_fusion.3), channel_id=1, source_target_pairs={{0,14},{1,15},{6,4},{7,5},{16,30},{17,31},{22,20},{23,21},{32,46},... | collective-permute-start | bytes 196616 | tf_op jit(solution)/shard_map/ppermute | solution.py:28
  21.1 1.3 %collective-permute-start.4 = (f32[128,128]{1,0:T(8,128)S(1)}, f32[128,128]{1,0:T(8,128)S(1)}, u32[]{:S(2)}, u32[]{:S(2)}) collective-permute-start(f32[128,128]{1,0:T(8,128)S(1)} %add_add_fusion.3), channel_id=1, source_target_pairs={{0,2},{1,3},{6,8},{7,9},{10,12},{11,13},{16,18},{17,19},{22,24},{2... | collective-permute-start | bytes 196616 | tf_op jit(solution)/shard_map/ppermute | solution.py:28
  22.5 1.3 %collective-permute-start.3 = (f32[8,128,128]{2,1,0:T(8,128)S(1)}, f32[8,128,128]{2,1,0:T(8,128)S(1)}, u32[]{:S(2)}, u32[]{:S(2)}) collective-permute-start(f32[8,128,128]{2,1,0:T(8,128)S(1)} %select_bitcast_fusion), channel_id=1, source_target_pairs={{0,10},{1,11},{16,26},{17,27},{32,42},{33,43},{48,58},{49,59},{64,... | collective-permute-start | bytes 1572872 | tf_op jit(solution)/shard_map/ppermute | solution.py:28
  23.8 1.3 %collective-permute-start.2 = (f32[8,128,128]{2,1,0:T(8,128)S(1)}, f32[8,128,128]{2,1,0:T(8,128)S(1)}, u32[]{:S(2)}, u32[]{:S(2)}) collective-permute-start(f32[8,128,128]{2,1,0:T(8,128)S(1)} %select_bitcast_fusion), channel_id=1, source_target_pairs={{0,6},{1,7},{16,22},{17,23},{32,38},{33,39},{48,54},{49,55},{64,70... | collective-permute-start | bytes 1572872 | tf_op jit(solution)/shard_map/ppermute | solution.py:28
  25.2 2.1 %collective-permute-start.8 = (f32[128,128]{1,0:T(8,128)S(1)}, f32[128,128]{1,0:T(8,128)S(1)}, u32[]{:S(2)}, u32[]{:S(2)}) collective-permute-start(f32[128,128]{1,0:T(8,128)S(1)} %add_add_fusion.2), channel_id=1, source_target_pairs={{0,192},{1,193},{2,194},{3,195},{4,196},{5,197},{6,198},{7,199},{8... | collective-permute-start | bytes 196616 | tf_op jit(solution)/shard_map/ppermute | solution.py:28
  27.2 1.4 %collective-permute-start.7 = (f32[128,128]{1,0:T(8,128)S(1)}, f32[128,128]{1,0:T(8,128)S(1)}, u32[]{:S(2)}, u32[]{:S(2)}) collective-permute-start(f32[128,128]{1,0:T(8,128)S(1)} %add_add_fusion.2), channel_id=1, source_target_pairs={{0,128},{1,129},{2,130},{3,131},{4,132},{5,133},{6,134},{7,135},{8... | collective-permute-start | bytes 196616 | tf_op jit(solution)/shard_map/ppermute | solution.py:28
  29.6 2.6 %collective-permute-start.24 = (f32[32,8,128]{2,1,0:T(8,128)S(1)}, f32[32,8,128]{2,1,0:T(8,128)S(1)}, u32[]{:S(2)}, u32[]{:S(2)}) collective-permute-start(f32[32,8,128]{2,1,0:T(8,128)S(1)} %bitcast_select_fusion), channel_id=1, source_target_pairs={{0,48},{1,49},{2,50},{3,51},{4,52},{5,53},{6,54},{7,55},{8,56},{9,... | collective-permute-start | bytes 393224 | tf_op jit(solution)/shard_map/ppermute | solution.py:28
  32.2 2.4 %collective-permute-start.23 = (f32[32,8,128]{2,1,0:T(8,128)S(1)}, f32[32,8,128]{2,1,0:T(8,128)S(1)}, u32[]{:S(2)}, u32[]{:S(2)}) collective-permute-start(f32[32,8,128]{2,1,0:T(8,128)S(1)} %bitcast_select_fusion), channel_id=1, source_target_pairs={{0,32},{1,33},{2,34},{3,35},{4,36},{5,37},{6,38},{7,39},{8,40},{9,... | collective-permute-start | bytes 393224 | tf_op jit(solution)/shard_map/ppermute | solution.py:28
  35.0 2.5 %collective-permute-start.11 = (f32[128,128]{1,0:T(8,128)S(1)}, f32[128,128]{1,0:T(8,128)S(1)}, u32[]{:S(2)}, u32[]{:S(2)}) collective-permute-start(f32[128,128]{1,0:T(8,128)S(1)} %select_select_fusion), channel_id=1, source_target_pairs={{0,48},{1,49},{2,50},{3,51},{4,52},{5,53},{6,54},{7,55},{8,56},{9,... | collective-permute-start | bytes 196616 | tf_op jit(solution)/shard_map/ppermute | solution.py:28
  37.5 2.5 %collective-permute-start.10 = (f32[128,128]{1,0:T(8,128)S(1)}, f32[128,128]{1,0:T(8,128)S(1)}, u32[]{:S(2)}, u32[]{:S(2)}) collective-permute-start(f32[128,128]{1,0:T(8,128)S(1)} %select_select_fusion), channel_id=1, source_target_pairs={{0,32},{1,33},{2,34},{3,35},{4,36},{5,37},{6,38},{7,39},{8,40},{9,... | collective-permute-start | bytes 196616 | tf_op jit(solution)/shard_map/ppermute | solution.py:28
  40.0 1.2 %collective-permute-start.9 = (f32[128,128]{1,0:T(8,128)S(1)}, f32[128,128]{1,0:T(8,128)S(1)}, u32[]{:S(2)}, u32[]{:S(2)}) collective-permute-start(f32[128,128]{1,0:T(8,128)S(1)} %select_select_fusion), channel_id=1, source_target_pairs={{0,16},{1,17},{2,18},{3,19},{4,20},{5,21},{6,22},{7,23},{8,24},{9,... | collective-permute-start | bytes 196616 | tf_op jit(solution)/shard_map/ppermute | solution.py:28
  41.4 2.0 %collective-permute-start.27 = (f32[2,32,8,128]{3,2,1,0:T(8,128)S(1)}, f32[2,32,8,128]{3,2,1,0:T(8,128)S(1)}, u32[]{:S(2)}, u32[]{:S(2)}) collective-permute-start(f32[2,32,8,128]{3,2,1,0:T(8,128)S(1)} %pad_maximum_fusion.h0_ref), channel_id=1, source_target_pairs={{0,192},{1,193},{2,194},{3,195},{4,196},{5,197},{6,198},{7,199},{8... | collective-permute-start | bytes 786440 | tf_op jit(solution)/shard_map/ppermute | solution.py:28
  43.4 1.1 %collective-permute-start.26 = (f32[2,32,8,128]{3,2,1,0:T(8,128)S(1)}, f32[2,32,8,128]{3,2,1,0:T(8,128)S(1)}, u32[]{:S(2)}, u32[]{:S(2)}) collective-permute-start(f32[2,32,8,128]{3,2,1,0:T(8,128)S(1)} %pad_maximum_fusion.h0_ref), channel_id=1, source_target_pairs={{0,128},{1,129},{2,130},{3,131},{4,132},{5,133},{6,134},{7,135},{8... | collective-permute-start | bytes 786440 | tf_op jit(solution)/shard_map/ppermute | solution.py:28
  44.8 2.1 %collective-permute-start.25 = (f32[2,32,8,128]{3,2,1,0:T(8,128)S(1)}, f32[2,32,8,128]{3,2,1,0:T(8,128)S(1)}, u32[]{:S(2)}, u32[]{:S(2)}) collective-permute-start(f32[2,32,8,128]{3,2,1,0:T(8,128)S(1)} %pad_maximum_fusion.h0_ref), channel_id=1, source_target_pairs={{0,64},{1,65},{2,66},{3,67},{4,68},{5,69},{6,70},{7,71},{8,72},{9,... | collective-permute-start | bytes 786440 | tf_op jit(solution)/shard_map/ppermute | solution.py:28
  47.0 5.3 %collective-permute-start.12 = (f32[2,128,128]{2,1,0:T(8,128)S(1)}, f32[2,128,128]{2,1,0:T(8,128)S(1)}, u32[]{:S(2)}, u32[]{:S(2)}) collective-permute-start(f32[2,128,128]{2,1,0:T(8,128)S(1)} %pad_maximum_fusion.1.held_ref), channel_id=1, source_target_pairs={{0,1},{1,0},{2,3},{3,2},{4,5},{5,4},{6,7},{7,6},{8,9},{9,8},{10,11... | collective-permute-start | bytes 393224 | tf_op jit(solution)/shard_map/ppermute | solution.py:28
  52.4 5.8 %collective-permute-start.14 = (f32[8,128,128]{2,1,0:T(8,128)S(1)}, f32[8,128,128]{2,1,0:T(8,128)S(1)}, u32[]{:S(2)}, u32[]{:S(2)}) collective-permute-start(f32[8,128,128]{2,1,0:T(8,128)S(1)} %add_add_fusion.1), channel_id=1, source_target_pairs={{0,14},{1,15},{6,4},{7,5},{16,30},{17,31},{22,20},{23,21},{32,46},... | collective-permute-start | bytes 1572872 | tf_op jit(solution)/shard_map/ppermute | solution.py:28
  58.2 1.3 %collective-permute-start.13 = (f32[8,128,128]{2,1,0:T(8,128)S(1)}, f32[8,128,128]{2,1,0:T(8,128)S(1)}, u32[]{:S(2)}, u32[]{:S(2)}) collective-permute-start(f32[8,128,128]{2,1,0:T(8,128)S(1)} %add_add_fusion.1), channel_id=1, source_target_pairs={{0,2},{1,3},{6,8},{7,9},{10,12},{11,13},{16,18},{17,19},{22,24},{2... | collective-permute-start | bytes 1572872 | tf_op jit(solution)/shard_map/ppermute | solution.py:28
  59.5 10.0 %shard_map.28.w_ref = f32[256,256]{1,0:T(8,128)S(1)} custom-call(s32[1]{0:T(128)S(6)} %and.25.core_ref, f32[2,128,128]{2,1,0:T(8,128)S(1)} %pad_maximum_fusion.1.held_ref, f32[2,128,128]{2,1,0:T(8,128)S(1)} %collective-permute-done.12.other_ref), custom_call_target="tpu_custom_call" | custom-call | flops 12000000000 | bytes 500000 | tf_op jit(solution)/shard_map/pallas_call | solution.py:94
  69.5 1.3 %collective-permute-done.13 = f32[8,128,128]{2,1,0:T(8,128)S(1)} collective-permute-done((f32[8,128,128]{2,1,0:T(8,128)S(1)}, f32[8,128,128]{2,1,0:T(8,128)S(1)}, u32[]{:S(2)}, u32[]{:S(2)}) %collective-permute-start.13) | collective-permute-done | bytes 524320 | tf_op jit(solution)/shard_map/ppermute | solution.py:28
  73.7 5.6 %shard_map.29 = f32[8,128,8,128]{3,2,1,0:T(8,128)} custom-call(s32[2]{0:T(128)S(1)} %pad_add_fusion.place_ref, f32[8,128,8,128]{3,2,1,0:T(8,128)S(1)} %copy-done, f32[8,128,128]{2,1,0:T(8,128)S(1)} %add_add_fusion.held_ref, f32[2,128,128]{2,1,0:T(8,128)S(1)} %collective-permute-done.15.o0_ref, f32[2,128,128]{2,1,0:T(8,128)S(1)} %collective-permute-done.16.o1_ref, ...), custom_call_target="tpu_custom_call" | custom-call | flops 1610612736 | bytes 8388608 | tf_op jit(solution)/shard_map/pallas_call | solution.py:152
  (54 shorter events, 8.7 us)
Async XLA Ops:
  1.8 17.9 %collective-permute-start.1 = (f32[128,128]{1,0:T(8,128)S(1)}, f32[128,128]{1,0:T(8,128)S(1)}, u32[]{:S(2)}, u32[]{:S(2)}) collective-permute-start(f32[128,128]{1,0:T(8,128)S(1)} %add_select_fusion), channel_id=1, source_target_pairs={{0,10},{1,11},{16,26},{17,27},{32,42},{33,43},{48,58},{49,59},{64,... | collective-permute-start | bytes 196616 | tf_op jit(solution)/shard_map/ppermute | solution.py:28
  11.0 8.7 %collective-permute-start = (f32[128,128]{1,0:T(8,128)S(1)}, f32[128,128]{1,0:T(8,128)S(1)}, u32[]{:S(2)}, u32[]{:S(2)}) collective-permute-start(f32[128,128]{1,0:T(8,128)S(1)} %add_select_fusion), channel_id=1, source_target_pairs={{0,6},{1,7},{16,22},{17,23},{32,38},{33,39},{48,54},{49,55},{64,70... | collective-permute-start | bytes 196616 | tf_op jit(solution)/shard_map/ppermute | solution.py:28
  13.4 11.8 %collective-permute-start.21 = (f32[32,8,128]{2,1,0:T(8,128)S(1)}, f32[32,8,128]{2,1,0:T(8,128)S(1)}, u32[]{:S(2)}, u32[]{:S(2)}) collective-permute-start(f32[32,8,128]{2,1,0:T(8,128)S(1)} %get-tuple-element.9), channel_id=1, source_target_pairs={{0,192},{1,193},{2,194},{3,195},{4,196},{5,197},{6,198},{7,199},{8... | collective-permute-start | bytes 393224 | tf_op jit(solution)/shard_map/ppermute | solution.py:28
  16.2 11.1 %collective-permute-start.20 = (f32[32,8,128]{2,1,0:T(8,128)S(1)}, f32[32,8,128]{2,1,0:T(8,128)S(1)}, u32[]{:S(2)}, u32[]{:S(2)}) collective-permute-start(f32[32,8,128]{2,1,0:T(8,128)S(1)} %get-tuple-element.10), channel_id=1, source_target_pairs={{0,128},{1,129},{2,130},{3,131},{4,132},{5,133},{6,134},{7,135},{8... | collective-permute-start | bytes 393224 | tf_op jit(solution)/shard_map/ppermute | solution.py:28
  16.5 12.1 %collective-permute-start.19 = (f32[32,8,128]{2,1,0:T(8,128)S(1)}, f32[32,8,128]{2,1,0:T(8,128)S(1)}, u32[]{:S(2)}, u32[]{:S(2)}) collective-permute-start(f32[32,8,128]{2,1,0:T(8,128)S(1)} %get-tuple-element.11), channel_id=1, source_target_pairs={{0,64},{1,65},{2,66},{3,67},{4,68},{5,69},{6,70},{7,71},{8,72},{9,... | collective-permute-start | bytes 393224 | tf_op jit(solution)/shard_map/ppermute | solution.py:28
  19.8 2.7 %collective-permute-start.5 = (f32[128,128]{1,0:T(8,128)S(1)}, f32[128,128]{1,0:T(8,128)S(1)}, u32[]{:S(2)}, u32[]{:S(2)}) collective-permute-start(f32[128,128]{1,0:T(8,128)S(1)} %add_add_fusion.3), channel_id=1, source_target_pairs={{0,14},{1,15},{6,4},{7,5},{16,30},{17,31},{22,20},{23,21},{32,46},... | collective-permute-start | bytes 196616 | tf_op jit(solution)/shard_map/ppermute | solution.py:28
  21.1 2.7 %collective-permute-start.4 = (f32[128,128]{1,0:T(8,128)S(1)}, f32[128,128]{1,0:T(8,128)S(1)}, u32[]{:S(2)}, u32[]{:S(2)}) collective-permute-start(f32[128,128]{1,0:T(8,128)S(1)} %add_add_fusion.3), channel_id=1, source_target_pairs={{0,2},{1,3},{6,8},{7,9},{10,12},{11,13},{16,18},{17,19},{22,24},{2... | collective-permute-start | bytes 196616 | tf_op jit(solution)/shard_map/ppermute | solution.py:28
  22.5 24.5 %collective-permute-start.3 = (f32[8,128,128]{2,1,0:T(8,128)S(1)}, f32[8,128,128]{2,1,0:T(8,128)S(1)}, u32[]{:S(2)}, u32[]{:S(2)}) collective-permute-start(f32[8,128,128]{2,1,0:T(8,128)S(1)} %select_bitcast_fusion), channel_id=1, source_target_pairs={{0,10},{1,11},{16,26},{17,27},{32,42},{33,43},{48,58},{49,59},{64,... | collective-permute-start | bytes 1572872 | tf_op jit(solution)/shard_map/ppermute | solution.py:28
  23.8 28.5 %collective-permute-start.2 = (f32[8,128,128]{2,1,0:T(8,128)S(1)}, f32[8,128,128]{2,1,0:T(8,128)S(1)}, u32[]{:S(2)}, u32[]{:S(2)}) collective-permute-start(f32[8,128,128]{2,1,0:T(8,128)S(1)} %select_bitcast_fusion), channel_id=1, source_target_pairs={{0,6},{1,7},{16,22},{17,23},{32,38},{33,39},{48,54},{49,55},{64,70... | collective-permute-start | bytes 1572872 | tf_op jit(solution)/shard_map/ppermute | solution.py:28
  25.2 4.4 %collective-permute-start.8 = (f32[128,128]{1,0:T(8,128)S(1)}, f32[128,128]{1,0:T(8,128)S(1)}, u32[]{:S(2)}, u32[]{:S(2)}) collective-permute-start(f32[128,128]{1,0:T(8,128)S(1)} %add_add_fusion.2), channel_id=1, source_target_pairs={{0,192},{1,193},{2,194},{3,195},{4,196},{5,197},{6,198},{7,199},{8... | collective-permute-start | bytes 196616 | tf_op jit(solution)/shard_map/ppermute | solution.py:28
  27.2 4.9 %collective-permute-start.7 = (f32[128,128]{1,0:T(8,128)S(1)}, f32[128,128]{1,0:T(8,128)S(1)}, u32[]{:S(2)}, u32[]{:S(2)}) collective-permute-start(f32[128,128]{1,0:T(8,128)S(1)} %add_add_fusion.2), channel_id=1, source_target_pairs={{0,128},{1,129},{2,130},{3,131},{4,132},{5,133},{6,134},{7,135},{8... | collective-permute-start | bytes 196616 | tf_op jit(solution)/shard_map/ppermute | solution.py:28
  28.7 6.0 %collective-permute-start.6 = (f32[128,128]{1,0:T(8,128)S(1)}, f32[128,128]{1,0:T(8,128)S(1)}, u32[]{:S(2)}, u32[]{:S(2)}) collective-permute-start(f32[128,128]{1,0:T(8,128)S(1)} %add_add_fusion.2), channel_id=1, source_target_pairs={{0,64},{1,65},{2,66},{3,67},{4,68},{5,69},{6,70},{7,71},{8,72},{9,... | collective-permute-start | bytes 196616 | tf_op jit(solution)/shard_map/ppermute | solution.py:28
  29.6 5.3 %collective-permute-start.24 = (f32[32,8,128]{2,1,0:T(8,128)S(1)}, f32[32,8,128]{2,1,0:T(8,128)S(1)}, u32[]{:S(2)}, u32[]{:S(2)}) collective-permute-start(f32[32,8,128]{2,1,0:T(8,128)S(1)} %bitcast_select_fusion), channel_id=1, source_target_pairs={{0,48},{1,49},{2,50},{3,51},{4,52},{5,53},{6,54},{7,55},{8,56},{9,... | collective-permute-start | bytes 393224 | tf_op jit(solution)/shard_map/ppermute | solution.py:28
  32.2 5.3 %collective-permute-start.23 = (f32[32,8,128]{2,1,0:T(8,128)S(1)}, f32[32,8,128]{2,1,0:T(8,128)S(1)}, u32[]{:S(2)}, u32[]{:S(2)}) collective-permute-start(f32[32,8,128]{2,1,0:T(8,128)S(1)} %bitcast_select_fusion), channel_id=1, source_target_pairs={{0,32},{1,33},{2,34},{3,35},{4,36},{5,37},{6,38},{7,39},{8,40},{9,... | collective-permute-start | bytes 393224 | tf_op jit(solution)/shard_map/ppermute | solution.py:28
  34.6 5.4 %collective-permute-start.22 = (f32[32,8,128]{2,1,0:T(8,128)S(1)}, f32[32,8,128]{2,1,0:T(8,128)S(1)}, u32[]{:S(2)}, u32[]{:S(2)}) collective-permute-start(f32[32,8,128]{2,1,0:T(8,128)S(1)} %bitcast_select_fusion), channel_id=1, source_target_pairs={{0,16},{1,17},{2,18},{3,19},{4,20},{5,21},{6,22},{7,23},{8,24},{9,... | collective-permute-start | bytes 393224 | tf_op jit(solution)/shard_map/ppermute | solution.py:28
  35.0 6.4 %collective-permute-start.11 = (f32[128,128]{1,0:T(8,128)S(1)}, f32[128,128]{1,0:T(8,128)S(1)}, u32[]{:S(2)}, u32[]{:S(2)}) collective-permute-start(f32[128,128]{1,0:T(8,128)S(1)} %select_select_fusion), channel_id=1, source_target_pairs={{0,48},{1,49},{2,50},{3,51},{4,52},{5,53},{6,54},{7,55},{8,56},{9,... | collective-permute-start | bytes 196616 | tf_op jit(solution)/shard_map/ppermute | solution.py:28
  37.5 5.9 %collective-permute-start.10 = (f32[128,128]{1,0:T(8,128)S(1)}, f32[128,128]{1,0:T(8,128)S(1)}, u32[]{:S(2)}, u32[]{:S(2)}) collective-permute-start(f32[128,128]{1,0:T(8,128)S(1)} %select_select_fusion), channel_id=1, source_target_pairs={{0,32},{1,33},{2,34},{3,35},{4,36},{5,37},{6,38},{7,39},{8,40},{9,... | collective-permute-start | bytes 196616 | tf_op jit(solution)/shard_map/ppermute | solution.py:28
  40.0 4.8 %collective-permute-start.9 = (f32[128,128]{1,0:T(8,128)S(1)}, f32[128,128]{1,0:T(8,128)S(1)}, u32[]{:S(2)}, u32[]{:S(2)}) collective-permute-start(f32[128,128]{1,0:T(8,128)S(1)} %select_select_fusion), channel_id=1, source_target_pairs={{0,16},{1,17},{2,18},{3,19},{4,20},{5,21},{6,22},{7,23},{8,24},{9,... | collective-permute-start | bytes 196616 | tf_op jit(solution)/shard_map/ppermute | solution.py:28
  41.4 30.5 %collective-permute-start.27 = (f32[2,32,8,128]{3,2,1,0:T(8,128)S(1)}, f32[2,32,8,128]{3,2,1,0:T(8,128)S(1)}, u32[]{:S(2)}, u32[]{:S(2)}) collective-permute-start(f32[2,32,8,128]{3,2,1,0:T(8,128)S(1)} %pad_maximum_fusion.h0_ref), channel_id=1, source_target_pairs={{0,192},{1,193},{2,194},{3,195},{4,196},{5,197},{6,198},{7,199},{8... | collective-permute-start | bytes 786440 | tf_op jit(solution)/shard_map/ppermute | solution.py:28
  43.4 29.0 %collective-permute-start.26 = (f32[2,32,8,128]{3,2,1,0:T(8,128)S(1)}, f32[2,32,8,128]{3,2,1,0:T(8,128)S(1)}, u32[]{:S(2)}, u32[]{:S(2)}) collective-permute-start(f32[2,32,8,128]{3,2,1,0:T(8,128)S(1)} %pad_maximum_fusion.h0_ref), channel_id=1, source_target_pairs={{0,128},{1,129},{2,130},{3,131},{4,132},{5,133},{6,134},{7,135},{8... | collective-permute-start | bytes 786440 | tf_op jit(solution)/shard_map/ppermute | solution.py:28
  44.8 27.9 %collective-permute-start.25 = (f32[2,32,8,128]{3,2,1,0:T(8,128)S(1)}, f32[2,32,8,128]{3,2,1,0:T(8,128)S(1)}, u32[]{:S(2)}, u32[]{:S(2)}) collective-permute-start(f32[2,32,8,128]{3,2,1,0:T(8,128)S(1)} %pad_maximum_fusion.h0_ref), channel_id=1, source_target_pairs={{0,64},{1,65},{2,66},{3,67},{4,68},{5,69},{6,70},{7,71},{8,72},{9,... | collective-permute-start | bytes 786440 | tf_op jit(solution)/shard_map/ppermute | solution.py:28
  47.0 11.1 %collective-permute-start.12 = (f32[2,128,128]{2,1,0:T(8,128)S(1)}, f32[2,128,128]{2,1,0:T(8,128)S(1)}, u32[]{:S(2)}, u32[]{:S(2)}) collective-permute-start(f32[2,128,128]{2,1,0:T(8,128)S(1)} %pad_maximum_fusion.1.held_ref), channel_id=1, source_target_pairs={{0,1},{1,0},{2,3},{3,2},{4,5},{5,4},{6,7},{7,6},{8,9},{9,8},{10,11... | collective-permute-start | bytes 393224 | tf_op jit(solution)/shard_map/ppermute | solution.py:28
  52.4 17.1 %collective-permute-start.14 = (f32[8,128,128]{2,1,0:T(8,128)S(1)}, f32[8,128,128]{2,1,0:T(8,128)S(1)}, u32[]{:S(2)}, u32[]{:S(2)}) collective-permute-start(f32[8,128,128]{2,1,0:T(8,128)S(1)} %add_add_fusion.1), channel_id=1, source_target_pairs={{0,14},{1,15},{6,4},{7,5},{16,30},{17,31},{22,20},{23,21},{32,46},... | collective-permute-start | bytes 1572872 | tf_op jit(solution)/shard_map/ppermute | solution.py:28
  58.2 12.6 %collective-permute-start.13 = (f32[8,128,128]{2,1,0:T(8,128)S(1)}, f32[8,128,128]{2,1,0:T(8,128)S(1)}, u32[]{:S(2)}, u32[]{:S(2)}) collective-permute-start(f32[8,128,128]{2,1,0:T(8,128)S(1)} %add_add_fusion.1), channel_id=1, source_target_pairs={{0,2},{1,3},{6,8},{7,9},{10,12},{11,13},{16,18},{17,19},{22,24},{2... | collective-permute-start | bytes 1572872 | tf_op jit(solution)/shard_map/ppermute | solution.py:28
  (5 other events, 20.2 us)

commit v4 on v3

--- a/solution.py
+++ b/solution.py
@@ -29,19 +29,21 @@
 
 
 def invert_factor(rows):
-    sub = lax.broadcasted_iota(jnp.int32, (8, 128), 0)
-    lane = lax.broadcasted_iota(jnp.int32, (8, 128), 1)
-    spread = lambda v, i: jnp.broadcast_to(v[i:i + 1, :], (8, 128))
+    size = rows[0].shape[0]
+    shape = (size, 128)
+    sub = lax.broadcasted_iota(jnp.int32, shape, 0)
+    lane = lax.broadcasted_iota(jnp.int32, shape, 1)
+    spread = lambda v, i: jnp.broadcast_to(v[i:i + 1, :], shape)
     rows = list(rows)
     out = []
-    for g in range(16):
-        first = 8 * g
-        column = lambda i, l: jnp.broadcast_to(rows[i][:, first + l:first + l + 1], (8, 128))
-        own = [column(g, l) for l in range(8)]
-        below = [[column(i, l) for l in range(8)] for i in range(g + 1, 16)]
+    for g in range(128 // size):
+        first = size * g
+        column = lambda i, l: jnp.broadcast_to(rows[i][:, first + l:first + l + 1], shape)
+        own = [column(g, l) for l in range(size)]
+        below = [column(g + 1, l) for l in range(size)] if g + 1 < 128 // size else []
         panel = rows[g]
-        kept = jnp.zeros((8, 128), f32)
-        for p in range(8):
+        kept = jnp.zeros(shape, f32)
+        for p in range(size):
             here = sub == p
             panel = jnp.where(lane == first + p, jnp.where(here, 1.0, 0.0), panel)
             pivot = spread(own[p], p)
@@ -50,17 +52,28 @@
             row = spread(panel, p)
             kept = jnp.where(here, row * lax.rsqrt(pivot), kept)
             panel = jnp.where(here, row * inv, panel - factor * row)
-            for l in range(p + 1, 8):
+            for l in range(p + 1, size):
                 mine = spread(own[l], p)
                 own[l] = jnp.where(here, mine * inv, own[l] - factor * mine)
         out.append(jnp.where(lane <= sub + first, kept, 0.0))
-        cleared = (lane >= first) & (lane < first + 8)
-        spreads = [spread(panel, l) for l in range(8)]
-        for n, i in enumerate(range(g + 1, 16)):
-            acc = jnp.where(cleared, 0.0, rows[i])
-            for l in range(8):
-                acc = acc - below[n][l] * spreads[l]
-            rows[i] = acc
+        cleared = (lane >= first) & (lane < first + size)
+        left = rows[g + 1:]
+        if not left:
+            break
+        acc = jnp.where(cleared, 0.0, left[0])
+        for l in range(size):
+            acc = acc - below[l] * spread(panel, l)
+        rows[g + 1] = acc
+        if len(left) > 1:
+            rest = jnp.concatenate(left[1:], axis=0)
+            lanes = lax.broadcasted_iota(jnp.int32, rest.shape, 1)
+            cleared = (lanes >= first) & (lanes < first + size)
+            zero = jnp.zeros(shape, f32)
+            right = jnp.concatenate([panel if i == g else zero for i in range(128 // size)], axis=0)
+            rest = jnp.where(cleared, 0.0, rest) - jnp.dot(
+                jnp.where(cleared, rest, 0.0), right, precision=HIGHEST, preferred_element_type=f32)
+            for n in range(len(left) - 1):
+                rows[g + 2 + n] = rest[size * n:size * n + size]
     return out
 
 
@@ -69,7 +82,7 @@
 
 
 def groups(block):
-    return [block[8 * i:8 * i + 8, :] for i in range(16)]
+    return [block[16 * i:16 * i + 16, :] for i in range(8)]
 
 
 def factor_kernel(core_ref, held_ref, other_ref, w_ref):
@@ -188,22 +201,21 @@
     return lax.optimization_barrier((value, *others))[0]
 
 
-def first_z(held):
-    near = send(held, lambda x, y, z, k: (x, y, 3, k) if z == 0 else None)
-    far = send(held, lambda x, y, z, k: (x, y, 5, k) if z == 0 else None)
-    return held, near, far
-
-
-def second_z(held):
-    up = {0: 1, 3: 4, 5: 6}
-    down = {0: 7, 3: 2}
-    near = send(held, lambda x, y, z, k: (x, y, up[z], k) if z in up else None)
-    far = send(held, lambda x, y, z, k: (x, y, down[z], k) if z in down else None)
-    return held, near, far
+def along_z(step, held):
+    moves = ({0: 2}, {0: 6, 2: 4}, {0: 1, 2: 3, 4: 5, 6: 7})[step - 1]
+
+    def target(x, y, z, k):
+        turned = z if k == 0 else -z & 7
+        if turned not in moves:
+            return None
+        to = moves[turned]
+        return x, y, to if k == 0 else -to & 7, k
+
+    return held, send(held, target)
 
 
 def total(parts):
-    return parts[0] + parts[1] + parts[2]
+    return parts[0] + parts[1]
 
 
 def swap(held):
@@ -223,21 +235,26 @@
     x, y, z, core = place_of(row, col)
     place = jnp.stack([row, col]).astype(jnp.int32)
 
-    pivot = jnp.where(z == 0, pivot_block(coupling, diagonal, x, core), 0.0)
     rows = jnp.where(z == 0, coupling[:, :, 0, :], 0.0)
-    pivot = total(first_z(pivot))
-    rows = first_z(after(rows, pivot))
-    pivot = total(second_z(pivot))
+    pivot = pivot_block(coupling, diagonal, x, core)
     quarters = [coupling[0, 32 * n:32 * n + 32] for n in range(4)]
+    turned = turns([pivot] * 3, along_y)
+    pivot, rows = lax.optimization_barrier((pivot, rows))
+    pivot = pick(y, [pivot, *turned])
     cols = pick(y, [quarters[0], *turns(quarters[1:], along_y)])
-    pivot = pick(y, [pivot, *turns([pivot] * 3, along_y)])
+    pivots = columns_zero_and_one(pivot, turns([pivot] * 3, along_x), x)
+    rows = along_z(1, after(rows, pivots))
+    pivots = total(along_z(1, jnp.where(z == 0, pivots, 0.0)))
+    rows = along_z(2, after(total(rows), pivots))
+    pivots, cols = lax.optimization_barrier((pivots, cols))
     cols = columns_zero_and_one(cols, turns([cols] * 3, along_x), x)
-    pivots = columns_zero_and_one(pivot, turns([pivot] * 3, along_x), x)
+    pivots = total(along_z(2, pivots))
+    pivots = total(along_z(3, pivots))
     other_pivots = swap(pivots)
-    rows = second_z(total(rows))
+    rows = along_z(3, after(total(rows), pivots))
     cols = [cols, *turns([cols] * 3, along_y)]
     w = factor(place[1:] & 1, pivots, other_pivots)
-    rows = total((after(rows[0], w), *rows[1:]))
+    rows = total((after(rows[0], w), rows[1]))
     return update(place, coupling, (rows, *[swap(rows[2 * n:2 * n + 2]) for n in range(4)]), cols, w)
 
 

time: 79.8 us -> 72 us (0.902)
  starting transfers between devices: 54.1 us -> 40.4 us
  waiting for transfers between devices: 2.61 us -> 11.4 us
  Pallas kernels: 15.5 us -> 11.8 us
    ppermute x28 -> x26, starting transfers between devices: 54.1 us -> 40.4 us  [send(): return lax.ppermute(value, AXES, pairs)]
    ppermute x28 -> x26, waiting for transfers between devices: 2.61 us -> 11.4 us  [send(): return lax.ppermute(value, AXES, pairs)]
    pallas_call x1, Pallas kernels: 9.98 us -> 6.28 us  [factor(): pl.pallas_call(factor_kernel, in_specs=[pl.BlockSpec(memory_space=pltpu.S...]
  transfers between devices with their start and end apart: 28 -> 26, of which waited for: 6 -> 12; matrix products, arithmetic and copies ran while one was open for 6% -> 7% of each run, Pallas kernels for 13% -> 9%
where the time goes in v4:
time: 72 us; the launch traced here: 70.9 us
  starting transfers between devices  40.4 us (56%)
  Pallas kernels  11.8 us (16%)
  waiting for transfers between devices  11.4 us (16%)
  local copies, waits for them, and re-layouts  5.35 us (7%)
  other arithmetic  1.46 us (2%)
    ppermute x26, starting transfers between devices, send(): return lax.ppermute(value, AXES, pairs)  40.4 us
    ppermute x26, waiting for transfers between devices, send(): return lax.ppermute(value, AXES, pairs)  11.4 us
    pallas_call x1, Pallas kernels, factor(): pl.pallas_call(factor_kernel, in_specs=[pl.BlockSpec(memory_space=pltpu.S...  6.28 us
    pallas_call x1, Pallas kernels, update(): pl.pallas_call(update_kernel, in_specs=[pl.BlockSpec(memory_space=pltpu.S...  5.56 us
    slice x1, local copies, waits for them, and re-layouts, on_device(): rows = jnp.where(z == 0, coupling[:, :, 0, :], 0.0)  2.49 us
  transfers between devices with their start and end apart: 26, of which 12 were waited for; matrix products, arithmetic and copies ran while one was open for 7% of the time, Pallas kernels for 9%

profile of v4, /device:TPU:1, one launch (start us, length us, event | category | flops | bytes accessed | tf_op | source)
XLA Modules:
  0.0 70.9 jit_solution(11364544046794937139)
XLA Ops:
  0.7 1.1 %slice.33 = f32[1,128,1,128]{3,2,1,0:T(1,128)S(1)} slice(f32[8,128,8,128]{3,2,1,0:T(8,128)} %x_ref.1), slice={[0:1], [0:128], [0:1], [0:128]} | slice | bytes 131072 | tf_op jit(solution)/shard_map/slice | solution.py:226
  1.8 3.6 %collective-permute-start.2 = (f32[128,128]{1,0:T(8,128)S(1)}, f32[128,128]{1,0:T(8,128)S(1)}, u32[]{:S(2)}, u32[]{:S(2)}) collective-permute-start(f32[128,128]{1,0:T(8,128)S(1)} %select_add_fusion), channel_id=1, source_target_pairs={{0,192},{1,193},{2,194},{3,195},{4,196},{5,197},{6,198},{7,199},{8... | collective-permute-start | bytes 196616 | tf_op jit(solution)/shard_map/ppermute | solution.py:28
  6.5 2.5 %slice.35 = f32[8,128,1,128]{3,2,1,0:T(1,128)S(1)} slice(f32[8,128,8,128]{3,2,1,0:T(8,128)} %x_ref.1), slice={[0:8], [0:128], [0:1], [0:128]} | slice | bytes 1048576 | tf_op jit(solution)/shard_map/slice | solution.py:238
  9.1 1.1 %collective-permute-done.1 = f32[128,128]{1,0:T(8,128)S(1)} collective-permute-done((f32[128,128]{1,0:T(8,128)S(1)}, f32[128,128]{1,0:T(8,128)S(1)}, u32[]{:S(2)}, u32[]{:S(2)}) %collective-permute-start.1) | collective-permute-done | bytes 65568 | tf_op jit(solution)/shard_map/ppermute | solution.py:28
  10.8 2.6 %collective-permute-start.5 = (f32[128,128]{1,0:T(8,128)S(1)}, f32[128,128]{1,0:T(8,128)S(1)}, u32[]{:S(2)}, u32[]{:S(2)}) collective-permute-start(f32[128,128]{1,0:T(8,128)S(1)} %select_select_fusion), channel_id=1, source_target_pairs={{0,48},{1,49},{2,50},{3,51},{4,52},{5,53},{6,54},{7,55},{8,56},{9,... | collective-permute-start | bytes 196616 | tf_op jit(solution)/shard_map/ppermute | solution.py:28
  14.5 1.1 %slice_bitcast_fusion = (f32[32,8,128]{2,1,0:T(8,128)S(1)}, f32[32,8,128]{2,1,0:T(8,128)S(1)}, f32[32,8,128]{2,1,0:T(8,128)S(1)}) fusion(f32[8,128,8,128]{3,2,1,0:T(8,128)} %x_ref.1), kind=kLoop, calls=%fused_computation.6 | loop fusion | bytes 786432 | tf_op jit(solution)/shard_map/squeeze | solution.py:240
  16.2 1.1 %collective-permute-start.10 = (f32[32,8,128]{2,1,0:T(8,128)S(1)}, f32[32,8,128]{2,1,0:T(8,128)S(1)}, u32[]{:S(2)}, u32[]{:S(2)}) collective-permute-start(f32[32,8,128]{2,1,0:T(8,128)S(1)} %get-tuple-element.22), channel_id=1, source_target_pairs={{0,128},{1,129},{2,130},{3,131},{4,132},{5,133},{6,134},{7,135},{8... | collective-permute-start | bytes 393224 | tf_op jit(solution)/shard_map/ppermute | solution.py:28
  18.0 7.9 %collective-permute-start.6 = (f32[8,128,128]{2,1,0:T(8,128)S(1)}, f32[8,128,128]{2,1,0:T(8,128)S(1)}, u32[]{:S(2)}, u32[]{:S(2)}) collective-permute-start(f32[8,128,128]{2,1,0:T(8,128)S(1)} %select_bitcast_fusion), channel_id=1, source_target_pairs={{0,4},{1,13},{16,20},{17,29},{32,36},{33,45},{48,52},{49,61},{64,6... | collective-permute-start | bytes 1572872 | tf_op jit(solution)/shard_map/ppermute | solution.py:28
  26.0 1.3 %collective-permute-start.7 = (f32[2,128,128]{2,1,0:T(8,128)S(1)}, f32[2,128,128]{2,1,0:T(8,128)S(1)}, u32[]{:S(2)}, u32[]{:S(2)}) collective-permute-start(f32[2,128,128]{2,1,0:T(8,128)S(1)} %broadcast_select_fusion), channel_id=1, source_target_pairs={{0,4},{1,13},{16,20},{17,29},{32,36},{33,45},{48,52},{49,61},{64,6... | collective-permute-start | bytes 393224 | tf_op jit(solution)/shard_map/ppermute | solution.py:28
  27.4 0.9 %bitcast_select_fusion = f32[32,8,128]{2,1,0:T(8,128)S(1)} fusion(f32[32,8,128]{2,1,0:T(8,128)S(1)} %collective-permute-done.9, f32[32,8,128]{2,1,0:T(8,128)S(1)} %collective-permute-done.10, f32[32,8,128]{2,1,0:T(8,128)S(1)} %collective-permute-done.11, f32[8,128,8,128]{3,2,1,0:T(8,128)} %x_ref.1, pred[]{:T(512)S(6)} %eq.52, pred[]{:T(512)S(6)} %eq.51, ...), kind=kLoop, calls=%fused_computation.3 | loop fusion | flops 98304 | bytes 655363 | tf_op jit(solution)/shard_map/jit(_where)/select_n | solution.py:191
  28.3 5.1 %collective-permute-done.7 = f32[2,128,128]{2,1,0:T(8,128)S(1)} collective-permute-done((f32[2,128,128]{2,1,0:T(8,128)S(1)}, f32[2,128,128]{2,1,0:T(8,128)S(1)}, u32[]{:S(2)}, u32[]{:S(2)}) %collective-permute-start.7) | collective-permute-done | bytes 131104 | tf_op jit(solution)/shard_map/ppermute | solution.py:28
  33.5 1.3 %collective-permute-start.12 = (f32[2,128,128]{2,1,0:T(8,128)S(1)}, f32[2,128,128]{2,1,0:T(8,128)S(1)}, u32[]{:S(2)}, u32[]{:S(2)}) collective-permute-start(f32[2,128,128]{2,1,0:T(8,128)S(1)} %fusion.2), channel_id=1, source_target_pairs={{0,12},{1,5},{4,8},{13,9},{16,28},{17,21},{20,24},{29,25},{32,44},... | collective-permute-start | bytes 393224 | tf_op jit(solution)/shard_map/ppermute | solution.py:28
  34.9 1.3 %collective-permute-start.8 = (f32[8,128,128]{2,1,0:T(8,128)S(1)}, f32[8,128,128]{2,1,0:T(8,128)S(1)}, u32[]{:S(2)}, u32[]{:S(2)}) collective-permute-start(f32[8,128,128]{2,1,0:T(8,128)S(1)} %add.27), channel_id=1, source_target_pairs={{0,12},{1,5},{4,8},{13,9},{16,28},{17,21},{20,24},{29,25},{32,44},... | collective-permute-start | bytes 1572872 | tf_op jit(solution)/shard_map/ppermute | solution.py:28
  36.7 1.3 %collective-permute-start.13 = (f32[2,128,128]{2,1,0:T(8,128)S(1)}, f32[2,128,128]{2,1,0:T(8,128)S(1)}, u32[]{:S(2)}, u32[]{:S(2)}) collective-permute-start(f32[2,128,128]{2,1,0:T(8,128)S(1)} %add.30), channel_id=1, source_target_pairs={{0,2},{1,15},{4,6},{5,3},{8,10},{9,7},{12,14},{13,11},{16,18},{17,... | collective-permute-start | bytes 393224 | tf_op jit(solution)/shard_map/ppermute | solution.py:28
  38.0 2.1 %collective-permute-start.22 = (f32[32,8,128]{2,1,0:T(8,128)S(1)}, f32[32,8,128]{2,1,0:T(8,128)S(1)}, u32[]{:S(2)}, u32[]{:S(2)}) collective-permute-start(f32[32,8,128]{2,1,0:T(8,128)S(1)} %bitcast_select_fusion), channel_id=1, source_target_pairs={{0,48},{1,49},{2,50},{3,51},{4,52},{5,53},{6,54},{7,55},{8,56},{9,... | collective-permute-start | bytes 393224 | tf_op jit(solution)/shard_map/ppermute | solution.py:28
  40.1 1.2 %collective-permute-start.21 = (f32[32,8,128]{2,1,0:T(8,128)S(1)}, f32[32,8,128]{2,1,0:T(8,128)S(1)}, u32[]{:S(2)}, u32[]{:S(2)}) collective-permute-start(f32[32,8,128]{2,1,0:T(8,128)S(1)} %bitcast_select_fusion), channel_id=1, source_target_pairs={{0,32},{1,33},{2,34},{3,35},{4,36},{5,37},{6,38},{7,39},{8,40},{9,... | collective-permute-start | bytes 393224 | tf_op jit(solution)/shard_map/ppermute | solution.py:28
  41.4 2.7 %collective-permute-start.14 = (f32[2,128,128]{2,1,0:T(8,128)S(1)}, f32[2,128,128]{2,1,0:T(8,128)S(1)}, u32[]{:S(2)}, u32[]{:S(2)}) collective-permute-start(f32[2,128,128]{2,1,0:T(8,128)S(1)} %add.31.held_ref), channel_id=1, source_target_pairs={{0,1},{1,0},{2,3},{3,2},{4,5},{5,4},{6,7},{7,6},{8,9},{9,8},{10,11... | collective-permute-start | bytes 393224 | tf_op jit(solution)/shard_map/ppermute | solution.py:28
  44.1 1.4 %collective-permute-done.21 = f32[32,8,128]{2,1,0:T(8,128)S(1)} collective-permute-done((f32[32,8,128]{2,1,0:T(8,128)S(1)}, f32[32,8,128]{2,1,0:T(8,128)S(1)}, u32[]{:S(2)}, u32[]{:S(2)}) %collective-permute-start.21) | collective-permute-done | bytes 131104 | tf_op jit(solution)/shard_map/ppermute | solution.py:28
  45.5 1.4 %collective-permute-done.20 = f32[32,8,128]{2,1,0:T(8,128)S(1)} collective-permute-done((f32[32,8,128]{2,1,0:T(8,128)S(1)}, f32[32,8,128]{2,1,0:T(8,128)S(1)}, u32[]{:S(2)}, u32[]{:S(2)}) %collective-permute-start.20) | collective-permute-done | bytes 131104 | tf_op jit(solution)/shard_map/ppermute | solution.py:28
  46.9 2.8 %collective-permute-start.25 = (f32[2,32,8,128]{3,2,1,0:T(8,128)S(1)}, f32[2,32,8,128]{3,2,1,0:T(8,128)S(1)}, u32[]{:S(2)}, u32[]{:S(2)}) collective-permute-start(f32[2,32,8,128]{3,2,1,0:T(8,128)S(1)} %pad_maximum_fusion.h0_ref), channel_id=1, source_target_pairs={{0,192},{1,193},{2,194},{3,195},{4,196},{5,197},{6,198},{7,199},{8... | collective-permute-start | bytes 786440 | tf_op jit(solution)/shard_map/ppermute | solution.py:28
  50.6 3.1 %collective-permute-start.15 = (f32[8,128,128]{2,1,0:T(8,128)S(1)}, f32[8,128,128]{2,1,0:T(8,128)S(1)}, u32[]{:S(2)}, u32[]{:S(2)}) collective-permute-start(f32[8,128,128]{2,1,0:T(8,128)S(1)} %add.29), channel_id=1, source_target_pairs={{0,2},{1,15},{4,6},{5,3},{8,10},{9,7},{12,14},{13,11},{16,18},{17,... | collective-permute-start | bytes 1572872 | tf_op jit(solution)/shard_map/ppermute | solution.py:28
  53.8 6.3 %shard_map.28.w_ref = f32[256,256]{1,0:T(8,128)S(1)} custom-call(s32[1]{0:T(128)S(6)} %and.26.core_ref, f32[2,128,128]{2,1,0:T(8,128)S(1)} %add.31.held_ref, f32[2,128,128]{2,1,0:T(8,128)S(1)} %collective-permute-done.14.other_ref), custom_call_target="tpu_custom_call" | custom-call | flops 12000000000 | bytes 500000 | tf_op jit(solution)/shard_map/pallas_call | solution.py:107
  60.2 3.1 %collective-permute-start.19 = (f32[2,128,128]{2,1,0:T(8,128)S(1)}, f32[2,128,128]{2,1,0:T(8,128)S(1)}, u32[]{:S(2)}, u32[]{:S(2)}) collective-permute-start(f32[2,128,128]{2,1,0:T(8,128)S(1)} %get-tuple-element.26), channel_id=1, source_target_pairs={{0,1},{1,0},{2,3},{3,2},{4,5},{5,4},{6,7},{7,6},{8,9},{9,8},{10,11... | collective-permute-start | bytes 393224 | tf_op jit(solution)/shard_map/ppermute | solution.py:28
  65.1 5.6 %shard_map.29 = f32[8,128,8,128]{3,2,1,0:T(8,128)} custom-call(s32[2]{0:T(128)S(1)} %pad_add_fusion.place_ref, f32[8,128,8,128]{3,2,1,0:T(8,128)S(1)} %copy-done, f32[8,128,128]{2,1,0:T(8,128)S(1)} %add.32.held_ref, f32[2,128,128]{2,1,0:T(8,128)S(1)} %collective-permute-done.16.o0_ref, f32[2,128,128]{2,1,0:T(8,128)S(1)} %collective-permute-done.17.o1_ref, ...), custom_call_target="tpu_custom_call" | custom-call | flops 1610612736 | bytes 8388608 | tf_op jit(solution)/shard_map/pallas_call | solution.py:165
  (52 shorter events, 8.6 us)
Async XLA Ops:
  1.8 7.2 %collective-permute-start.2 = (f32[128,128]{1,0:T(8,128)S(1)}, f32[128,128]{1,0:T(8,128)S(1)}, u32[]{:S(2)}, u32[]{:S(2)}) collective-permute-start(f32[128,128]{1,0:T(8,128)S(1)} %select_add_fusion), channel_id=1, source_target_pairs={{0,192},{1,193},{2,194},{3,195},{4,196},{5,197},{6,198},{7,199},{8... | collective-permute-start | bytes 196616 | tf_op jit(solution)/shard_map/ppermute | solution.py:28
  5.4 4.7 %collective-permute-start.1 = (f32[128,128]{1,0:T(8,128)S(1)}, f32[128,128]{1,0:T(8,128)S(1)}, u32[]{:S(2)}, u32[]{:S(2)}) collective-permute-start(f32[128,128]{1,0:T(8,128)S(1)} %select_add_fusion), channel_id=1, source_target_pairs={{0,128},{1,129},{2,130},{3,131},{4,132},{5,133},{6,134},{7,135},{8... | collective-permute-start | bytes 196616 | tf_op jit(solution)/shard_map/ppermute | solution.py:28
  5.8 5.0 %collective-permute-start = (f32[128,128]{1,0:T(8,128)S(1)}, f32[128,128]{1,0:T(8,128)S(1)}, u32[]{:S(2)}, u32[]{:S(2)}) collective-permute-start(f32[128,128]{1,0:T(8,128)S(1)} %select_add_fusion), channel_id=1, source_target_pairs={{0,64},{1,65},{2,66},{3,67},{4,68},{5,69},{6,70},{7,71},{8,72},{9,... | collective-permute-start | bytes 196616 | tf_op jit(solution)/shard_map/ppermute | solution.py:28
  10.8 6.5 %collective-permute-start.5 = (f32[128,128]{1,0:T(8,128)S(1)}, f32[128,128]{1,0:T(8,128)S(1)}, u32[]{:S(2)}, u32[]{:S(2)}) collective-permute-start(f32[128,128]{1,0:T(8,128)S(1)} %select_select_fusion), channel_id=1, source_target_pairs={{0,48},{1,49},{2,50},{3,51},{4,52},{5,53},{6,54},{7,55},{8,56},{9,... | collective-permute-start | bytes 196616 | tf_op jit(solution)/shard_map/ppermute | solution.py:28
  13.3 4.7 %collective-permute-start.4 = (f32[128,128]{1,0:T(8,128)S(1)}, f32[128,128]{1,0:T(8,128)S(1)}, u32[]{:S(2)}, u32[]{:S(2)}) collective-permute-start(f32[128,128]{1,0:T(8,128)S(1)} %select_select_fusion), channel_id=1, source_target_pairs={{0,32},{1,33},{2,34},{3,35},{4,36},{5,37},{6,38},{7,39},{8,40},{9,... | collective-permute-start | bytes 196616 | tf_op jit(solution)/shard_map/ppermute | solution.py:28
  13.9 12.1 %collective-permute-start.3 = (f32[128,128]{1,0:T(8,128)S(1)}, f32[128,128]{1,0:T(8,128)S(1)}, u32[]{:S(2)}, u32[]{:S(2)}) collective-permute-start(f32[128,128]{1,0:T(8,128)S(1)} %select_select_fusion), channel_id=1, source_target_pairs={{0,16},{1,17},{2,18},{3,19},{4,20},{5,21},{6,22},{7,23},{8,24},{9,... | collective-permute-start | bytes 196616 | tf_op jit(solution)/shard_map/ppermute | solution.py:28
  15.5 11.8 %collective-permute-start.11 = (f32[32,8,128]{2,1,0:T(8,128)S(1)}, f32[32,8,128]{2,1,0:T(8,128)S(1)}, u32[]{:S(2)}, u32[]{:S(2)}) collective-permute-start(f32[32,8,128]{2,1,0:T(8,128)S(1)} %get-tuple-element.21), channel_id=1, source_target_pairs={{0,192},{1,193},{2,194},{3,195},{4,196},{5,197},{6,198},{7,199},{8... | collective-permute-start | bytes 393224 | tf_op jit(solution)/shard_map/ppermute | solution.py:28
  16.2 11.2 %collective-permute-start.10 = (f32[32,8,128]{2,1,0:T(8,128)S(1)}, f32[32,8,128]{2,1,0:T(8,128)S(1)}, u32[]{:S(2)}, u32[]{:S(2)}) collective-permute-start(f32[32,8,128]{2,1,0:T(8,128)S(1)} %get-tuple-element.22), channel_id=1, source_target_pairs={{0,128},{1,129},{2,130},{3,131},{4,132},{5,133},{6,134},{7,135},{8... | collective-permute-start | bytes 393224 | tf_op jit(solution)/shard_map/ppermute | solution.py:28
  17.3 10.0 %collective-permute-start.9 = (f32[32,8,128]{2,1,0:T(8,128)S(1)}, f32[32,8,128]{2,1,0:T(8,128)S(1)}, u32[]{:S(2)}, u32[]{:S(2)}) collective-permute-start(f32[32,8,128]{2,1,0:T(8,128)S(1)} %get-tuple-element.23), channel_id=1, source_target_pairs={{0,64},{1,65},{2,66},{3,67},{4,68},{5,69},{6,70},{7,71},{8,72},{9,... | collective-permute-start | bytes 393224 | tf_op jit(solution)/shard_map/ppermute | solution.py:28
  18.0 16.8 %collective-permute-start.6 = (f32[8,128,128]{2,1,0:T(8,128)S(1)}, f32[8,128,128]{2,1,0:T(8,128)S(1)}, u32[]{:S(2)}, u32[]{:S(2)}) collective-permute-start(f32[8,128,128]{2,1,0:T(8,128)S(1)} %select_bitcast_fusion), channel_id=1, source_target_pairs={{0,4},{1,13},{16,20},{17,29},{32,36},{33,45},{48,52},{49,61},{64,6... | collective-permute-start | bytes 1572872 | tf_op jit(solution)/shard_map/ppermute | solution.py:28
  26.0 7.4 %collective-permute-start.7 = (f32[2,128,128]{2,1,0:T(8,128)S(1)}, f32[2,128,128]{2,1,0:T(8,128)S(1)}, u32[]{:S(2)}, u32[]{:S(2)}) collective-permute-start(f32[2,128,128]{2,1,0:T(8,128)S(1)} %broadcast_select_fusion), channel_id=1, source_target_pairs={{0,4},{1,13},{16,20},{17,29},{32,36},{33,45},{48,52},{49,61},{64,6... | collective-permute-start | bytes 393224 | tf_op jit(solution)/shard_map/ppermute | solution.py:28
  33.5 3.2 %collective-permute-start.12 = (f32[2,128,128]{2,1,0:T(8,128)S(1)}, f32[2,128,128]{2,1,0:T(8,128)S(1)}, u32[]{:S(2)}, u32[]{:S(2)}) collective-permute-start(f32[2,128,128]{2,1,0:T(8,128)S(1)} %fusion.2), channel_id=1, source_target_pairs={{0,12},{1,5},{4,8},{13,9},{16,28},{17,21},{20,24},{29,25},{32,44},... | collective-permute-start | bytes 393224 | tf_op jit(solution)/shard_map/ppermute | solution.py:28
  34.9 15.7 %collective-permute-start.8 = (f32[8,128,128]{2,1,0:T(8,128)S(1)}, f32[8,128,128]{2,1,0:T(8,128)S(1)}, u32[]{:S(2)}, u32[]{:S(2)}) collective-permute-start(f32[8,128,128]{2,1,0:T(8,128)S(1)} %add.27), channel_id=1, source_target_pairs={{0,12},{1,5},{4,8},{13,9},{16,28},{17,21},{20,24},{29,25},{32,44},... | collective-permute-start | bytes 1572872 | tf_op jit(solution)/shard_map/ppermute | solution.py:28
  36.7 4.7 %collective-permute-start.13 = (f32[2,128,128]{2,1,0:T(8,128)S(1)}, f32[2,128,128]{2,1,0:T(8,128)S(1)}, u32[]{:S(2)}, u32[]{:S(2)}) collective-permute-start(f32[2,128,128]{2,1,0:T(8,128)S(1)} %add.30), channel_id=1, source_target_pairs={{0,2},{1,15},{4,6},{5,3},{8,10},{9,7},{12,14},{13,11},{16,18},{17,... | collective-permute-start | bytes 393224 | tf_op jit(solution)/shard_map/ppermute | solution.py:28
  38.0 6.1 %collective-permute-start.22 = (f32[32,8,128]{2,1,0:T(8,128)S(1)}, f32[32,8,128]{2,1,0:T(8,128)S(1)}, u32[]{:S(2)}, u32[]{:S(2)}) collective-permute-start(f32[32,8,128]{2,1,0:T(8,128)S(1)} %bitcast_select_fusion), channel_id=1, source_target_pairs={{0,48},{1,49},{2,50},{3,51},{4,52},{5,53},{6,54},{7,55},{8,56},{9,... | collective-permute-start | bytes 393224 | tf_op jit(solution)/shard_map/ppermute | solution.py:28
  40.1 5.4 %collective-permute-start.21 = (f32[32,8,128]{2,1,0:T(8,128)S(1)}, f32[32,8,128]{2,1,0:T(8,128)S(1)}, u32[]{:S(2)}, u32[]{:S(2)}) collective-permute-start(f32[32,8,128]{2,1,0:T(8,128)S(1)} %bitcast_select_fusion), channel_id=1, source_target_pairs={{0,32},{1,33},{2,34},{3,35},{4,36},{5,37},{6,38},{7,39},{8,40},{9,... | collective-permute-start | bytes 393224 | tf_op jit(solution)/shard_map/ppermute | solution.py:28
  41.3 5.5 %collective-permute-start.20 = (f32[32,8,128]{2,1,0:T(8,128)S(1)}, f32[32,8,128]{2,1,0:T(8,128)S(1)}, u32[]{:S(2)}, u32[]{:S(2)}) collective-permute-start(f32[32,8,128]{2,1,0:T(8,128)S(1)} %bitcast_select_fusion), channel_id=1, source_target_pairs={{0,16},{1,17},{2,18},{3,19},{4,20},{5,21},{6,22},{7,23},{8,24},{9,... | collective-permute-start | bytes 393224 | tf_op jit(solution)/shard_map/ppermute | solution.py:28
  41.4 12.3 %collective-permute-start.14 = (f32[2,128,128]{2,1,0:T(8,128)S(1)}, f32[2,128,128]{2,1,0:T(8,128)S(1)}, u32[]{:S(2)}, u32[]{:S(2)}) collective-permute-start(f32[2,128,128]{2,1,0:T(8,128)S(1)} %add.31.held_ref), channel_id=1, source_target_pairs={{0,1},{1,0},{2,3},{3,2},{4,5},{5,4},{6,7},{7,6},{8,9},{9,8},{10,11... | collective-permute-start | bytes 393224 | tf_op jit(solution)/shard_map/ppermute | solution.py:28
  46.9 16.5 %collective-permute-start.25 = (f32[2,32,8,128]{3,2,1,0:T(8,128)S(1)}, f32[2,32,8,128]{3,2,1,0:T(8,128)S(1)}, u32[]{:S(2)}, u32[]{:S(2)}) collective-permute-start(f32[2,32,8,128]{3,2,1,0:T(8,128)S(1)} %pad_maximum_fusion.h0_ref), channel_id=1, source_target_pairs={{0,192},{1,193},{2,194},{3,195},{4,196},{5,197},{6,198},{7,199},{8... | collective-permute-start | bytes 786440 | tf_op jit(solution)/shard_map/ppermute | solution.py:28
  49.7 14.0 %collective-permute-start.24 = (f32[2,32,8,128]{3,2,1,0:T(8,128)S(1)}, f32[2,32,8,128]{3,2,1,0:T(8,128)S(1)}, u32[]{:S(2)}, u32[]{:S(2)}) collective-permute-start(f32[2,32,8,128]{3,2,1,0:T(8,128)S(1)} %pad_maximum_fusion.h0_ref), channel_id=1, source_target_pairs={{0,128},{1,129},{2,130},{3,131},{4,132},{5,133},{6,134},{7,135},{8... | collective-permute-start | bytes 786440 | tf_op jit(solution)/shard_map/ppermute | solution.py:28
  50.1 14.0 %collective-permute-start.23 = (f32[2,32,8,128]{3,2,1,0:T(8,128)S(1)}, f32[2,32,8,128]{3,2,1,0:T(8,128)S(1)}, u32[]{:S(2)}, u32[]{:S(2)}) collective-permute-start(f32[2,32,8,128]{3,2,1,0:T(8,128)S(1)} %pad_maximum_fusion.h0_ref), channel_id=1, source_target_pairs={{0,64},{1,65},{2,66},{3,67},{4,68},{5,69},{6,70},{7,71},{8,72},{9,... | collective-permute-start | bytes 786440 | tf_op jit(solution)/shard_map/ppermute | solution.py:28
  50.6 9.4 %collective-permute-start.15 = (f32[8,128,128]{2,1,0:T(8,128)S(1)}, f32[8,128,128]{2,1,0:T(8,128)S(1)}, u32[]{:S(2)}, u32[]{:S(2)}) collective-permute-start(f32[8,128,128]{2,1,0:T(8,128)S(1)} %add.29), channel_id=1, source_target_pairs={{0,2},{1,15},{4,6},{5,3},{8,10},{9,7},{12,14},{13,11},{16,18},{17,... | collective-permute-start | bytes 1572872 | tf_op jit(solution)/shard_map/ppermute | solution.py:28
  60.2 4.1 %collective-permute-start.19 = (f32[2,128,128]{2,1,0:T(8,128)S(1)}, f32[2,128,128]{2,1,0:T(8,128)S(1)}, u32[]{:S(2)}, u32[]{:S(2)}) collective-permute-start(f32[2,128,128]{2,1,0:T(8,128)S(1)} %get-tuple-element.26), channel_id=1, source_target_pairs={{0,1},{1,0},{2,3},{3,2},{4,5},{5,4},{6,7},{7,6},{8,9},{9,8},{10,11... | collective-permute-start | bytes 393224 | tf_op jit(solution)/shard_map/ppermute | solution.py:28
  63.4 1.4 %collective-permute-start.17 = (f32[2,128,128]{2,1,0:T(8,128)S(1)}, f32[2,128,128]{2,1,0:T(8,128)S(1)}, u32[]{:S(2)}, u32[]{:S(2)}) collective-permute-start(f32[2,128,128]{2,1,0:T(8,128)S(1)} %get-tuple-element.28), channel_id=1, source_target_pairs={{0,1},{1,0},{2,3},{3,2},{4,5},{5,4},{6,7},{7,6},{8,9},{9,8},{10,11... | collective-permute-start | bytes 393224 | tf_op jit(solution)/shard_map/ppermute | solution.py:28
  (3 other events, 14.1 us)

commit v5 on v4

--- a/solution.py
+++ b/solution.py
@@ -125,7 +125,7 @@
     return dot(ah, bh) + (dot(ah, bl) + dot(al, bh))
 
 
-def update_kernel(place_ref, x_ref, held_ref, o0_ref, o1_ref, o2_ref, o3_ref, h0_ref, h1_ref, h2_ref, h3_ref, w_ref, o_ref, out_ref, col_ref, sem):
+def update_kernel(place_ref, x_ref, r0_ref, r1_ref, o0_ref, o1_ref, o2_ref, o3_ref, h0_ref, h1_ref, h2_ref, h3_ref, w_ref, o_ref, out_ref, col_ref, sem):
     w = halves(w_ref[...])
     y_place = place_ref[0] // 4
     for n, h in enumerate((h0_ref, h1_ref, h2_ref, h3_ref)):
@@ -136,11 +136,12 @@
         [jnp.concatenate([col_ref[p, :, c, :] for c in range(8)], axis=1) for p in range(2)], axis=0
     )
     first = lax.rem(place_ref[1], 2) == 0
+    held = [ref[n] for ref in (r0_ref, r1_ref) for n in range(4)]
     other = [ref[n] for ref in (o0_ref, o1_ref, o2_ref, o3_ref) for n in range(2)]
     z = halves(product(w, halves(cols)))
     y = [
         halves(product(halves(jnp.concatenate(
-            [jnp.where(first, held_ref[a], other[a]), jnp.where(first, other[a], held_ref[a])], axis=1
+            [jnp.where(first, held[a], other[a]), jnp.where(first, other[a], held[a])], axis=1
         )), w, NT))
         for a in range(8)
     ]
@@ -164,7 +165,7 @@
     vmem = pl.BlockSpec(memory_space=pltpu.VMEM)
     return pl.pallas_call(
         update_kernel,
-        in_specs=[pl.BlockSpec(memory_space=pltpu.SMEM)] + [vmem] * 11,
+        in_specs=[pl.BlockSpec(memory_space=pltpu.SMEM)] + [vmem] * 12,
         out_specs=pl.BlockSpec(memory_space=pl.ANY),
         scratch_shapes=[pltpu.VMEM((8, 128, 8, 128), f32), pltpu.VMEM((2, 128, 8, 128), f32), pltpu.SemaphoreType.DMA((8,))],
         out_shape=jax.ShapeDtypeStruct((8, 128, 8, 128), f32),
@@ -238,11 +239,17 @@
     rows = jnp.where(z == 0, coupling[:, :, 0, :], 0.0)
     pivot = pivot_block(coupling, diagonal, x, core)
     quarters = [coupling[0, 32 * n:32 * n + 32] for n in range(4)]
-    turned = turns([pivot] * 3, along_y)
+    turned = [
+        send(pivot, lambda x, y, z, k: (x, n, z, k) if x < 2 and y == z == 0 else None) for n in (1, 2, 3)
+    ]
     pivot, rows = lax.optimization_barrier((pivot, rows))
     pivot = pick(y, [pivot, *turned])
     cols = pick(y, [quarters[0], *turns(quarters[1:], along_y)])
-    pivots = columns_zero_and_one(pivot, turns([pivot] * 3, along_x), x)
+    turned = [
+        send(pivot, lambda x, y, z, k: ((x + n) & 3, y, z, k) if x < 2 and z == 0 else None)
+        for n in (1, 2, 3)
+    ]
+    pivots = columns_zero_and_one(pivot, turned, x)
     rows = along_z(1, after(rows, pivots))
     pivots = total(along_z(1, jnp.where(z == 0, pivots, 0.0)))
     rows = along_z(2, after(total(rows), pivots))
@@ -251,11 +258,13 @@
     pivots = total(along_z(2, pivots))
     pivots = total(along_z(3, pivots))
     other_pivots = swap(pivots)
-    rows = along_z(3, after(total(rows), pivots))
+    rows = after(total(rows), pivots)
+    rows = [along_z(3, half) for half in (rows[0:4], rows[4:8])]
     cols = [cols, *turns([cols] * 3, along_y)]
     w = factor(place[1:] & 1, pivots, other_pivots)
-    rows = total((after(rows[0], w), rows[1]))
-    return update(place, coupling, (rows, *[swap(rows[2 * n:2 * n + 2]) for n in range(4)]), cols, w)
+    rows = [total((after(held, w), got)) for held, got in rows]
+    others = [swap(half[2 * n:2 * n + 2]) for half in rows for n in range(2)]
+    return update(place, coupling, (*rows, *others), cols, w)
 
 
 def solution(mesh):

time: 72 us -> 68.4 us (0.950)
  starting transfers between devices: 40.4 us -> 37.6 us
    ppermute x26 -> x27, starting transfers between devices: 40.4 us -> 37.6 us  [send(): return lax.ppermute(value, AXES, pairs)]
    ppermute x26 -> x27, waiting for transfers between devices: 11.4 us -> 11 us  [send(): return lax.ppermute(value, AXES, pairs)]
  transfers between devices with their start and end apart: 26 -> 27, of which waited for: 12 -> 8; matrix products, arithmetic and copies ran while one was open for 7% -> 7% of each run, Pallas kernels for 9% -> 9%
where the time goes in v5:
time: 68.4 us; the launch traced here: 67.8 us
  starting transfers between devices  37.6 us (55%)
  Pallas kernels  11.8 us (17%)
  waiting for transfers between devices  11 us (16%)
  local copies, waits for them, and re-layouts  5.4 us (8%)
  other arithmetic  1.43 us (2%)
    ppermute x27, starting transfers between devices, send(): return lax.ppermute(value, AXES, pairs)  37.6 us
    ppermute x27, waiting for transfers between devices, send(): return lax.ppermute(value, AXES, pairs)  11 us
    pallas_call x1, Pallas kernels, factor(): pl.pallas_call(factor_kernel, in_specs=[pl.BlockSpec(memory_space=pltpu.S...  6.28 us
    pallas_call x1, Pallas kernels, update(): pl.pallas_call(update_kernel, in_specs=[pl.BlockSpec(memory_space=pltpu.S...  5.56 us
    slice x1, local copies, waits for them, and re-layouts, on_device(): rows = jnp.where(z == 0, coupling[:, :, 0, :], 0.0)  2.49 us
  transfers between devices with their start and end apart: 27, of which 8 were waited for; matrix products, arithmetic and copies ran while one was open for 7% of the time, Pallas kernels for 9%

profile of v5, /device:TPU:1, one launch (start us, length us, event | category | flops | bytes accessed | tf_op | source)
XLA Modules:
  0.0 67.8 jit_solution(14399584521354960262)
XLA Ops:
  1.8 5.5 %collective-permute-start.2 = (f32[128,128]{1,0:T(8,128)S(1)}, f32[128,128]{1,0:T(8,128)S(1)}, u32[]{:S(2)}, u32[]{:S(2)}) collective-permute-start(f32[128,128]{1,0:T(8,128)S(1)} %select_add_fusion), channel_id=1, source_target_pairs={{0,192},{1,193},{16,208},{17,209}} | collective-permute-start | bytes 196616 | tf_op jit(solution)/shard_map/ppermute | solution.py:28
  7.3 1.3 %collective-permute-start.1 = (f32[128,128]{1,0:T(8,128)S(1)}, f32[128,128]{1,0:T(8,128)S(1)}, u32[]{:S(2)}, u32[]{:S(2)}) collective-permute-start(f32[128,128]{1,0:T(8,128)S(1)} %select_add_fusion), channel_id=1, source_target_pairs={{0,128},{1,129},{16,144},{17,145}} | collective-permute-start | bytes 196616 | tf_op jit(solution)/shard_map/ppermute | solution.py:28
  8.6 1.3 %collective-permute-start = (f32[128,128]{1,0:T(8,128)S(1)}, f32[128,128]{1,0:T(8,128)S(1)}, u32[]{:S(2)}, u32[]{:S(2)}) collective-permute-start(f32[128,128]{1,0:T(8,128)S(1)} %select_add_fusion), channel_id=1, source_target_pairs={{0,64},{1,65},{16,80},{17,81}} | collective-permute-start | bytes 196616 | tf_op jit(solution)/shard_map/ppermute | solution.py:28
  9.9 2.5 %slice.41 = f32[8,128,1,128]{3,2,1,0:T(1,128)S(1)} slice(f32[8,128,8,128]{3,2,1,0:T(8,128)} %x_ref.1), slice={[0:8], [0:128], [0:1], [0:128]} | slice | bytes 1048576 | tf_op jit(solution)/shard_map/slice | solution.py:239
  12.5 1.9 %collective-permute-start.5 = (f32[128,128]{1,0:T(8,128)S(1)}, f32[128,128]{1,0:T(8,128)S(1)}, u32[]{:S(2)}, u32[]{:S(2)}) collective-permute-start(f32[128,128]{1,0:T(8,128)S(1)} %select_select_fusion), channel_id=1, source_target_pairs={{0,48},{1,49},{16,0},{17,1},{64,112},{65,113},{80,64},{81,65},{128... | collective-permute-start | bytes 196616 | tf_op jit(solution)/shard_map/ppermute | solution.py:28
  14.4 1.3 %collective-permute-start.4 = (f32[128,128]{1,0:T(8,128)S(1)}, f32[128,128]{1,0:T(8,128)S(1)}, u32[]{:S(2)}, u32[]{:S(2)}) collective-permute-start(f32[128,128]{1,0:T(8,128)S(1)} %select_select_fusion), channel_id=1, source_target_pairs={{0,32},{1,33},{16,48},{17,49},{64,96},{65,97},{80,112},{81,113},{1... | collective-permute-start | bytes 196616 | tf_op jit(solution)/shard_map/ppermute | solution.py:28
  15.7 3.4 %collective-permute-start.3 = (f32[128,128]{1,0:T(8,128)S(1)}, f32[128,128]{1,0:T(8,128)S(1)}, u32[]{:S(2)}, u32[]{:S(2)}) collective-permute-start(f32[128,128]{1,0:T(8,128)S(1)} %select_select_fusion), channel_id=1, source_target_pairs={{0,16},{1,17},{16,32},{17,33},{64,80},{65,81},{80,96},{81,97},{128... | collective-permute-start | bytes 196616 | tf_op jit(solution)/shard_map/ppermute | solution.py:28
  19.1 1.3 %collective-permute-start.6 = (f32[8,128,128]{2,1,0:T(8,128)S(1)}, f32[8,128,128]{2,1,0:T(8,128)S(1)}, u32[]{:S(2)}, u32[]{:S(2)}) collective-permute-start(f32[8,128,128]{2,1,0:T(8,128)S(1)} %select_bitcast_fusion), channel_id=1, source_target_pairs={{0,4},{1,13},{16,20},{17,29},{32,36},{33,45},{48,52},{49,61},{64,6... | collective-permute-start | bytes 1572872 | tf_op jit(solution)/shard_map/ppermute | solution.py:28
  20.5 1.3 %collective-permute-start.7 = (f32[2,128,128]{2,1,0:T(8,128)S(1)}, f32[2,128,128]{2,1,0:T(8,128)S(1)}, u32[]{:S(2)}, u32[]{:S(2)}) collective-permute-start(f32[2,128,128]{2,1,0:T(8,128)S(1)} %broadcast_select_fusion), channel_id=1, source_target_pairs={{0,4},{1,13},{16,20},{17,29},{32,36},{33,45},{48,52},{49,61},{64,6... | collective-permute-start | bytes 393224 | tf_op jit(solution)/shard_map/ppermute | solution.py:28
  23.0 3.2 %collective-permute-start.10 = (f32[32,8,128]{2,1,0:T(8,128)S(1)}, f32[32,8,128]{2,1,0:T(8,128)S(1)}, u32[]{:S(2)}, u32[]{:S(2)}) collective-permute-start(f32[32,8,128]{2,1,0:T(8,128)S(1)} %get-tuple-element.24), channel_id=1, source_target_pairs={{0,128},{1,129},{2,130},{3,131},{4,132},{5,133},{6,134},{7,135},{8... | collective-permute-start | bytes 393224 | tf_op jit(solution)/shard_map/ppermute | solution.py:28
  26.2 1.7 %collective-permute-done.7 = f32[2,128,128]{2,1,0:T(8,128)S(1)} collective-permute-done((f32[2,128,128]{2,1,0:T(8,128)S(1)}, f32[2,128,128]{2,1,0:T(8,128)S(1)}, u32[]{:S(2)}, u32[]{:S(2)}) %collective-permute-start.7) | collective-permute-done | bytes 131104 | tf_op jit(solution)/shard_map/ppermute | solution.py:28
  28.0 1.3 %collective-permute-start.8 = (f32[8,128,128]{2,1,0:T(8,128)S(1)}, f32[8,128,128]{2,1,0:T(8,128)S(1)}, u32[]{:S(2)}, u32[]{:S(2)}) collective-permute-start(f32[8,128,128]{2,1,0:T(8,128)S(1)} %add.30), channel_id=1, source_target_pairs={{0,12},{1,5},{4,8},{13,9},{16,28},{17,21},{20,24},{29,25},{32,44},... | collective-permute-start | bytes 1572872 | tf_op jit(solution)/shard_map/ppermute | solution.py:28
  29.4 3.2 %collective-permute-done.9 = f32[32,8,128]{2,1,0:T(8,128)S(1)} collective-permute-done((f32[32,8,128]{2,1,0:T(8,128)S(1)}, f32[32,8,128]{2,1,0:T(8,128)S(1)}, u32[]{:S(2)}, u32[]{:S(2)}) %collective-permute-start.9) | collective-permute-done | bytes 131104 | tf_op jit(solution)/shard_map/ppermute | solution.py:28
  33.5 1.3 %collective-permute-start.12 = (f32[2,128,128]{2,1,0:T(8,128)S(1)}, f32[2,128,128]{2,1,0:T(8,128)S(1)}, u32[]{:S(2)}, u32[]{:S(2)}) collective-permute-start(f32[2,128,128]{2,1,0:T(8,128)S(1)} %fusion.4), channel_id=1, source_target_pairs={{0,12},{1,5},{4,8},{13,9},{16,28},{17,21},{20,24},{29,25},{32,44},... | collective-permute-start | bytes 393224 | tf_op jit(solution)/shard_map/ppermute | solution.py:28
  35.9 2.5 %collective-permute-start.22 = (f32[32,8,128]{2,1,0:T(8,128)S(1)}, f32[32,8,128]{2,1,0:T(8,128)S(1)}, u32[]{:S(2)}, u32[]{:S(2)}) collective-permute-start(f32[32,8,128]{2,1,0:T(8,128)S(1)} %bitcast_select_fusion), channel_id=1, source_target_pairs={{0,32},{1,33},{2,34},{3,35},{4,36},{5,37},{6,38},{7,39},{8,40},{9,... | collective-permute-start | bytes 393224 | tf_op jit(solution)/shard_map/ppermute | solution.py:28
  38.5 1.3 %collective-permute-start.13 = (f32[2,128,128]{2,1,0:T(8,128)S(1)}, f32[2,128,128]{2,1,0:T(8,128)S(1)}, u32[]{:S(2)}, u32[]{:S(2)}) collective-permute-start(f32[2,128,128]{2,1,0:T(8,128)S(1)} %add.33), channel_id=1, source_target_pairs={{0,2},{1,15},{4,6},{5,3},{8,10},{9,7},{12,14},{13,11},{16,18},{17,... | collective-permute-start | bytes 393224 | tf_op jit(solution)/shard_map/ppermute | solution.py:28
  39.8 1.5 %collective-permute-done.22 = f32[32,8,128]{2,1,0:T(8,128)S(1)} collective-permute-done((f32[32,8,128]{2,1,0:T(8,128)S(1)}, f32[32,8,128]{2,1,0:T(8,128)S(1)}, u32[]{:S(2)}, u32[]{:S(2)}) %collective-permute-start.22) | collective-permute-done | bytes 131104 | tf_op jit(solution)/shard_map/ppermute | solution.py:28
  41.3 3.6 %collective-permute-done.21 = f32[32,8,128]{2,1,0:T(8,128)S(1)} collective-permute-done((f32[32,8,128]{2,1,0:T(8,128)S(1)}, f32[32,8,128]{2,1,0:T(8,128)S(1)}, u32[]{:S(2)}, u32[]{:S(2)}) %collective-permute-start.21) | collective-permute-done | bytes 131104 | tf_op jit(solution)/shard_map/ppermute | solution.py:28
  45.1 1.4 %collective-permute-start.24 = (f32[2,32,8,128]{3,2,1,0:T(8,128)S(1)}, f32[2,32,8,128]{3,2,1,0:T(8,128)S(1)}, u32[]{:S(2)}, u32[]{:S(2)}) collective-permute-start(f32[2,32,8,128]{3,2,1,0:T(8,128)S(1)} %pad_maximum_fusion.h0_ref), channel_id=1, source_target_pairs={{0,64},{1,65},{2,66},{3,67},{4,68},{5,69},{6,70},{7,71},{8,72},{9,... | collective-permute-start | bytes 786440 | tf_op jit(solution)/shard_map/ppermute | solution.py:28
  46.5 3.9 %collective-permute-start.14 = (f32[2,128,128]{2,1,0:T(8,128)S(1)}, f32[2,128,128]{2,1,0:T(8,128)S(1)}, u32[]{:S(2)}, u32[]{:S(2)}) collective-permute-start(f32[2,128,128]{2,1,0:T(8,128)S(1)} %add.34.held_ref), channel_id=1, source_target_pairs={{0,1},{1,0},{2,3},{3,2},{4,5},{5,4},{6,7},{7,6},{8,9},{9,8},{10,11... | collective-permute-start | bytes 393224 | tf_op jit(solution)/shard_map/ppermute | solution.py:28
  50.5 1.3 %collective-permute-start.16 = (f32[4,128,128]{2,1,0:T(8,128)S(1)}, f32[4,128,128]{2,1,0:T(8,128)S(1)}, u32[]{:S(2)}, u32[]{:S(2)}) collective-permute-start(f32[4,128,128]{2,1,0:T(8,128)S(1)} %get-tuple-element.21), channel_id=1, source_target_pairs={{0,2},{1,15},{4,6},{5,3},{8,10},{9,7},{12,14},{13,11},{16,18},{17,... | collective-permute-start | bytes 786440 | tf_op jit(solution)/shard_map/ppermute | solution.py:28
  51.9 1.5 %collective-permute-start.15 = (f32[4,128,128]{2,1,0:T(8,128)S(1)}, f32[4,128,128]{2,1,0:T(8,128)S(1)}, u32[]{:S(2)}, u32[]{:S(2)}) collective-permute-start(f32[4,128,128]{2,1,0:T(8,128)S(1)} %get-tuple-element.20), channel_id=1, source_target_pairs={{0,2},{1,15},{4,6},{5,3},{8,10},{9,7},{12,14},{13,11},{16,18},{17,... | collective-permute-start | bytes 786440 | tf_op jit(solution)/shard_map/ppermute | solution.py:28
  53.4 6.3 %shard_map.28.w_ref = f32[256,256]{1,0:T(8,128)S(1)} custom-call(s32[1]{0:T(128)S(6)} %and.26.core_ref, f32[2,128,128]{2,1,0:T(8,128)S(1)} %add.34.held_ref, f32[2,128,128]{2,1,0:T(8,128)S(1)} %collective-permute-done.14.other_ref), custom_call_target="tpu_custom_call" | custom-call | flops 12000000000 | bytes 500000 | tf_op jit(solution)/shard_map/pallas_call | solution.py:107
  62.0 5.6 %shard_map.29 = f32[8,128,8,128]{3,2,1,0:T(8,128)} custom-call(s32[2]{0:T(128)S(1)} %pad_add_fusion.place_ref, f32[8,128,8,128]{3,2,1,0:T(8,128)S(1)} %copy-done, f32[4,128,128]{2,1,0:T(8,128)S(1)} %add.35.r0_ref, f32[4,128,128]{2,1,0:T(8,128)S(1)} %add.36.r1_ref, f32[2,128,128]{2,1,0:T(8,128)S(1)} %collective-permute-done.17.o0_ref, ...), custom_call_target="tpu_custom_call" | custom-call | flops 1610612736 | bytes 8388608 | tf_op jit(solution)/shard_map/pallas_call | solution.py:166
  (57 shorter events, 8.0 us)
Async XLA Ops:
  1.8 10.6 %collective-permute-start.2 = (f32[128,128]{1,0:T(8,128)S(1)}, f32[128,128]{1,0:T(8,128)S(1)}, u32[]{:S(2)}, u32[]{:S(2)}) collective-permute-start(f32[128,128]{1,0:T(8,128)S(1)} %select_add_fusion), channel_id=1, source_target_pairs={{0,192},{1,193},{16,208},{17,209}} | collective-permute-start | bytes 196616 | tf_op jit(solution)/shard_map/ppermute | solution.py:28
  7.3 5.2 %collective-permute-start.1 = (f32[128,128]{1,0:T(8,128)S(1)}, f32[128,128]{1,0:T(8,128)S(1)}, u32[]{:S(2)}, u32[]{:S(2)}) collective-permute-start(f32[128,128]{1,0:T(8,128)S(1)} %select_add_fusion), channel_id=1, source_target_pairs={{0,128},{1,129},{16,144},{17,145}} | collective-permute-start | bytes 196616 | tf_op jit(solution)/shard_map/ppermute | solution.py:28
  8.6 3.9 %collective-permute-start = (f32[128,128]{1,0:T(8,128)S(1)}, f32[128,128]{1,0:T(8,128)S(1)}, u32[]{:S(2)}, u32[]{:S(2)}) collective-permute-start(f32[128,128]{1,0:T(8,128)S(1)} %select_add_fusion), channel_id=1, source_target_pairs={{0,64},{1,65},{16,80},{17,81}} | collective-permute-start | bytes 196616 | tf_op jit(solution)/shard_map/ppermute | solution.py:28
  12.5 7.9 %collective-permute-start.5 = (f32[128,128]{1,0:T(8,128)S(1)}, f32[128,128]{1,0:T(8,128)S(1)}, u32[]{:S(2)}, u32[]{:S(2)}) collective-permute-start(f32[128,128]{1,0:T(8,128)S(1)} %select_select_fusion), channel_id=1, source_target_pairs={{0,48},{1,49},{16,0},{17,1},{64,112},{65,113},{80,64},{81,65},{128... | collective-permute-start | bytes 196616 | tf_op jit(solution)/shard_map/ppermute | solution.py:28
  14.4 6.0 %collective-permute-start.4 = (f32[128,128]{1,0:T(8,128)S(1)}, f32[128,128]{1,0:T(8,128)S(1)}, u32[]{:S(2)}, u32[]{:S(2)}) collective-permute-start(f32[128,128]{1,0:T(8,128)S(1)} %select_select_fusion), channel_id=1, source_target_pairs={{0,32},{1,33},{16,48},{17,49},{64,96},{65,97},{80,112},{81,113},{1... | collective-permute-start | bytes 196616 | tf_op jit(solution)/shard_map/ppermute | solution.py:28
  15.7 4.7 %collective-permute-start.3 = (f32[128,128]{1,0:T(8,128)S(1)}, f32[128,128]{1,0:T(8,128)S(1)}, u32[]{:S(2)}, u32[]{:S(2)}) collective-permute-start(f32[128,128]{1,0:T(8,128)S(1)} %select_select_fusion), channel_id=1, source_target_pairs={{0,16},{1,17},{16,32},{17,33},{64,80},{65,81},{80,96},{81,97},{128... | collective-permute-start | bytes 196616 | tf_op jit(solution)/shard_map/ppermute | solution.py:28
  19.1 8.8 %collective-permute-start.6 = (f32[8,128,128]{2,1,0:T(8,128)S(1)}, f32[8,128,128]{2,1,0:T(8,128)S(1)}, u32[]{:S(2)}, u32[]{:S(2)}) collective-permute-start(f32[8,128,128]{2,1,0:T(8,128)S(1)} %select_bitcast_fusion), channel_id=1, source_target_pairs={{0,4},{1,13},{16,20},{17,29},{32,36},{33,45},{48,52},{49,61},{64,6... | collective-permute-start | bytes 1572872 | tf_op jit(solution)/shard_map/ppermute | solution.py:28
  20.5 7.4 %collective-permute-start.7 = (f32[2,128,128]{2,1,0:T(8,128)S(1)}, f32[2,128,128]{2,1,0:T(8,128)S(1)}, u32[]{:S(2)}, u32[]{:S(2)}) collective-permute-start(f32[2,128,128]{2,1,0:T(8,128)S(1)} %broadcast_select_fusion), channel_id=1, source_target_pairs={{0,4},{1,13},{16,20},{17,29},{32,36},{33,45},{48,52},{49,61},{64,6... | collective-permute-start | bytes 393224 | tf_op jit(solution)/shard_map/ppermute | solution.py:28
  22.9 6.4 %collective-permute-start.11 = (f32[32,8,128]{2,1,0:T(8,128)S(1)}, f32[32,8,128]{2,1,0:T(8,128)S(1)}, u32[]{:S(2)}, u32[]{:S(2)}) collective-permute-start(f32[32,8,128]{2,1,0:T(8,128)S(1)} %get-tuple-element.23), channel_id=1, source_target_pairs={{0,192},{1,193},{2,194},{3,195},{4,196},{5,197},{6,198},{7,199},{8... | collective-permute-start | bytes 393224 | tf_op jit(solution)/shard_map/ppermute | solution.py:28
  23.0 6.4 %collective-permute-start.10 = (f32[32,8,128]{2,1,0:T(8,128)S(1)}, f32[32,8,128]{2,1,0:T(8,128)S(1)}, u32[]{:S(2)}, u32[]{:S(2)}) collective-permute-start(f32[32,8,128]{2,1,0:T(8,128)S(1)} %get-tuple-element.24), channel_id=1, source_target_pairs={{0,128},{1,129},{2,130},{3,131},{4,132},{5,133},{6,134},{7,135},{8... | collective-permute-start | bytes 393224 | tf_op jit(solution)/shard_map/ppermute | solution.py:28
  26.2 6.3 %collective-permute-start.9 = (f32[32,8,128]{2,1,0:T(8,128)S(1)}, f32[32,8,128]{2,1,0:T(8,128)S(1)}, u32[]{:S(2)}, u32[]{:S(2)}) collective-permute-start(f32[32,8,128]{2,1,0:T(8,128)S(1)} %get-tuple-element.25), channel_id=1, source_target_pairs={{0,64},{1,65},{2,66},{3,67},{4,68},{5,69},{6,70},{7,71},{8,72},{9,... | collective-permute-start | bytes 393224 | tf_op jit(solution)/shard_map/ppermute | solution.py:28
  28.0 22.4 %collective-permute-start.8 = (f32[8,128,128]{2,1,0:T(8,128)S(1)}, f32[8,128,128]{2,1,0:T(8,128)S(1)}, u32[]{:S(2)}, u32[]{:S(2)}) collective-permute-start(f32[8,128,128]{2,1,0:T(8,128)S(1)} %add.30), channel_id=1, source_target_pairs={{0,12},{1,5},{4,8},{13,9},{16,28},{17,21},{20,24},{29,25},{32,44},... | collective-permute-start | bytes 1572872 | tf_op jit(solution)/shard_map/ppermute | solution.py:28
  33.5 5.0 %collective-permute-start.12 = (f32[2,128,128]{2,1,0:T(8,128)S(1)}, f32[2,128,128]{2,1,0:T(8,128)S(1)}, u32[]{:S(2)}, u32[]{:S(2)}) collective-permute-start(f32[2,128,128]{2,1,0:T(8,128)S(1)} %fusion.4), channel_id=1, source_target_pairs={{0,12},{1,5},{4,8},{13,9},{16,28},{17,21},{20,24},{29,25},{32,44},... | collective-permute-start | bytes 393224 | tf_op jit(solution)/shard_map/ppermute | solution.py:28
  34.8 5.0 %collective-permute-start.23 = (f32[32,8,128]{2,1,0:T(8,128)S(1)}, f32[32,8,128]{2,1,0:T(8,128)S(1)}, u32[]{:S(2)}, u32[]{:S(2)}) collective-permute-start(f32[32,8,128]{2,1,0:T(8,128)S(1)} %bitcast_select_fusion), channel_id=1, source_target_pairs={{0,48},{1,49},{2,50},{3,51},{4,52},{5,53},{6,54},{7,55},{8,56},{9,... | collective-permute-start | bytes 393224 | tf_op jit(solution)/shard_map/ppermute | solution.py:28
  35.9 5.3 %collective-permute-start.22 = (f32[32,8,128]{2,1,0:T(8,128)S(1)}, f32[32,8,128]{2,1,0:T(8,128)S(1)}, u32[]{:S(2)}, u32[]{:S(2)}) collective-permute-start(f32[32,8,128]{2,1,0:T(8,128)S(1)} %bitcast_select_fusion), channel_id=1, source_target_pairs={{0,32},{1,33},{2,34},{3,35},{4,36},{5,37},{6,38},{7,39},{8,40},{9,... | collective-permute-start | bytes 393224 | tf_op jit(solution)/shard_map/ppermute | solution.py:28
  38.4 6.4 %collective-permute-start.21 = (f32[32,8,128]{2,1,0:T(8,128)S(1)}, f32[32,8,128]{2,1,0:T(8,128)S(1)}, u32[]{:S(2)}, u32[]{:S(2)}) collective-permute-start(f32[32,8,128]{2,1,0:T(8,128)S(1)} %bitcast_select_fusion), channel_id=1, source_target_pairs={{0,16},{1,17},{2,18},{3,19},{4,20},{5,21},{6,22},{7,23},{8,24},{9,... | collective-permute-start | bytes 393224 | tf_op jit(solution)/shard_map/ppermute | solution.py:28
  38.5 8.0 %collective-permute-start.13 = (f32[2,128,128]{2,1,0:T(8,128)S(1)}, f32[2,128,128]{2,1,0:T(8,128)S(1)}, u32[]{:S(2)}, u32[]{:S(2)}) collective-permute-start(f32[2,128,128]{2,1,0:T(8,128)S(1)} %add.33), channel_id=1, source_target_pairs={{0,2},{1,15},{4,6},{5,3},{8,10},{9,7},{12,14},{13,11},{16,18},{17,... | collective-permute-start | bytes 393224 | tf_op jit(solution)/shard_map/ppermute | solution.py:28
  44.9 15.5 %collective-permute-start.26 = (f32[2,32,8,128]{3,2,1,0:T(8,128)S(1)}, f32[2,32,8,128]{3,2,1,0:T(8,128)S(1)}, u32[]{:S(2)}, u32[]{:S(2)}) collective-permute-start(f32[2,32,8,128]{3,2,1,0:T(8,128)S(1)} %pad_maximum_fusion.h0_ref), channel_id=1, source_target_pairs={{0,192},{1,193},{2,194},{3,195},{4,196},{5,197},{6,198},{7,199},{8... | collective-permute-start | bytes 786440 | tf_op jit(solution)/shard_map/ppermute | solution.py:28
  45.0 15.6 %collective-permute-start.25 = (f32[2,32,8,128]{3,2,1,0:T(8,128)S(1)}, f32[2,32,8,128]{3,2,1,0:T(8,128)S(1)}, u32[]{:S(2)}, u32[]{:S(2)}) collective-permute-start(f32[2,32,8,128]{3,2,1,0:T(8,128)S(1)} %pad_maximum_fusion.h0_ref), channel_id=1, source_target_pairs={{0,128},{1,129},{2,130},{3,131},{4,132},{5,133},{6,134},{7,135},{8... | collective-permute-start | bytes 786440 | tf_op jit(solution)/shard_map/ppermute | solution.py:28
  45.1 16.0 %collective-permute-start.24 = (f32[2,32,8,128]{3,2,1,0:T(8,128)S(1)}, f32[2,32,8,128]{3,2,1,0:T(8,128)S(1)}, u32[]{:S(2)}, u32[]{:S(2)}) collective-permute-start(f32[2,32,8,128]{3,2,1,0:T(8,128)S(1)} %pad_maximum_fusion.h0_ref), channel_id=1, source_target_pairs={{0,64},{1,65},{2,66},{3,67},{4,68},{5,69},{6,70},{7,71},{8,72},{9,... | collective-permute-start | bytes 786440 | tf_op jit(solution)/shard_map/ppermute | solution.py:28
  46.5 5.4 %collective-permute-start.14 = (f32[2,128,128]{2,1,0:T(8,128)S(1)}, f32[2,128,128]{2,1,0:T(8,128)S(1)}, u32[]{:S(2)}, u32[]{:S(2)}) collective-permute-start(f32[2,128,128]{2,1,0:T(8,128)S(1)} %add.34.held_ref), channel_id=1, source_target_pairs={{0,1},{1,0},{2,3},{3,2},{4,5},{5,4},{6,7},{7,6},{8,9},{9,8},{10,11... | collective-permute-start | bytes 393224 | tf_op jit(solution)/shard_map/ppermute | solution.py:28
  50.5 9.1 %collective-permute-start.16 = (f32[4,128,128]{2,1,0:T(8,128)S(1)}, f32[4,128,128]{2,1,0:T(8,128)S(1)}, u32[]{:S(2)}, u32[]{:S(2)}) collective-permute-start(f32[4,128,128]{2,1,0:T(8,128)S(1)} %get-tuple-element.21), channel_id=1, source_target_pairs={{0,2},{1,15},{4,6},{5,3},{8,10},{9,7},{12,14},{13,11},{16,18},{17,... | collective-permute-start | bytes 786440 | tf_op jit(solution)/shard_map/ppermute | solution.py:28
  51.9 8.0 %collective-permute-start.15 = (f32[4,128,128]{2,1,0:T(8,128)S(1)}, f32[4,128,128]{2,1,0:T(8,128)S(1)}, u32[]{:S(2)}, u32[]{:S(2)}) collective-permute-start(f32[4,128,128]{2,1,0:T(8,128)S(1)} %get-tuple-element.20), channel_id=1, source_target_pairs={{0,2},{1,15},{4,6},{5,3},{8,10},{9,7},{12,14},{13,11},{16,18},{17,... | collective-permute-start | bytes 786440 | tf_op jit(solution)/shard_map/ppermute | solution.py:28
  59.9 1.5 %collective-permute-start.19 = (f32[2,128,128]{2,1,0:T(8,128)S(1)}, f32[2,128,128]{2,1,0:T(8,128)S(1)}, u32[]{:S(2)}, u32[]{:S(2)}) collective-permute-start(f32[2,128,128]{2,1,0:T(8,128)S(1)} %get-tuple-element.31), channel_id=1, source_target_pairs={{0,1},{1,0},{2,3},{3,2},{4,5},{5,4},{6,7},{7,6},{8,9},{9,8},{10,11... | collective-permute-start | bytes 393224 | tf_op jit(solution)/shard_map/ppermute | solution.py:28
  (4 other events, 13.0 us)

commit v6 on v5

--- a/solution.py
+++ b/solution.py
@@ -125,7 +125,7 @@
     return dot(ah, bh) + (dot(ah, bl) + dot(al, bh))
 
 
-def update_kernel(place_ref, x_ref, r0_ref, r1_ref, o0_ref, o1_ref, o2_ref, o3_ref, h0_ref, h1_ref, h2_ref, h3_ref, w_ref, o_ref, out_ref, col_ref, sem):
+def update_kernel(place_ref, x_ref, r0_ref, r1_ref, o0_ref, o1_ref, h0_ref, h1_ref, h2_ref, h3_ref, w_ref, o_ref, out_ref, col_ref, sem):
     w = halves(w_ref[...])
     y_place = place_ref[0] // 4
     for n, h in enumerate((h0_ref, h1_ref, h2_ref, h3_ref)):
@@ -137,7 +137,7 @@
     )
     first = lax.rem(place_ref[1], 2) == 0
     held = [ref[n] for ref in (r0_ref, r1_ref) for n in range(4)]
-    other = [ref[n] for ref in (o0_ref, o1_ref, o2_ref, o3_ref) for n in range(2)]
+    other = [ref[n] for ref in (o0_ref, o1_ref) for n in range(4)]
     z = halves(product(w, halves(cols)))
     y = [
         halves(product(halves(jnp.concatenate(
@@ -165,7 +165,7 @@
     vmem = pl.BlockSpec(memory_space=pltpu.VMEM)
     return pl.pallas_call(
         update_kernel,
-        in_specs=[pl.BlockSpec(memory_space=pltpu.SMEM)] + [vmem] * 12,
+        in_specs=[pl.BlockSpec(memory_space=pltpu.SMEM)] + [vmem] * 10,
         out_specs=pl.BlockSpec(memory_space=pl.ANY),
         scratch_shapes=[pltpu.VMEM((8, 128, 8, 128), f32), pltpu.VMEM((2, 128, 8, 128), f32), pltpu.SemaphoreType.DMA((8,))],
         out_shape=jax.ShapeDtypeStruct((8, 128, 8, 128), f32),
@@ -263,7 +263,7 @@
     cols = [cols, *turns([cols] * 3, along_y)]
     w = factor(place[1:] & 1, pivots, other_pivots)
     rows = [total((after(held, w), got)) for held, got in rows]
-    others = [swap(half[2 * n:2 * n + 2]) for half in rows for n in range(2)]
+    others = [swap(half) for half in rows]
     return update(place, coupling, (*rows, *others), cols, w)
 
 

time: 68.4 us -> 68.1 us (level)
    ppermute x27 -> x25, starting transfers between devices: 37.6 us -> 37 us  [send(): return lax.ppermute(value, AXES, pairs)]
    ppermute x27 -> x25, waiting for transfers between devices: 11 us -> 11.2 us  [send(): return lax.ppermute(value, AXES, pairs)]
  transfers between devices with their start and end apart: 27 -> 25, of which waited for: 8 -> 6; matrix products, arithmetic and copies ran while one was open for 7% -> 7% of each run, Pallas kernels for 9% -> 9%
where the time goes in v6:
time: 68.1 us; the launch traced here: 67.5 us
  starting transfers between devices  37 us (54%)
  Pallas kernels  11.8 us (17%)
  waiting for transfers between devices  11.2 us (16%)
  local copies, waits for them, and re-layouts  5.36 us (8%)
  other arithmetic  1.45 us (2%)
    ppermute x25, starting transfers between devices, send(): return lax.ppermute(value, AXES, pairs)  37 us
    ppermute x25, waiting for transfers between devices, send(): return lax.ppermute(value, AXES, pairs)  11.2 us
    pallas_call x1, Pallas kernels, factor(): pl.pallas_call(factor_kernel, in_specs=[pl.BlockSpec(memory_space=pltpu.S...  6.27 us
    pallas_call x1, Pallas kernels, update(): pl.pallas_call(update_kernel, in_specs=[pl.BlockSpec(memory_space=pltpu.S...  5.55 us
    slice x1, local copies, waits for them, and re-layouts, on_device(): rows = jnp.where(z == 0, coupling[:, :, 0, :], 0.0)  2.49 us
  transfers between devices with their start and end apart: 25, of which 6 were waited for; matrix products, arithmetic and copies ran while one was open for 7% of the time, Pallas kernels for 9%

profile of v6, /device:TPU:1, one launch (start us, length us, event | category | flops | bytes accessed | tf_op | source)
XLA Modules:
  0.0 67.5 jit_solution(5723024345845598248)
XLA Ops:
  1.8 5.5 %collective-permute-start.2 = (f32[128,128]{1,0:T(8,128)S(1)}, f32[128,128]{1,0:T(8,128)S(1)}, u32[]{:S(2)}, u32[]{:S(2)}) collective-permute-start(f32[128,128]{1,0:T(8,128)S(1)} %select_add_fusion), channel_id=1, source_target_pairs={{0,192},{1,193},{16,208},{17,209}} | collective-permute-start | bytes 196616 | tf_op jit(solution)/shard_map/ppermute | solution.py:28
  7.3 1.3 %collective-permute-start.1 = (f32[128,128]{1,0:T(8,128)S(1)}, f32[128,128]{1,0:T(8,128)S(1)}, u32[]{:S(2)}, u32[]{:S(2)}) collective-permute-start(f32[128,128]{1,0:T(8,128)S(1)} %select_add_fusion), channel_id=1, source_target_pairs={{0,128},{1,129},{16,144},{17,145}} | collective-permute-start | bytes 196616 | tf_op jit(solution)/shard_map/ppermute | solution.py:28
  8.6 1.3 %collective-permute-start = (f32[128,128]{1,0:T(8,128)S(1)}, f32[128,128]{1,0:T(8,128)S(1)}, u32[]{:S(2)}, u32[]{:S(2)}) collective-permute-start(f32[128,128]{1,0:T(8,128)S(1)} %select_add_fusion), channel_id=1, source_target_pairs={{0,64},{1,65},{16,80},{17,81}} | collective-permute-start | bytes 196616 | tf_op jit(solution)/shard_map/ppermute | solution.py:28
  9.9 2.5 %slice.29 = f32[8,128,1,128]{3,2,1,0:T(1,128)S(1)} slice(f32[8,128,8,128]{3,2,1,0:T(8,128)} %x_ref.1), slice={[0:8], [0:128], [0:1], [0:128]} | slice | bytes 1048576 | tf_op jit(solution)/shard_map/slice | solution.py:239
  12.5 1.9 %collective-permute-start.5 = (f32[128,128]{1,0:T(8,128)S(1)}, f32[128,128]{1,0:T(8,128)S(1)}, u32[]{:S(2)}, u32[]{:S(2)}) collective-permute-start(f32[128,128]{1,0:T(8,128)S(1)} %select_select_fusion), channel_id=1, source_target_pairs={{0,48},{1,49},{16,0},{17,1},{64,112},{65,113},{80,64},{81,65},{128... | collective-permute-start | bytes 196616 | tf_op jit(solution)/shard_map/ppermute | solution.py:28
  14.4 1.3 %collective-permute-start.4 = (f32[128,128]{1,0:T(8,128)S(1)}, f32[128,128]{1,0:T(8,128)S(1)}, u32[]{:S(2)}, u32[]{:S(2)}) collective-permute-start(f32[128,128]{1,0:T(8,128)S(1)} %select_select_fusion), channel_id=1, source_target_pairs={{0,32},{1,33},{16,48},{17,49},{64,96},{65,97},{80,112},{81,113},{1... | collective-permute-start | bytes 196616 | tf_op jit(solution)/shard_map/ppermute | solution.py:28
  15.7 3.4 %collective-permute-start.3 = (f32[128,128]{1,0:T(8,128)S(1)}, f32[128,128]{1,0:T(8,128)S(1)}, u32[]{:S(2)}, u32[]{:S(2)}) collective-permute-start(f32[128,128]{1,0:T(8,128)S(1)} %select_select_fusion), channel_id=1, source_target_pairs={{0,16},{1,17},{16,32},{17,33},{64,80},{65,81},{80,96},{81,97},{128... | collective-permute-start | bytes 196616 | tf_op jit(solution)/shard_map/ppermute | solution.py:28
  19.1 1.3 %collective-permute-start.6 = (f32[8,128,128]{2,1,0:T(8,128)S(1)}, f32[8,128,128]{2,1,0:T(8,128)S(1)}, u32[]{:S(2)}, u32[]{:S(2)}) collective-permute-start(f32[8,128,128]{2,1,0:T(8,128)S(1)} %select_bitcast_fusion), channel_id=1, source_target_pairs={{0,4},{1,13},{16,20},{17,29},{32,36},{33,45},{48,52},{49,61},{64,6... | collective-permute-start | bytes 1572872 | tf_op jit(solution)/shard_map/ppermute | solution.py:28
  20.5 1.3 %collective-permute-start.7 = (f32[2,128,128]{2,1,0:T(8,128)S(1)}, f32[2,128,128]{2,1,0:T(8,128)S(1)}, u32[]{:S(2)}, u32[]{:S(2)}) collective-permute-start(f32[2,128,128]{2,1,0:T(8,128)S(1)} %broadcast_select_fusion), channel_id=1, source_target_pairs={{0,4},{1,13},{16,20},{17,29},{32,36},{33,45},{48,52},{49,61},{64,6... | collective-permute-start | bytes 393224 | tf_op jit(solution)/shard_map/ppermute | solution.py:28
  23.0 3.2 %collective-permute-start.10 = (f32[32,8,128]{2,1,0:T(8,128)S(1)}, f32[32,8,128]{2,1,0:T(8,128)S(1)}, u32[]{:S(2)}, u32[]{:S(2)}) collective-permute-start(f32[32,8,128]{2,1,0:T(8,128)S(1)} %get-tuple-element.24), channel_id=1, source_target_pairs={{0,128},{1,129},{2,130},{3,131},{4,132},{5,133},{6,134},{7,135},{8... | collective-permute-start | bytes 393224 | tf_op jit(solution)/shard_map/ppermute | solution.py:28
  26.2 1.7 %collective-permute-done.7 = f32[2,128,128]{2,1,0:T(8,128)S(1)} collective-permute-done((f32[2,128,128]{2,1,0:T(8,128)S(1)}, f32[2,128,128]{2,1,0:T(8,128)S(1)}, u32[]{:S(2)}, u32[]{:S(2)}) %collective-permute-start.7) | collective-permute-done | bytes 131104 | tf_op jit(solution)/shard_map/ppermute | solution.py:28
  28.0 1.3 %collective-permute-start.8 = (f32[8,128,128]{2,1,0:T(8,128)S(1)}, f32[8,128,128]{2,1,0:T(8,128)S(1)}, u32[]{:S(2)}, u32[]{:S(2)}) collective-permute-start(f32[8,128,128]{2,1,0:T(8,128)S(1)} %add.30), channel_id=1, source_target_pairs={{0,12},{1,5},{4,8},{13,9},{16,28},{17,21},{20,24},{29,25},{32,44},... | collective-permute-start | bytes 1572872 | tf_op jit(solution)/shard_map/ppermute | solution.py:28
  29.4 3.2 %collective-permute-done.9 = f32[32,8,128]{2,1,0:T(8,128)S(1)} collective-permute-done((f32[32,8,128]{2,1,0:T(8,128)S(1)}, f32[32,8,128]{2,1,0:T(8,128)S(1)}, u32[]{:S(2)}, u32[]{:S(2)}) %collective-permute-start.9) | collective-permute-done | bytes 131104 | tf_op jit(solution)/shard_map/ppermute | solution.py:28
  33.5 1.3 %collective-permute-start.12 = (f32[2,128,128]{2,1,0:T(8,128)S(1)}, f32[2,128,128]{2,1,0:T(8,128)S(1)}, u32[]{:S(2)}, u32[]{:S(2)}) collective-permute-start(f32[2,128,128]{2,1,0:T(8,128)S(1)} %fusion.2), channel_id=1, source_target_pairs={{0,12},{1,5},{4,8},{13,9},{16,28},{17,21},{20,24},{29,25},{32,44},... | collective-permute-start | bytes 393224 | tf_op jit(solution)/shard_map/ppermute | solution.py:28
  35.9 2.5 %collective-permute-start.20 = (f32[32,8,128]{2,1,0:T(8,128)S(1)}, f32[32,8,128]{2,1,0:T(8,128)S(1)}, u32[]{:S(2)}, u32[]{:S(2)}) collective-permute-start(f32[32,8,128]{2,1,0:T(8,128)S(1)} %bitcast_select_fusion), channel_id=1, source_target_pairs={{0,32},{1,33},{2,34},{3,35},{4,36},{5,37},{6,38},{7,39},{8,40},{9,... | collective-permute-start | bytes 393224 | tf_op jit(solution)/shard_map/ppermute | solution.py:28
  38.5 1.3 %collective-permute-start.13 = (f32[2,128,128]{2,1,0:T(8,128)S(1)}, f32[2,128,128]{2,1,0:T(8,128)S(1)}, u32[]{:S(2)}, u32[]{:S(2)}) collective-permute-start(f32[2,128,128]{2,1,0:T(8,128)S(1)} %add.33), channel_id=1, source_target_pairs={{0,2},{1,15},{4,6},{5,3},{8,10},{9,7},{12,14},{13,11},{16,18},{17,... | collective-permute-start | bytes 393224 | tf_op jit(solution)/shard_map/ppermute | solution.py:28
  39.8 1.5 %collective-permute-done.20 = f32[32,8,128]{2,1,0:T(8,128)S(1)} collective-permute-done((f32[32,8,128]{2,1,0:T(8,128)S(1)}, f32[32,8,128]{2,1,0:T(8,128)S(1)}, u32[]{:S(2)}, u32[]{:S(2)}) %collective-permute-start.20) | collective-permute-done | bytes 131104 | tf_op jit(solution)/shard_map/ppermute | solution.py:28
  41.3 3.6 %collective-permute-done.19 = f32[32,8,128]{2,1,0:T(8,128)S(1)} collective-permute-done((f32[32,8,128]{2,1,0:T(8,128)S(1)}, f32[32,8,128]{2,1,0:T(8,128)S(1)}, u32[]{:S(2)}, u32[]{:S(2)}) %collective-permute-start.19) | collective-permute-done | bytes 131104 | tf_op jit(solution)/shard_map/ppermute | solution.py:28
  45.1 1.4 %collective-permute-start.22 = (f32[2,32,8,128]{3,2,1,0:T(8,128)S(1)}, f32[2,32,8,128]{3,2,1,0:T(8,128)S(1)}, u32[]{:S(2)}, u32[]{:S(2)}) collective-permute-start(f32[2,32,8,128]{3,2,1,0:T(8,128)S(1)} %pad_maximum_fusion.h0_ref), channel_id=1, source_target_pairs={{0,64},{1,65},{2,66},{3,67},{4,68},{5,69},{6,70},{7,71},{8,72},{9,... | collective-permute-start | bytes 786440 | tf_op jit(solution)/shard_map/ppermute | solution.py:28
  46.5 3.9 %collective-permute-start.14 = (f32[2,128,128]{2,1,0:T(8,128)S(1)}, f32[2,128,128]{2,1,0:T(8,128)S(1)}, u32[]{:S(2)}, u32[]{:S(2)}) collective-permute-start(f32[2,128,128]{2,1,0:T(8,128)S(1)} %add.34.held_ref), channel_id=1, source_target_pairs={{0,1},{1,0},{2,3},{3,2},{4,5},{5,4},{6,7},{7,6},{8,9},{9,8},{10,11... | collective-permute-start | bytes 393224 | tf_op jit(solution)/shard_map/ppermute | solution.py:28
  50.6 1.3 %collective-permute-start.16 = (f32[4,128,128]{2,1,0:T(8,128)S(1)}, f32[4,128,128]{2,1,0:T(8,128)S(1)}, u32[]{:S(2)}, u32[]{:S(2)}) collective-permute-start(f32[4,128,128]{2,1,0:T(8,128)S(1)} %get-tuple-element.21), channel_id=1, source_target_pairs={{0,2},{1,15},{4,6},{5,3},{8,10},{9,7},{12,14},{13,11},{16,18},{17,... | collective-permute-start | bytes 786440 | tf_op jit(solution)/shard_map/ppermute | solution.py:28
  51.9 1.5 %collective-permute-start.15 = (f32[4,128,128]{2,1,0:T(8,128)S(1)}, f32[4,128,128]{2,1,0:T(8,128)S(1)}, u32[]{:S(2)}, u32[]{:S(2)}) collective-permute-start(f32[4,128,128]{2,1,0:T(8,128)S(1)} %get-tuple-element.20), channel_id=1, source_target_pairs={{0,2},{1,15},{4,6},{5,3},{8,10},{9,7},{12,14},{13,11},{16,18},{17,... | collective-permute-start | bytes 786440 | tf_op jit(solution)/shard_map/ppermute | solution.py:28
  53.4 6.3 %shard_map.28.w_ref = f32[256,256]{1,0:T(8,128)S(1)} custom-call(s32[1]{0:T(128)S(6)} %and.26.core_ref, f32[2,128,128]{2,1,0:T(8,128)S(1)} %add.34.held_ref, f32[2,128,128]{2,1,0:T(8,128)S(1)} %collective-permute-done.14.other_ref), custom_call_target="tpu_custom_call" | custom-call | flops 12000000000 | bytes 500000 | tf_op jit(solution)/shard_map/pallas_call | solution.py:107
  61.7 5.6 %shard_map.29 = f32[8,128,8,128]{3,2,1,0:T(8,128)} custom-call(s32[2]{0:T(128)S(1)} %pad_add_fusion.place_ref, f32[8,128,8,128]{3,2,1,0:T(8,128)S(1)} %copy-done, f32[4,128,128]{2,1,0:T(8,128)S(1)} %add.35.r0_ref, f32[4,128,128]{2,1,0:T(8,128)S(1)} %add.36.r1_ref, f32[4,128,128]{2,1,0:T(8,128)S(1)} %collective-permute-done.17.o0_ref, ...), custom_call_target="tpu_custom_call" | custom-call | flops 1610612736 | bytes 8388608 | tf_op jit(solution)/shard_map/pallas_call | solution.py:166
  (51 shorter events, 7.7 us)
Async XLA Ops:
  1.8 10.6 %collective-permute-start.2 = (f32[128,128]{1,0:T(8,128)S(1)}, f32[128,128]{1,0:T(8,128)S(1)}, u32[]{:S(2)}, u32[]{:S(2)}) collective-permute-start(f32[128,128]{1,0:T(8,128)S(1)} %select_add_fusion), channel_id=1, source_target_pairs={{0,192},{1,193},{16,208},{17,209}} | collective-permute-start | bytes 196616 | tf_op jit(solution)/shard_map/ppermute | solution.py:28
  7.3 5.2 %collective-permute-start.1 = (f32[128,128]{1,0:T(8,128)S(1)}, f32[128,128]{1,0:T(8,128)S(1)}, u32[]{:S(2)}, u32[]{:S(2)}) collective-permute-start(f32[128,128]{1,0:T(8,128)S(1)} %select_add_fusion), channel_id=1, source_target_pairs={{0,128},{1,129},{16,144},{17,145}} | collective-permute-start | bytes 196616 | tf_op jit(solution)/shard_map/ppermute | solution.py:28
  8.6 3.9 %collective-permute-start = (f32[128,128]{1,0:T(8,128)S(1)}, f32[128,128]{1,0:T(8,128)S(1)}, u32[]{:S(2)}, u32[]{:S(2)}) collective-permute-start(f32[128,128]{1,0:T(8,128)S(1)} %select_add_fusion), channel_id=1, source_target_pairs={{0,64},{1,65},{16,80},{17,81}} | collective-permute-start | bytes 196616 | tf_op jit(solution)/shard_map/ppermute | solution.py:28
  12.5 7.9 %collective-permute-start.5 = (f32[128,128]{1,0:T(8,128)S(1)}, f32[128,128]{1,0:T(8,128)S(1)}, u32[]{:S(2)}, u32[]{:S(2)}) collective-permute-start(f32[128,128]{1,0:T(8,128)S(1)} %select_select_fusion), channel_id=1, source_target_pairs={{0,48},{1,49},{16,0},{17,1},{64,112},{65,113},{80,64},{81,65},{128... | collective-permute-start | bytes 196616 | tf_op jit(solution)/shard_map/ppermute | solution.py:28
  14.4 6.0 %collective-permute-start.4 = (f32[128,128]{1,0:T(8,128)S(1)}, f32[128,128]{1,0:T(8,128)S(1)}, u32[]{:S(2)}, u32[]{:S(2)}) collective-permute-start(f32[128,128]{1,0:T(8,128)S(1)} %select_select_fusion), channel_id=1, source_target_pairs={{0,32},{1,33},{16,48},{17,49},{64,96},{65,97},{80,112},{81,113},{1... | collective-permute-start | bytes 196616 | tf_op jit(solution)/shard_map/ppermute | solution.py:28
  15.7 4.7 %collective-permute-start.3 = (f32[128,128]{1,0:T(8,128)S(1)}, f32[128,128]{1,0:T(8,128)S(1)}, u32[]{:S(2)}, u32[]{:S(2)}) collective-permute-start(f32[128,128]{1,0:T(8,128)S(1)} %select_select_fusion), channel_id=1, source_target_pairs={{0,16},{1,17},{16,32},{17,33},{64,80},{65,81},{80,96},{81,97},{128... | collective-permute-start | bytes 196616 | tf_op jit(solution)/shard_map/ppermute | solution.py:28
  19.1 8.8 %collective-permute-start.6 = (f32[8,128,128]{2,1,0:T(8,128)S(1)}, f32[8,128,128]{2,1,0:T(8,128)S(1)}, u32[]{:S(2)}, u32[]{:S(2)}) collective-permute-start(f32[8,128,128]{2,1,0:T(8,128)S(1)} %select_bitcast_fusion), channel_id=1, source_target_pairs={{0,4},{1,13},{16,20},{17,29},{32,36},{33,45},{48,52},{49,61},{64,6... | collective-permute-start | bytes 1572872 | tf_op jit(solution)/shard_map/ppermute | solution.py:28
  20.5 7.4 %collective-permute-start.7 = (f32[2,128,128]{2,1,0:T(8,128)S(1)}, f32[2,128,128]{2,1,0:T(8,128)S(1)}, u32[]{:S(2)}, u32[]{:S(2)}) collective-permute-start(f32[2,128,128]{2,1,0:T(8,128)S(1)} %broadcast_select_fusion), channel_id=1, source_target_pairs={{0,4},{1,13},{16,20},{17,29},{32,36},{33,45},{48,52},{49,61},{64,6... | collective-permute-start | bytes 393224 | tf_op jit(solution)/shard_map/ppermute | solution.py:28
  22.9 6.4 %collective-permute-start.11 = (f32[32,8,128]{2,1,0:T(8,128)S(1)}, f32[32,8,128]{2,1,0:T(8,128)S(1)}, u32[]{:S(2)}, u32[]{:S(2)}) collective-permute-start(f32[32,8,128]{2,1,0:T(8,128)S(1)} %get-tuple-element.23), channel_id=1, source_target_pairs={{0,192},{1,193},{2,194},{3,195},{4,196},{5,197},{6,198},{7,199},{8... | collective-permute-start | bytes 393224 | tf_op jit(solution)/shard_map/ppermute | solution.py:28
  23.0 6.4 %collective-permute-start.10 = (f32[32,8,128]{2,1,0:T(8,128)S(1)}, f32[32,8,128]{2,1,0:T(8,128)S(1)}, u32[]{:S(2)}, u32[]{:S(2)}) collective-permute-start(f32[32,8,128]{2,1,0:T(8,128)S(1)} %get-tuple-element.24), channel_id=1, source_target_pairs={{0,128},{1,129},{2,130},{3,131},{4,132},{5,133},{6,134},{7,135},{8... | collective-permute-start | bytes 393224 | tf_op jit(solution)/shard_map/ppermute | solution.py:28
  26.2 6.3 %collective-permute-start.9 = (f32[32,8,128]{2,1,0:T(8,128)S(1)}, f32[32,8,128]{2,1,0:T(8,128)S(1)}, u32[]{:S(2)}, u32[]{:S(2)}) collective-permute-start(f32[32,8,128]{2,1,0:T(8,128)S(1)} %get-tuple-element.25), channel_id=1, source_target_pairs={{0,64},{1,65},{2,66},{3,67},{4,68},{5,69},{6,70},{7,71},{8,72},{9,... | collective-permute-start | bytes 393224 | tf_op jit(solution)/shard_map/ppermute | solution.py:28
  28.0 22.4 %collective-permute-start.8 = (f32[8,128,128]{2,1,0:T(8,128)S(1)}, f32[8,128,128]{2,1,0:T(8,128)S(1)}, u32[]{:S(2)}, u32[]{:S(2)}) collective-permute-start(f32[8,128,128]{2,1,0:T(8,128)S(1)} %add.30), channel_id=1, source_target_pairs={{0,12},{1,5},{4,8},{13,9},{16,28},{17,21},{20,24},{29,25},{32,44},... | collective-permute-start | bytes 1572872 | tf_op jit(solution)/shard_map/ppermute | solution.py:28
  33.5 5.0 %collective-permute-start.12 = (f32[2,128,128]{2,1,0:T(8,128)S(1)}, f32[2,128,128]{2,1,0:T(8,128)S(1)}, u32[]{:S(2)}, u32[]{:S(2)}) collective-permute-start(f32[2,128,128]{2,1,0:T(8,128)S(1)} %fusion.2), channel_id=1, source_target_pairs={{0,12},{1,5},{4,8},{13,9},{16,28},{17,21},{20,24},{29,25},{32,44},... | collective-permute-start | bytes 393224 | tf_op jit(solution)/shard_map/ppermute | solution.py:28
  34.8 5.0 %collective-permute-start.21 = (f32[32,8,128]{2,1,0:T(8,128)S(1)}, f32[32,8,128]{2,1,0:T(8,128)S(1)}, u32[]{:S(2)}, u32[]{:S(2)}) collective-permute-start(f32[32,8,128]{2,1,0:T(8,128)S(1)} %bitcast_select_fusion), channel_id=1, source_target_pairs={{0,48},{1,49},{2,50},{3,51},{4,52},{5,53},{6,54},{7,55},{8,56},{9,... | collective-permute-start | bytes 393224 | tf_op jit(solution)/shard_map/ppermute | solution.py:28
  35.9 5.3 %collective-permute-start.20 = (f32[32,8,128]{2,1,0:T(8,128)S(1)}, f32[32,8,128]{2,1,0:T(8,128)S(1)}, u32[]{:S(2)}, u32[]{:S(2)}) collective-permute-start(f32[32,8,128]{2,1,0:T(8,128)S(1)} %bitcast_select_fusion), channel_id=1, source_target_pairs={{0,32},{1,33},{2,34},{3,35},{4,36},{5,37},{6,38},{7,39},{8,40},{9,... | collective-permute-start | bytes 393224 | tf_op jit(solution)/shard_map/ppermute | solution.py:28
  38.4 6.4 %collective-permute-start.19 = (f32[32,8,128]{2,1,0:T(8,128)S(1)}, f32[32,8,128]{2,1,0:T(8,128)S(1)}, u32[]{:S(2)}, u32[]{:S(2)}) collective-permute-start(f32[32,8,128]{2,1,0:T(8,128)S(1)} %bitcast_select_fusion), channel_id=1, source_target_pairs={{0,16},{1,17},{2,18},{3,19},{4,20},{5,21},{6,22},{7,23},{8,24},{9,... | collective-permute-start | bytes 393224 | tf_op jit(solution)/shard_map/ppermute | solution.py:28
  38.5 8.0 %collective-permute-start.13 = (f32[2,128,128]{2,1,0:T(8,128)S(1)}, f32[2,128,128]{2,1,0:T(8,128)S(1)}, u32[]{:S(2)}, u32[]{:S(2)}) collective-permute-start(f32[2,128,128]{2,1,0:T(8,128)S(1)} %add.33), channel_id=1, source_target_pairs={{0,2},{1,15},{4,6},{5,3},{8,10},{9,7},{12,14},{13,11},{16,18},{17,... | collective-permute-start | bytes 393224 | tf_op jit(solution)/shard_map/ppermute | solution.py:28
  44.9 15.6 %collective-permute-start.24 = (f32[2,32,8,128]{3,2,1,0:T(8,128)S(1)}, f32[2,32,8,128]{3,2,1,0:T(8,128)S(1)}, u32[]{:S(2)}, u32[]{:S(2)}) collective-permute-start(f32[2,32,8,128]{3,2,1,0:T(8,128)S(1)} %pad_maximum_fusion.h0_ref), channel_id=1, source_target_pairs={{0,192},{1,193},{2,194},{3,195},{4,196},{5,197},{6,198},{7,199},{8... | collective-permute-start | bytes 786440 | tf_op jit(solution)/shard_map/ppermute | solution.py:28
  45.0 15.5 %collective-permute-start.23 = (f32[2,32,8,128]{3,2,1,0:T(8,128)S(1)}, f32[2,32,8,128]{3,2,1,0:T(8,128)S(1)}, u32[]{:S(2)}, u32[]{:S(2)}) collective-permute-start(f32[2,32,8,128]{3,2,1,0:T(8,128)S(1)} %pad_maximum_fusion.h0_ref), channel_id=1, source_target_pairs={{0,128},{1,129},{2,130},{3,131},{4,132},{5,133},{6,134},{7,135},{8... | collective-permute-start | bytes 786440 | tf_op jit(solution)/shard_map/ppermute | solution.py:28
  45.1 15.4 %collective-permute-start.22 = (f32[2,32,8,128]{3,2,1,0:T(8,128)S(1)}, f32[2,32,8,128]{3,2,1,0:T(8,128)S(1)}, u32[]{:S(2)}, u32[]{:S(2)}) collective-permute-start(f32[2,32,8,128]{3,2,1,0:T(8,128)S(1)} %pad_maximum_fusion.h0_ref), channel_id=1, source_target_pairs={{0,64},{1,65},{2,66},{3,67},{4,68},{5,69},{6,70},{7,71},{8,72},{9,... | collective-permute-start | bytes 786440 | tf_op jit(solution)/shard_map/ppermute | solution.py:28
  46.5 5.4 %collective-permute-start.14 = (f32[2,128,128]{2,1,0:T(8,128)S(1)}, f32[2,128,128]{2,1,0:T(8,128)S(1)}, u32[]{:S(2)}, u32[]{:S(2)}) collective-permute-start(f32[2,128,128]{2,1,0:T(8,128)S(1)} %add.34.held_ref), channel_id=1, source_target_pairs={{0,1},{1,0},{2,3},{3,2},{4,5},{5,4},{6,7},{7,6},{8,9},{9,8},{10,11... | collective-permute-start | bytes 393224 | tf_op jit(solution)/shard_map/ppermute | solution.py:28
  50.6 9.1 %collective-permute-start.16 = (f32[4,128,128]{2,1,0:T(8,128)S(1)}, f32[4,128,128]{2,1,0:T(8,128)S(1)}, u32[]{:S(2)}, u32[]{:S(2)}) collective-permute-start(f32[4,128,128]{2,1,0:T(8,128)S(1)} %get-tuple-element.21), channel_id=1, source_target_pairs={{0,2},{1,15},{4,6},{5,3},{8,10},{9,7},{12,14},{13,11},{16,18},{17,... | collective-permute-start | bytes 786440 | tf_op jit(solution)/shard_map/ppermute | solution.py:28
  51.9 8.0 %collective-permute-start.15 = (f32[4,128,128]{2,1,0:T(8,128)S(1)}, f32[4,128,128]{2,1,0:T(8,128)S(1)}, u32[]{:S(2)}, u32[]{:S(2)}) collective-permute-start(f32[4,128,128]{2,1,0:T(8,128)S(1)} %get-tuple-element.20), channel_id=1, source_target_pairs={{0,2},{1,15},{4,6},{5,3},{8,10},{9,7},{12,14},{13,11},{16,18},{17,... | collective-permute-start | bytes 786440 | tf_op jit(solution)/shard_map/ppermute | solution.py:28
  59.9 1.8 %collective-permute-start.17 = (f32[4,128,128]{2,1,0:T(8,128)S(1)}, f32[4,128,128]{2,1,0:T(8,128)S(1)}, u32[]{:S(2)}, u32[]{:S(2)}) collective-permute-start(f32[4,128,128]{2,1,0:T(8,128)S(1)} %add.35.r0_ref), channel_id=1, source_target_pairs={{0,1},{1,0},{2,3},{3,2},{4,5},{5,4},{6,7},{7,6},{8,9},{9,8},{10,11... | collective-permute-start | bytes 786440 | tf_op jit(solution)/shard_map/ppermute | solution.py:28
  (2 other events, 10.0 us)
